TPU v7x, 128 devices: a whole 4x4x4 slice. The times are simulated.
128 devices in a mesh: dp: 16 (over y, z_hi, core), tm: 8 (over x, z_lo).
Axes of the slice: x: 4, y: 4, z: 4 (z_hi: 2, z_lo: 2; z = z_hi * 2 + z_lo), core: 2. Of those that a mesh axis runs over, the one named last changes fastest.
Arguments:
- code_ids: int32 [16, 1024, 2], P('dp', 'tm'), may hold values from 0 to 1023
- code_table: bfloat16 [2048, 768], replicated, may hold values from -6 to 6
- kernel: float32 [7, 768], replicated, may hold values from -2 to 2
- up_weight: bfloat16 [768, 2304], replicated, may hold values from -0.21875 to 0.21875
- down_weight: bfloat16 [2304, 768], replicated, may hold values from -0.125 to 0.125
- layer_scale: float32 [768], replicated, may hold values from 0.3 to 1
- head_weight: bfloat16 [768, 1026], replicated, may hold values from -0.21875 to 0.21875
- target: float32 [16, 262144], P('dp', 'tm'), may hold values from -0.75 to 0.75, as said below
- loss_scale: float32 [], replicated, may hold values from 30000 to 100000
Outputs:
- spectral_loss: float32 [], replicated
- table_grad: float32 [2048, 768], P(('dp', 'tm'))
- kernel_grad: float32 [7, 768], P(None, ('dp', 'tm'))
- up_grad: float32 [768, 2304], P(('dp', 'tm'))
- down_grad: float32 [2304, 768], P(('dp', 'tm'))
- scale_grad: float32 [768], P(('dp', 'tm'))
- head_grad: float32 [768, 1026], P(('dp', 'tm'))
Inputs may be any that keep to these rules, and one draw needn't show every extreme that they name: target waveform samples.
All inputs are finite; a program needn't handle non-finite values.
Results may differ from a plain program's by a relative error of at most 0.02.
Values sent between devices are 32-bit elements; how exact they have to be, the bound alone decides.
A program may use at most 128 MiB of HBM per device.

v0:
```python
import jax
import jax.numpy as jnp
from jax import lax
from jax.sharding import PartitionSpec as P

KSIZE = 7
NFFT = 1024
HOP = 256


def extended_2(block, sides, width):
    for axis, dim in sides:
        count = lax.axis_size(axis)
        forward = [(i, i + 1) for i in range(count - 1)]
        backward = [(target, source) for source, target in forward]
        low = lax.ppermute(
            lax.slice_in_dim(block, block.shape[dim] - width, None, axis=dim), axis, forward
        )
        high = lax.ppermute(lax.slice_in_dim(block, 0, width, axis=dim), axis, backward)
        block = jnp.concatenate([low, block, high], axis=dim)
    return block


def layer_norm(values):
    centre = values - jnp.mean(values, axis=-1, keepdims=True)
    spread = jnp.mean(centre * centre, axis=-1, keepdims=True)
    return centre * lax.rsqrt(spread + 1e-06)


def hann_window(length):
    places = jnp.arange(length, dtype=jnp.float32)
    return 0.5 - 0.5 * jnp.cos(2.0 * jnp.pi * places / length)


def fourier_angles(length):
    frequency = jnp.arange(length // 2 + 1, dtype=jnp.int32)
    places = jnp.arange(length, dtype=jnp.int32)
    product = frequency[:, None] * places[None, :] % length
    return 2.0 * jnp.pi * product.astype(jnp.float32) / length


def synthesis_table(length):
    angles = fourier_angles(length)
    frequency = jnp.arange(length // 2 + 1, dtype=jnp.int32)
    factor = (
        jnp.where((frequency == 0) | (frequency == length // 2), 1.0, 2.0).astype(jnp.float32)
        / length
    )
    window = hann_window(length)
    cosine_part = factor[:, None] * jnp.cos(angles) * window[None, :]
    sine_part = -factor[:, None] * jnp.sin(angles) * window[None, :]
    return jnp.concatenate([cosine_part, sine_part], axis=0).astype(jnp.bfloat16)


def analysis_table(length):
    angles = fourier_angles(length)
    return jnp.concatenate([jnp.cos(angles).T, -jnp.sin(angles).T], axis=1).astype(jnp.bfloat16)


def envelope(first_sample, samples, frame_total):
    places = first_sample + jnp.arange(samples, dtype=jnp.int32)
    blocks = places // HOP
    summed = jnp.zeros((samples,), jnp.float32)
    for offset in (-1, 0, 1, 2):
        frame_index = blocks + offset
        inside = places - frame_index * HOP + NFFT // 2
        weight = 0.5 - 0.5 * jnp.cos(2.0 * jnp.pi * inside.astype(jnp.float32) / NFFT)
        within = (frame_index >= 0) & (frame_index < frame_total)
        summed = summed + jnp.where(within, weight * weight, 0.0)
    return summed


def frame_sum(frames_out):
    lead_rows, frame_count = (frames_out.shape[0], frames_out.shape[1])
    stride = frames_out.shape[2] // 4
    pieces = frames_out.reshape(lead_rows, frame_count, 4, stride)
    buffer = jnp.zeros((lead_rows, frame_count + 4, stride), jnp.float32)
    for offset in range(4):
        buffer = buffer + jnp.pad(pieces[:, :, offset], ((0, 0), (offset, 4 - offset), (0, 0)))
    return buffer.reshape(lead_rows, (frame_count + 4) * stride)


def framed(padded, stride):
    lead_rows = padded.shape[0]
    block_total = padded.shape[1] // stride
    blocks = padded.reshape(lead_rows, block_total, stride)
    number = block_total - 4
    return jnp.concatenate([blocks[:, offset : offset + number] for offset in range(4)], axis=-1)


def code_matrix(code_ids, vocab_total):
    codebooks = code_ids.shape[-1]
    shifted = code_ids + jnp.arange(codebooks, dtype=jnp.int32) * (vocab_total // codebooks)
    columns = jnp.arange(vocab_total, dtype=jnp.int32)
    matches = (shifted[..., :, None] == columns).astype(jnp.float32)
    return jnp.sum(matches, axis=-2).astype(jnp.bfloat16)


def embed_forward(code_ids, code_table, probe_embed):
    onehot = code_matrix(code_ids, code_table.shape[0])
    return layer_norm(jnp.dot(onehot, code_table, preferred_element_type=jnp.float32) + probe_embed)


def block_forward(
    extended,
    kernel,
    layer_scale,
    probe_up,
    probe_down,
    probe_head,
    up_weight,
    down_weight,
    head_weight,
):
    margin = kernel.shape[0] // 2
    frame_rows = extended.shape[1] - 2 * margin
    mixture = kernel[0] * extended[:, 0:frame_rows]
    for offset in range(1, kernel.shape[0]):
        mixture = mixture + kernel[offset] * extended[:, offset : offset + frame_rows]
    normed = layer_norm(mixture).astype(jnp.bfloat16)
    up_out = jnp.dot(normed, up_weight, preferred_element_type=jnp.float32) + probe_up
    hidden = jax.nn.gelu(up_out, approximate=False).astype(jnp.bfloat16)
    down_out = jnp.dot(hidden, down_weight, preferred_element_type=jnp.float32) + probe_down
    stream = extended[:, margin : margin + frame_rows] + layer_scale * down_out
    output_norm = layer_norm(stream).astype(jnp.bfloat16)
    head_out = jnp.dot(output_norm, head_weight, preferred_element_type=jnp.float32) + probe_head
    bin_count = head_out.shape[-1] // 2
    magnitude = jnp.exp(head_out[..., :bin_count])
    phases = head_out[..., bin_count:]
    spectrum = jnp.concatenate(
        [magnitude * jnp.cos(phases), magnitude * jnp.sin(phases)], axis=-1
    ).astype(jnp.bfloat16)
    frames_out = jnp.dot(
        spectrum, synthesis_table(2 * (bin_count - 1)), preferred_element_type=jnp.float32
    )
    buffer = frame_sum(frames_out)
    half_frame = frames_out.shape[-1] // 2
    rim_parts = jnp.concatenate([buffer[:, :half_frame], buffer[:, -half_frame:]], axis=1)
    return ((rim_parts, buffer[:, half_frame:-half_frame]), (normed, hidden, output_norm))


def spectral_stats(predicted, goal):
    columns = []
    for length, stride, margin in ((NFFT, NFFT // 4, 0), (NFFT // 2, NFFT // 8, NFFT // 4)):
        window = hann_window(length)
        dft_table = analysis_table(length)
        extent = predicted.shape[1] - margin
        results = []
        for signal in (predicted, goal):
            segment = framed(signal[:, margin:extent], stride) * window
            results.append(
                jnp.dot(segment.astype(jnp.bfloat16), dft_table, preferred_element_type=jnp.float32)
            )
        bin_count = length // 2 + 1
        pred_spec, goal_spec = results
        differ = pred_spec - goal_spec
        pred_power = (
            pred_spec[..., :bin_count] * pred_spec[..., :bin_count]
            + pred_spec[..., bin_count:] * pred_spec[..., bin_count:]
        )
        goal_power = (
            goal_spec[..., :bin_count] * goal_spec[..., :bin_count]
            + goal_spec[..., bin_count:] * goal_spec[..., bin_count:]
        )
        log_gap = jnp.log1p(pred_power) - jnp.log1p(goal_power)
        columns.extend(
            [
                jnp.sum(differ * differ, axis=(1, 2)),
                jnp.sum(goal_spec * goal_spec, axis=(1, 2)),
                jnp.sum(log_gap * log_gap, axis=(1, 2)),
            ]
        )
    return jnp.stack(columns, axis=-1)


def per_clip_loss(statistics, frame_total):
    counts = (frame_total * (NFFT // 2 + 1), 2 * frame_total * (NFFT // 4 + 1))
    summed = jnp.zeros(statistics.shape[:1], jnp.float32)
    for level in range(2):
        convergence = jnp.sqrt(statistics[:, 3 * level] + 1e-06) / jnp.sqrt(
            statistics[:, 3 * level + 1] + 1e-06
        )
        summed = summed + convergence + statistics[:, 3 * level + 2] / counts[level]
    return summed


def stat_cotangent(statistics, frame_total, factor):
    counts = (frame_total * (NFFT // 2 + 1), 2 * frame_total * (NFFT // 4 + 1))
    columns = []
    for level in range(2):
        first_sum = statistics[:, 3 * level]
        second_sum = statistics[:, 3 * level + 1]
        columns.append(factor * 0.5 / (jnp.sqrt(first_sum + 1e-06) * jnp.sqrt(second_sum + 1e-06)))
        columns.append(jnp.zeros_like(first_sum))
        columns.append(jnp.zeros_like(first_sum) + factor / counts[level])
    return jnp.stack(columns, axis=-1)


def weight_grad(inputs, cotangent):
    left_side = inputs.reshape(-1, inputs.shape[-1])
    right_side = cotangent.reshape(-1, cotangent.shape[-1]).astype(jnp.bfloat16)
    return jnp.dot(left_side.T, right_side, preferred_element_type=jnp.float32)


def frame_rim(values):
    return extended_2(values, (("tm", 1),), KSIZE // 2)


def sample_rim(values):
    return extended_2(values, (("tm", 1),), NFFT // 2)


def add_ends(middle, leading, trailing):
    length = middle.shape[1]
    width_end = leading.shape[1]
    return (
        middle
        + jnp.pad(leading, ((0, 0), (0, length - width_end)))
        + jnp.pad(trailing, ((0, 0), (length - width_end, 0)))
    )


def body(
    code_ids,
    code_table,
    kernel,
    up_weight,
    down_weight,
    layer_scale,
    head_weight,
    target,
    loss_scale,
):
    clip_rows, frame_rows = (code_ids.shape[0], code_ids.shape[1])
    samples_dev = frame_rows * HOP
    frame_total = frame_rows * lax.axis_size("tm")
    clip_total = clip_rows * lax.axis_size("dp")
    half_frame = NFFT // 2
    margin = KSIZE // 2
    factor = loss_scale / (2.0 * clip_total)
    divisor = envelope(lax.axis_index("tm") * samples_dev, samples_dev, frame_total)
    model_width = code_table.shape[1]

    def embed_part(probe_input):
        return embed_forward(code_ids, code_table, probe_input)

    stream_in, embed_pull = jax.vjp(
        embed_part, jnp.zeros((clip_rows, frame_rows, model_width), jnp.float32)
    )
    extended = frame_rim(stream_in)

    def block_part(extended_in, kernel_in, scale_in, probe_up, probe_down, probe_head):
        return block_forward(
            extended_in,
            kernel_in,
            scale_in,
            probe_up,
            probe_down,
            probe_head,
            up_weight,
            down_weight,
            head_weight,
        )

    outputs, block_pull, saved = jax.vjp(
        block_part,
        extended,
        kernel,
        layer_scale,
        jnp.zeros((clip_rows, frame_rows, up_weight.shape[1]), jnp.float32),
        jnp.zeros((clip_rows, frame_rows, model_width), jnp.float32),
        jnp.zeros((clip_rows, frame_rows, head_weight.shape[1]), jnp.float32),
        has_aux=True,
    )
    rim_ext = sample_rim(outputs[0])
    predicted = add_ends(outputs[1], rim_ext[:, :half_frame], rim_ext[:, -half_frame:]) / divisor
    pair_ext = sample_rim(jnp.concatenate([predicted, target], axis=0))
    goal_ext = pair_ext[clip_rows:]

    def loss_part(pred_input):
        return spectral_stats(pred_input, goal_ext)

    statistics, loss_pull = jax.vjp(loss_part, pair_ext[:clip_rows])
    clip_stats = lax.psum(statistics, "tm")
    spectral_loss = lax.psum(jnp.sum(per_clip_loss(clip_stats, frame_total)), "dp") / (
        2.0 * clip_total
    )
    (grad_padded,) = loss_pull(stat_cotangent(clip_stats, frame_total, factor))
    returned = sample_rim(
        jnp.concatenate([grad_padded[:, :half_frame], grad_padded[:, -half_frame:]], axis=1)
    )
    grad_audio = add_ends(
        grad_padded[:, half_frame:-half_frame], returned[:, :half_frame], returned[:, -half_frame:]
    )
    grad_middle = grad_audio / divisor
    spilled = sample_rim(grad_middle)
    grad_rims = jnp.concatenate([spilled[:, :half_frame], spilled[:, -half_frame:]], axis=1)
    grad_extended, kernel_grad, scale_grad, grad_up, grad_down, grad_head = block_pull(
        (grad_rims, grad_middle)
    )
    sent_back = frame_rim(
        jnp.concatenate([grad_extended[:, :margin], grad_extended[:, -margin:]], axis=1)
    )
    inner_grad = grad_extended[:, margin : margin + frame_rows]
    grad_stream = (
        inner_grad
        + jnp.pad(sent_back[:, :margin], ((0, 0), (0, frame_rows - margin), (0, 0)))
        + jnp.pad(sent_back[:, -margin:], ((0, 0), (frame_rows - margin, 0), (0, 0)))
    )
    (grad_embedded,) = embed_pull(grad_stream)
    normed, hidden, output_norm = saved
    onehot = code_matrix(code_ids, code_table.shape[0])
    table_grad = weight_grad(onehot, grad_embedded)
    up_grad = weight_grad(normed, grad_up)
    down_grad = weight_grad(hidden, grad_down)
    head_grad = weight_grad(output_norm, grad_head)
    shards = (
        lax.psum_scatter(table_grad, ("dp", "tm"), scatter_dimension=0, tiled=True),
        lax.psum_scatter(kernel_grad, ("dp", "tm"), scatter_dimension=1, tiled=True),
        lax.psum_scatter(up_grad, ("dp", "tm"), scatter_dimension=0, tiled=True),
        lax.psum_scatter(down_grad, ("dp", "tm"), scatter_dimension=0, tiled=True),
        lax.psum_scatter(scale_grad, ("dp", "tm"), scatter_dimension=0, tiled=True),
        lax.psum_scatter(head_grad, ("dp", "tm"), scatter_dimension=0, tiled=True),
    )
    return (spectral_loss, shards[0], shards[1], shards[2], shards[3], shards[4], shards[5])


def solution(mesh):
    in_specs = (P("dp", "tm", None), P(), P(), P(), P(), P(), P(), P("dp", "tm"), P())
    out_specs = (
        P(),
        P(("dp", "tm"), None),
        P(None, ("dp", "tm")),
        P(("dp", "tm"), None),
        P(("dp", "tm"), None),
        P(("dp", "tm")),
        P(("dp", "tm"), None),
    )
    return jax.shard_map(body, mesh=mesh, in_specs=in_specs, out_specs=out_specs, check_vma=False)
```

profile of v0, /device:TPU:0, one launch (start us, length us, event | category | flops | bytes accessed | tf_op | source)
XLA Modules:
  0.0 1181.8 jit_solution(3097445246834454550)
XLA Ops:
  8.4 2.7 fusion.167
  12.8 3.9 collective-permute-start
  18.1 11.6 negate_convert_fusion
  29.7 9.0 multiply_convert_fusion.1
  41.4 4.9 dot_general.79
  46.3 2.8 fusion.157
  50.0 4.2 multiply_convert_fusion.2
  60.4 5.1 collective-permute-start.2
  67.0 3.9 negate_convert_fusion.1
  71.3 17.0 %fusion.125 = f32[1,32768]{1,0:T(1,128)S(1)} fusion(f32[1,33792]{1,0:T(1,128)} %bitcast.189, f32[1,512]{1,0:T(1,128)} %collective-permute-done.3, f32[1,512]{1,0:T(1,128)} %collective-permute-done.2, s32[]{:T(128)S(6)} %mul.844), kind=kLoop, calls=%fused_computation.273 | loop fusion | flops 2392064 | bytes 266244 | tf_op jit(solution)/shard_map/div | solution.py:276
  90.3 4.8 collective-permute-start.4
  97.7 3.2 collective-permute-done.5
  119.9 4.4 stack.27
  126.0 19.6 %psum.14 = f32[1,6]{1,0:T(1,128)} all-reduce(f32[1,6]{1,0:T(1,128)} %stack.27), channel_id=1, replica_groups=mesh['dp'=16,'tm'=8] {'tm'}, use_global_device_ids=true, to_apply=%region_13.14 | all-reduce | flops 6 | bytes 48 | tf_op jit(solution)/shard_map/psum | solution.py:284
  158.4 4.2 collective-permute-done.7
  162.5 16.2 %fusion.123 = f32[1,32768]{1,0:T(1,128)S(1)} fusion(f32[1,33792]{1,0:T(1,128)S(1)} %pad_add_fusion.4, f32[1,512]{1,0:T(1,128)S(1)} %collective-permute-done.7, f32[1,512]{1,0:T(1,128)S(1)} %collective-permute-done.6, s32[]{:T(128)S(6)} %mul.844), kind=kLoop, calls=%fused_computation.254 | loop fusion | flops 2392064 | bytes 266244 | tf_op jit(solution)/shard_map/div | solution.py:295
  180.0 4.8 collective-permute-start.9
  192.4 2.5 fusion.10
  197.8 2.5 fusion.87
  202.5 5.4 multiply_add_fusion
  216.0 5.0 collective-permute-start.10
  222.5 5.3 collective-permute-done.11
  228.3 3.6 fusion.102
  232.6 5.3 fusion.43
  237.9 4.1 fusion.108
  242.0 499.4 %fusion.150 = (f32[8,2304]{1,0:T(8,128)}, f32[24,768]{1,0:T(8,128)}) fusion(f32[768,2304]{1,0:T(8,128)} %fusion.43, f32[2304,768]{1,0:T(8,128)} %fusion.108), kind=kCustom, calls=%all-reduce-scatter.2 | all-reduce-scatter fusion | flops 4718594 | bytes 14303232
  741.4 13.9 %collective-permute-start.42 = (f32[8,2304]{1,0:T(8,128)}, f32[8,2304]{1,0:T(8,128)}, u32[]{:S(2)}, u32[]{:S(2)}) collective-permute-start(f32[8,2304]{1,0:T(8,128)} %get-tuple-element.36), channel_id=1, source_target_pairs={{0,31},{1,32},{2,33},{3,34},{4,35},{5,36},{6,37},{7,38},{8,39},{9,... | collective-permute-start | bytes 221192
  755.3 10.3 collective-permute-start.41
  766.4 9.5 collective-permute-start.75
  776.9 10.2 collective-permute-start.43
  787.1 7.7 collective-permute-start.40
  794.8 4.7 collective-permute-start.39
  799.4 3.2 collective-permute-start.38
  802.6 3.6 collective-permute-start.37
  810.5 5.2 collective-permute-start.34
  815.7 2.5 collective-permute-start.33
  818.3 3.5 collective-permute-start.32
  827.8 3.0 collective-permute-start.28
  832.8 3.1 collective-permute-start.26
  837.7 2.9 collective-permute-start.24
  840.6 4.9 collective-permute-start.23
  849.6 3.1 collective-permute-start.20
  854.6 4.7 collective-permute-start.18
  859.3 3.7 collective-permute-start.17
  864.9 5.1 collective-permute-start.15
  872.5 3.2 collective-permute-start.13
  875.7 4.0 collective-permute-start.12
  898.8 2.7 collective-permute-start.64
  901.5 3.1 collective-permute-start.63
  906.5 2.8 collective-permute-start.61
  909.3 2.9 collective-permute-start.60
  916.5 3.4 collective-permute-start.57
  922.0 3.8 collective-permute-start.55
  929.1 34.4 %psum.15 = f32[]{:T(128)} all-reduce(f32[]{:T(128)} %bitcast.40), channel_id=1, replica_groups=mesh['dp'=16,'tm'=8] {'dp'}, use_global_device_ids=true, to_apply=%region_14.15 | all-reduce | flops 1 | bytes 8 | tf_op jit(solution)/shard_map/psum | solution.py:285
  969.2 3.4 collective-permute-start.52
  974.5 2.8 collective-permute-start.50
  979.9 65.6 %all-reduce.54 = (f32[7,768]{1,0:T(8,128)}, f32[768]{0:T(1024)S(1)}) all-reduce(f32[7,768]{1,0:T(8,128)} %pad_add_fusion.5, f32[768]{0:T(1024)S(1)} %copy-done.56), channel_id=3, replica_groups=mesh['dp'=16,'tm'=8] {'dp','tm'}, use_global_device_ids=true, to_apply=%region_29.30.clone | all-reduce | flops 6144 | bytes 49152
  1046.1 5.2 collective-permute-start.48
  1051.2 3.0 collective-permute-start.47
  1054.2 2.6 collective-permute-start.46
  1056.8 3.6 collective-permute-start.45
  1060.4 3.4 collective-permute-start.44
  1065.3 54.0 %concatenate.130 = f32[262,2304]{1,0:T(8,128)} concatenate(f32[6,2304]{1,0:T(8,128)} %copy-done.48, f32[8,2304]{1,0:T(8,128)} %collective-permute-done.42, f32[8,2304]{1,0:T(8,128)} %collective-permute-done.41, f32[8,2304]{1,0:T(8,128)} %collective-permute-done.40, f32[8,2304]{1,0:T(8,128)} %collective-permute-done.39, f32[8,2304]{1,0:T(8,128)} %collective-permute-done.38, ...), dimensions={0} | concatenate | bytes 4829184
  1119.3 49.7 %concatenate.131 = f32[786,768]{1,0:T(8,128)} concatenate(f32[18,768]{1,0:T(8,128)} %copy-done.47, f32[24,768]{1,0:T(8,128)} %collective-permute-done.74, f32[24,768]{1,0:T(8,128)} %collective-permute-done.73, f32[24,768]{1,0:T(8,128)} %collective-permute-done.72, f32[24,768]{1,0:T(8,128)} %collective-permute-done.71, f32[24,768]{1,0:T(8,128)} %collective-permute-done.70, ...), dimensions={0} | concatenate | bytes 4829184
  (391 shorter events, 146.0 us)
Async XLA Ops:
  7.2 1164.9 %all-reduce.58.cloned.1.call-start = ((), (), s32[]{:S(2)}) async-start(), calls=%async_computation.2 | async-start | bytes 7077888
  12.8 33.5 %collective-permute-start = (f32[1,3,768]{2,1,0:T(4,128)}, f32[1,3,768]{2,1,0:T(4,128)S(1)}, u32[]{:S(2)}, u32[]{:S(2)}) collective-permute-start(f32[1,3,768]{2,1,0:T(4,128)} %get-tuple-element.81), channel_id=1, source_target_pairs={{0,1},{1,2},{2,3},{3,4},{4,5},{5,6},{6,7},{8,9},{9,10},{10,11},{11... | collective-permute-start | bytes 27656 | tf_op jit(solution)/shard_map/ppermute | solution.py:16
  16.7 29.6 %collective-permute-start.1 = (f32[1,3,768]{2,1,0:T(4,128)}, f32[1,3,768]{2,1,0:T(4,128)}, u32[]{:S(2)}, u32[]{:S(2)}) collective-permute-start(f32[1,3,768]{2,1,0:T(4,128)} %get-tuple-element.82), channel_id=1, source_target_pairs={{1,0},{2,1},{3,2},{4,3},{5,4},{6,5},{7,6},{9,8},{10,9},{11,10},{12... | collective-permute-start | bytes 27656 | tf_op jit(solution)/shard_map/ppermute | solution.py:19
  60.4 10.6 collective-permute-start.2
  212.4 961.2 %reduce-scatter.7.cloned.1.call-start = ((), (), s32[]{:S(2)}) async-start(), calls=%async_computation.1 | async-start | bytes 6340608 | tf_op jit(solution)/shard_map/reduce_scatter | solution.py:318
  741.4 61.2 %collective-permute-start.42 = (f32[8,2304]{1,0:T(8,128)}, f32[8,2304]{1,0:T(8,128)}, u32[]{:S(2)}, u32[]{:S(2)}) collective-permute-start(f32[8,2304]{1,0:T(8,128)} %get-tuple-element.36), channel_id=1, source_target_pairs={{0,31},{1,32},{2,33},{3,34},{4,35},{5,36},{6,37},{7,38},{8,39},{9,... | collective-permute-start | bytes 221192
  755.3 50.9 %collective-permute-start.41 = (f32[8,2304]{1,0:T(8,128)}, f32[8,2304]{1,0:T(8,128)}, u32[]{:S(2)}, u32[]{:S(2)}) collective-permute-start(f32[8,2304]{1,0:T(8,128)} %get-tuple-element.36), channel_id=1, source_target_pairs={{0,30},{1,31},{2,32},{3,33},{4,34},{5,35},{6,36},{7,37},{8,38},{9,... | collective-permute-start | bytes 221192
  766.4 28.3 %collective-permute-start.75 = (f32[18,768]{1,0:T(8,128)S(1)}, f32[18,768]{1,0:T(8,128)S(1)}, u32[]{:S(2)}, u32[]{:S(2)}) collective-permute-start(f32[18,768]{1,0:T(8,128)S(1)} %slice.352), channel_id=1, source_target_pairs={{0,32},{1,33},{2,34},{3,35},{4,36},{5,37},{6,38},{7,39},{8,40},{9,... | collective-permute-start | bytes 165896
  776.9 22.5 %collective-permute-start.43 = (f32[6,2304]{1,0:T(8,128)S(1)}, f32[6,2304]{1,0:T(8,128)S(1)}, u32[]{:S(2)}, u32[]{:S(2)}) collective-permute-start(f32[6,2304]{1,0:T(8,128)S(1)} %slice.351), channel_id=1, source_target_pairs={{0,32},{1,33},{2,34},{3,35},{4,36},{5,37},{6,38},{7,39},{8,40},{9,... | collective-permute-start | bytes 165896
  787.1 21.5 %collective-permute-start.40 = (f32[8,2304]{1,0:T(8,128)}, f32[8,2304]{1,0:T(8,128)}, u32[]{:S(2)}, u32[]{:S(2)}) collective-permute-start(f32[8,2304]{1,0:T(8,128)} %get-tuple-element.36), channel_id=1, source_target_pairs={{0,29},{1,30},{2,31},{3,32},{4,33},{5,34},{6,35},{7,36},{8,37},{9,... | collective-permute-start | bytes 221192
  794.8 15.7 %collective-permute-start.39 = (f32[8,2304]{1,0:T(8,128)}, f32[8,2304]{1,0:T(8,128)}, u32[]{:S(2)}, u32[]{:S(2)}) collective-permute-start(f32[8,2304]{1,0:T(8,128)} %get-tuple-element.36), channel_id=1, source_target_pairs={{0,28},{1,29},{2,30},{3,31},{4,32},{5,33},{6,34},{7,35},{8,36},{9,... | collective-permute-start | bytes 221192
  799.4 16.3 %collective-permute-start.38 = (f32[8,2304]{1,0:T(8,128)}, f32[8,2304]{1,0:T(8,128)}, u32[]{:S(2)}, u32[]{:S(2)}) collective-permute-start(f32[8,2304]{1,0:T(8,128)} %get-tuple-element.36), channel_id=1, source_target_pairs={{0,27},{1,28},{2,29},{3,30},{4,31},{5,32},{6,33},{7,34},{8,35},{9,... | collective-permute-start | bytes 221192
  802.6 15.7 %collective-permute-start.37 = (f32[8,2304]{1,0:T(8,128)}, f32[8,2304]{1,0:T(8,128)}, u32[]{:S(2)}, u32[]{:S(2)}) collective-permute-start(f32[8,2304]{1,0:T(8,128)} %get-tuple-element.36), channel_id=1, source_target_pairs={{0,26},{1,27},{2,28},{3,29},{4,30},{5,31},{6,32},{7,33},{8,34},{9,... | collective-permute-start | bytes 221192
  806.1 15.6 %collective-permute-start.36 = (f32[8,2304]{1,0:T(8,128)}, f32[8,2304]{1,0:T(8,128)}, u32[]{:S(2)}, u32[]{:S(2)}) collective-permute-start(f32[8,2304]{1,0:T(8,128)} %get-tuple-element.36), channel_id=1, source_target_pairs={{0,25},{1,26},{2,27},{3,28},{4,29},{5,30},{6,31},{7,32},{8,33},{9,... | collective-permute-start | bytes 221192
  808.6 15.4 %collective-permute-start.35 = (f32[8,2304]{1,0:T(8,128)}, f32[8,2304]{1,0:T(8,128)}, u32[]{:S(2)}, u32[]{:S(2)}) collective-permute-start(f32[8,2304]{1,0:T(8,128)} %get-tuple-element.36), channel_id=1, source_target_pairs={{0,24},{1,25},{2,26},{3,27},{4,28},{5,29},{6,30},{7,31},{8,32},{9,... | collective-permute-start | bytes 221192
  810.5 15.4 %collective-permute-start.34 = (f32[8,2304]{1,0:T(8,128)}, f32[8,2304]{1,0:T(8,128)}, u32[]{:S(2)}, u32[]{:S(2)}) collective-permute-start(f32[8,2304]{1,0:T(8,128)} %get-tuple-element.36), channel_id=1, source_target_pairs={{0,23},{1,24},{2,25},{3,26},{4,27},{5,28},{6,29},{7,30},{8,31},{9,... | collective-permute-start | bytes 221192
  815.7 12.0 %collective-permute-start.33 = (f32[8,2304]{1,0:T(8,128)}, f32[8,2304]{1,0:T(8,128)}, u32[]{:S(2)}, u32[]{:S(2)}) collective-permute-start(f32[8,2304]{1,0:T(8,128)} %get-tuple-element.36), channel_id=1, source_target_pairs={{0,22},{1,23},{2,24},{3,25},{4,26},{5,27},{6,28},{7,29},{8,30},{9,... | collective-permute-start | bytes 221192
  818.3 12.6 %collective-permute-start.32 = (f32[8,2304]{1,0:T(8,128)}, f32[8,2304]{1,0:T(8,128)}, u32[]{:S(2)}, u32[]{:S(2)}) collective-permute-start(f32[8,2304]{1,0:T(8,128)} %get-tuple-element.36), channel_id=1, source_target_pairs={{0,21},{1,22},{2,23},{3,24},{4,25},{5,26},{6,27},{7,28},{8,29},{9,... | collective-permute-start | bytes 221192
  821.7 11.0 collective-permute-start.31
  823.9 11.9 %collective-permute-start.30 = (f32[8,2304]{1,0:T(8,128)}, f32[8,2304]{1,0:T(8,128)}, u32[]{:S(2)}, u32[]{:S(2)}) collective-permute-start(f32[8,2304]{1,0:T(8,128)} %get-tuple-element.36), channel_id=1, source_target_pairs={{0,19},{1,20},{2,21},{3,22},{4,23},{5,24},{6,25},{7,26},{8,27},{9,... | collective-permute-start | bytes 221192
  825.9 11.9 %collective-permute-start.29 = (f32[8,2304]{1,0:T(8,128)}, f32[8,2304]{1,0:T(8,128)}, u32[]{:S(2)}, u32[]{:S(2)}) collective-permute-start(f32[8,2304]{1,0:T(8,128)} %get-tuple-element.36), channel_id=1, source_target_pairs={{0,18},{1,19},{2,20},{3,21},{4,22},{5,23},{6,24},{7,25},{8,26},{9,... | collective-permute-start | bytes 221192
  827.8 12.9 %collective-permute-start.28 = (f32[8,2304]{1,0:T(8,128)}, f32[8,2304]{1,0:T(8,128)}, u32[]{:S(2)}, u32[]{:S(2)}) collective-permute-start(f32[8,2304]{1,0:T(8,128)} %get-tuple-element.36), channel_id=1, source_target_pairs={{0,17},{1,18},{2,19},{3,20},{4,21},{5,22},{6,23},{7,24},{8,25},{9,... | collective-permute-start | bytes 221192
  830.8 14.7 %collective-permute-start.27 = (f32[8,2304]{1,0:T(8,128)}, f32[8,2304]{1,0:T(8,128)}, u32[]{:S(2)}, u32[]{:S(2)}) collective-permute-start(f32[8,2304]{1,0:T(8,128)} %get-tuple-element.36), channel_id=1, source_target_pairs={{0,16},{1,17},{2,18},{3,19},{4,20},{5,21},{6,22},{7,23},{8,24},{9,... | collective-permute-start | bytes 221192
  832.8 14.7 %collective-permute-start.26 = (f32[8,2304]{1,0:T(8,128)}, f32[8,2304]{1,0:T(8,128)}, u32[]{:S(2)}, u32[]{:S(2)}) collective-permute-start(f32[8,2304]{1,0:T(8,128)} %get-tuple-element.36), channel_id=1, source_target_pairs={{0,15},{1,16},{2,17},{3,18},{4,19},{5,20},{6,21},{7,22},{8,23},{9,... | collective-permute-start | bytes 221192
  835.8 13.7 %collective-permute-start.25 = (f32[8,2304]{1,0:T(8,128)}, f32[8,2304]{1,0:T(8,128)}, u32[]{:S(2)}, u32[]{:S(2)}) collective-permute-start(f32[8,2304]{1,0:T(8,128)} %get-tuple-element.36), channel_id=1, source_target_pairs={{0,14},{1,15},{2,16},{3,17},{4,18},{5,19},{6,20},{7,21},{8,22},{9,... | collective-permute-start | bytes 221192
  837.7 15.0 %collective-permute-start.24 = (f32[8,2304]{1,0:T(8,128)}, f32[8,2304]{1,0:T(8,128)}, u32[]{:S(2)}, u32[]{:S(2)}) collective-permute-start(f32[8,2304]{1,0:T(8,128)} %get-tuple-element.36), channel_id=1, source_target_pairs={{0,13},{1,14},{2,15},{3,16},{4,17},{5,18},{6,19},{7,20},{8,21},{9,... | collective-permute-start | bytes 221192
  840.6 14.0 %collective-permute-start.23 = (f32[8,2304]{1,0:T(8,128)}, f32[8,2304]{1,0:T(8,128)}, u32[]{:S(2)}, u32[]{:S(2)}) collective-permute-start(f32[8,2304]{1,0:T(8,128)} %get-tuple-element.36), channel_id=1, source_target_pairs={{0,12},{1,13},{2,14},{3,15},{4,16},{5,17},{6,18},{7,19},{8,20},{9,... | collective-permute-start | bytes 221192
  845.6 13.8 %collective-permute-start.22 = (f32[8,2304]{1,0:T(8,128)}, f32[8,2304]{1,0:T(8,128)}, u32[]{:S(2)}, u32[]{:S(2)}) collective-permute-start(f32[8,2304]{1,0:T(8,128)} %get-tuple-element.36), channel_id=1, source_target_pairs={{0,11},{1,12},{2,13},{3,14},{4,15},{5,16},{6,17},{7,18},{8,19},{9,... | collective-permute-start | bytes 221192
  847.5 15.5 %collective-permute-start.21 = (f32[8,2304]{1,0:T(8,128)}, f32[8,2304]{1,0:T(8,128)}, u32[]{:S(2)}, u32[]{:S(2)}) collective-permute-start(f32[8,2304]{1,0:T(8,128)} %get-tuple-element.36), channel_id=1, source_target_pairs={{0,10},{1,11},{2,12},{3,13},{4,14},{5,15},{6,16},{7,17},{8,18},{9,... | collective-permute-start | bytes 221192
  849.6 15.4 %collective-permute-start.20 = (f32[8,2304]{1,0:T(8,128)}, f32[8,2304]{1,0:T(8,128)}, u32[]{:S(2)}, u32[]{:S(2)}) collective-permute-start(f32[8,2304]{1,0:T(8,128)} %get-tuple-element.36), channel_id=1, source_target_pairs={{0,9},{1,10},{2,11},{3,12},{4,13},{5,14},{6,15},{7,16},{8,17},{9,1... | collective-permute-start | bytes 221192
  852.7 17.4 %collective-permute-start.19 = (f32[8,2304]{1,0:T(8,128)}, f32[8,2304]{1,0:T(8,128)}, u32[]{:S(2)}, u32[]{:S(2)}) collective-permute-start(f32[8,2304]{1,0:T(8,128)} %get-tuple-element.36), channel_id=1, source_target_pairs={{0,8},{1,9},{2,10},{3,11},{4,12},{5,13},{6,14},{7,15},{8,16},{9,17... | collective-permute-start | bytes 221192
  854.6 17.9 %collective-permute-start.18 = (f32[8,2304]{1,0:T(8,128)}, f32[8,2304]{1,0:T(8,128)}, u32[]{:S(2)}, u32[]{:S(2)}) collective-permute-start(f32[8,2304]{1,0:T(8,128)} %get-tuple-element.36), channel_id=1, source_target_pairs={{0,7},{1,8},{2,9},{3,10},{4,11},{5,12},{6,13},{7,14},{8,15},{9,16}... | collective-permute-start | bytes 221192
  859.3 16.3 %collective-permute-start.17 = (f32[8,2304]{1,0:T(8,128)}, f32[8,2304]{1,0:T(8,128)}, u32[]{:S(2)}, u32[]{:S(2)}) collective-permute-start(f32[8,2304]{1,0:T(8,128)} %get-tuple-element.36), channel_id=1, source_target_pairs={{0,6},{1,7},{2,8},{3,9},{4,10},{5,11},{6,12},{7,13},{8,14},{9,15},... | collective-permute-start | bytes 221192
  863.0 16.6 %collective-permute-start.16 = (f32[8,2304]{1,0:T(8,128)}, f32[8,2304]{1,0:T(8,128)}, u32[]{:S(2)}, u32[]{:S(2)}) collective-permute-start(f32[8,2304]{1,0:T(8,128)} %get-tuple-element.36), channel_id=1, source_target_pairs={{0,5},{1,6},{2,7},{3,8},{4,9},{5,10},{6,11},{7,12},{8,13},{9,14},{... | collective-permute-start | bytes 221192
  864.9 16.6 %collective-permute-start.15 = (f32[8,2304]{1,0:T(8,128)}, f32[8,2304]{1,0:T(8,128)}, u32[]{:S(2)}, u32[]{:S(2)}) collective-permute-start(f32[8,2304]{1,0:T(8,128)} %get-tuple-element.36), channel_id=1, source_target_pairs={{0,4},{1,5},{2,6},{3,7},{4,8},{5,9},{6,10},{7,11},{8,12},{9,13},{1... | collective-permute-start | bytes 221192
  870.1 13.4 %collective-permute-start.14 = (f32[8,2304]{1,0:T(8,128)}, f32[8,2304]{1,0:T(8,128)}, u32[]{:S(2)}, u32[]{:S(2)}) collective-permute-start(f32[8,2304]{1,0:T(8,128)} %get-tuple-element.36), channel_id=1, source_target_pairs={{0,3},{1,4},{2,5},{3,6},{4,7},{5,8},{6,9},{7,10},{8,11},{9,12},{10... | collective-permute-start | bytes 221192
  872.5 12.9 %collective-permute-start.13 = (f32[8,2304]{1,0:T(8,128)}, f32[8,2304]{1,0:T(8,128)}, u32[]{:S(2)}, u32[]{:S(2)}) collective-permute-start(f32[8,2304]{1,0:T(8,128)} %get-tuple-element.36), channel_id=1, source_target_pairs={{0,2},{1,3},{2,4},{3,5},{4,6},{5,7},{6,8},{7,9},{8,10},{9,11},{10,... | collective-permute-start | bytes 221192
  875.7 11.6 collective-permute-start.12
  889.2 9.6 collective-permute-start.69
  891.1 10.4 collective-permute-start.68
  893.0 11.5 collective-permute-start.67
  895.0 11.6 collective-permute-start.66
  896.9 12.4 %collective-permute-start.65 = (f32[24,768]{1,0:T(8,128)}, f32[24,768]{1,0:T(8,128)}, u32[]{:S(2)}, u32[]{:S(2)}) collective-permute-start(f32[24,768]{1,0:T(8,128)} %get-tuple-element.37), channel_id=1, source_target_pairs={{0,22},{1,23},{2,24},{3,25},{4,26},{5,27},{6,28},{7,29},{8,30},{9,... | collective-permute-start | bytes 221192
  898.8 13.4 %collective-permute-start.64 = (f32[24,768]{1,0:T(8,128)}, f32[24,768]{1,0:T(8,128)}, u32[]{:S(2)}, u32[]{:S(2)}) collective-permute-start(f32[24,768]{1,0:T(8,128)} %get-tuple-element.37), channel_id=1, source_target_pairs={{0,21},{1,22},{2,23},{3,24},{4,25},{5,26},{6,27},{7,28},{8,29},{9,... | collective-permute-start | bytes 221192
  901.5 12.7 %collective-permute-start.63 = (f32[24,768]{1,0:T(8,128)}, f32[24,768]{1,0:T(8,128)}, u32[]{:S(2)}, u32[]{:S(2)}) collective-permute-start(f32[24,768]{1,0:T(8,128)} %get-tuple-element.37), channel_id=1, source_target_pairs={{0,20},{1,21},{2,22},{3,23},{4,24},{5,25},{6,26},{7,27},{8,28},{9,... | collective-permute-start | bytes 221192
  904.6 11.9 %collective-permute-start.62 = (f32[24,768]{1,0:T(8,128)}, f32[24,768]{1,0:T(8,128)}, u32[]{:S(2)}, u32[]{:S(2)}) collective-permute-start(f32[24,768]{1,0:T(8,128)} %get-tuple-element.37), channel_id=1, source_target_pairs={{0,19},{1,20},{2,21},{3,22},{4,23},{5,24},{6,25},{7,26},{8,27},{9,... | collective-permute-start | bytes 221192
  906.5 13.4 %collective-permute-start.61 = (f32[24,768]{1,0:T(8,128)}, f32[24,768]{1,0:T(8,128)}, u32[]{:S(2)}, u32[]{:S(2)}) collective-permute-start(f32[24,768]{1,0:T(8,128)} %get-tuple-element.37), channel_id=1, source_target_pairs={{0,18},{1,19},{2,20},{3,21},{4,22},{5,23},{6,24},{7,25},{8,26},{9,... | collective-permute-start | bytes 221192
  909.3 12.7 %collective-permute-start.60 = (f32[24,768]{1,0:T(8,128)}, f32[24,768]{1,0:T(8,128)}, u32[]{:S(2)}, u32[]{:S(2)}) collective-permute-start(f32[24,768]{1,0:T(8,128)} %get-tuple-element.37), channel_id=1, source_target_pairs={{0,17},{1,18},{2,19},{3,20},{4,21},{5,22},{6,23},{7,24},{8,25},{9,... | collective-permute-start | bytes 221192
  912.2 13.7 %collective-permute-start.59 = (f32[24,768]{1,0:T(8,128)}, f32[24,768]{1,0:T(8,128)}, u32[]{:S(2)}, u32[]{:S(2)}) collective-permute-start(f32[24,768]{1,0:T(8,128)} %get-tuple-element.37), channel_id=1, source_target_pairs={{0,16},{1,17},{2,18},{3,19},{4,20},{5,21},{6,22},{7,23},{8,24},{9,... | collective-permute-start | bytes 221192
  914.3 52.6 %collective-permute-start.58 = (f32[24,768]{1,0:T(8,128)}, f32[24,768]{1,0:T(8,128)}, u32[]{:S(2)}, u32[]{:S(2)}) collective-permute-start(f32[24,768]{1,0:T(8,128)} %get-tuple-element.37), channel_id=1, source_target_pairs={{0,15},{1,16},{2,17},{3,18},{4,19},{5,20},{6,21},{7,22},{8,23},{9,... | collective-permute-start | bytes 221192
  916.5 52.7 %collective-permute-start.57 = (f32[24,768]{1,0:T(8,128)}, f32[24,768]{1,0:T(8,128)}, u32[]{:S(2)}, u32[]{:S(2)}) collective-permute-start(f32[24,768]{1,0:T(8,128)} %get-tuple-element.37), channel_id=1, source_target_pairs={{0,14},{1,15},{2,16},{3,17},{4,18},{5,19},{6,20},{7,21},{8,22},{9,... | collective-permute-start | bytes 221192
  919.9 52.7 %collective-permute-start.56 = (f32[24,768]{1,0:T(8,128)}, f32[24,768]{1,0:T(8,128)}, u32[]{:S(2)}, u32[]{:S(2)}) collective-permute-start(f32[24,768]{1,0:T(8,128)} %get-tuple-element.37), channel_id=1, source_target_pairs={{0,13},{1,14},{2,15},{3,16},{4,17},{5,18},{6,19},{7,20},{8,21},{9,... | collective-permute-start | bytes 221192
  922.0 52.5 %collective-permute-start.55 = (f32[24,768]{1,0:T(8,128)}, f32[24,768]{1,0:T(8,128)}, u32[]{:S(2)}, u32[]{:S(2)}) collective-permute-start(f32[24,768]{1,0:T(8,128)} %get-tuple-element.37), channel_id=1, source_target_pairs={{0,12},{1,13},{2,14},{3,15},{4,16},{5,17},{6,18},{7,19},{8,20},{9,... | collective-permute-start | bytes 221192
  925.9 51.4 %collective-permute-start.54 = (f32[24,768]{1,0:T(8,128)}, f32[24,768]{1,0:T(8,128)}, u32[]{:S(2)}, u32[]{:S(2)}) collective-permute-start(f32[24,768]{1,0:T(8,128)} %get-tuple-element.37), channel_id=1, source_target_pairs={{0,11},{1,12},{2,13},{3,14},{4,15},{5,16},{6,17},{7,18},{8,19},{9,... | collective-permute-start | bytes 221192
  966.9 79.2 %collective-permute-start.53 = (f32[24,768]{1,0:T(8,128)}, f32[24,768]{1,0:T(8,128)}, u32[]{:S(2)}, u32[]{:S(2)}) collective-permute-start(f32[24,768]{1,0:T(8,128)} %get-tuple-element.37), channel_id=1, source_target_pairs={{0,10},{1,11},{2,12},{3,13},{4,14},{5,15},{6,16},{7,17},{8,18},{9,... | collective-permute-start | bytes 221192
  969.2 82.0 %collective-permute-start.52 = (f32[24,768]{1,0:T(8,128)}, f32[24,768]{1,0:T(8,128)}, u32[]{:S(2)}, u32[]{:S(2)}) collective-permute-start(f32[24,768]{1,0:T(8,128)} %get-tuple-element.37), channel_id=1, source_target_pairs={{0,9},{1,10},{2,11},{3,12},{4,13},{5,14},{6,15},{7,16},{8,17},{9,1... | collective-permute-start | bytes 221192
  972.6 81.7 %collective-permute-start.51 = (f32[24,768]{1,0:T(8,128)}, f32[24,768]{1,0:T(8,128)}, u32[]{:S(2)}, u32[]{:S(2)}) collective-permute-start(f32[24,768]{1,0:T(8,128)} %get-tuple-element.37), channel_id=1, source_target_pairs={{0,8},{1,9},{2,10},{3,11},{4,12},{5,13},{6,14},{7,15},{8,16},{9,17... | collective-permute-start | bytes 221192
  974.5 82.3 %collective-permute-start.50 = (f32[24,768]{1,0:T(8,128)}, f32[24,768]{1,0:T(8,128)}, u32[]{:S(2)}, u32[]{:S(2)}) collective-permute-start(f32[24,768]{1,0:T(8,128)} %get-tuple-element.37), channel_id=1, source_target_pairs={{0,7},{1,8},{2,9},{3,10},{4,11},{5,12},{6,13},{7,14},{8,15},{9,16}... | collective-permute-start | bytes 221192
  977.3 83.1 %collective-permute-start.49 = (f32[24,768]{1,0:T(8,128)}, f32[24,768]{1,0:T(8,128)}, u32[]{:S(2)}, u32[]{:S(2)}) collective-permute-start(f32[24,768]{1,0:T(8,128)} %get-tuple-element.37), channel_id=1, source_target_pairs={{0,6},{1,7},{2,8},{3,9},{4,10},{5,11},{6,12},{7,13},{8,14},{9,15},... | collective-permute-start | bytes 221192
  1046.1 73.2 %collective-permute-start.48 = (f32[24,768]{1,0:T(8,128)}, f32[24,768]{1,0:T(8,128)}, u32[]{:S(2)}, u32[]{:S(2)}) collective-permute-start(f32[24,768]{1,0:T(8,128)} %get-tuple-element.37), channel_id=1, source_target_pairs={{0,5},{1,6},{2,7},{3,8},{4,9},{5,10},{6,11},{7,12},{8,13},{9,14},{... | collective-permute-start | bytes 221192
  1051.2 68.0 %collective-permute-start.47 = (f32[24,768]{1,0:T(8,128)}, f32[24,768]{1,0:T(8,128)}, u32[]{:S(2)}, u32[]{:S(2)}) collective-permute-start(f32[24,768]{1,0:T(8,128)} %get-tuple-element.37), channel_id=1, source_target_pairs={{0,4},{1,5},{2,6},{3,7},{4,8},{5,9},{6,10},{7,11},{8,12},{9,13},{1... | collective-permute-start | bytes 221192
  1054.2 65.0 %collective-permute-start.46 = (f32[24,768]{1,0:T(8,128)}, f32[24,768]{1,0:T(8,128)}, u32[]{:S(2)}, u32[]{:S(2)}) collective-permute-start(f32[24,768]{1,0:T(8,128)} %get-tuple-element.37), channel_id=1, source_target_pairs={{0,3},{1,4},{2,5},{3,6},{4,7},{5,8},{6,9},{7,10},{8,11},{9,12},{10... | collective-permute-start | bytes 221192
  1056.8 62.5 %collective-permute-start.45 = (f32[24,768]{1,0:T(8,128)}, f32[24,768]{1,0:T(8,128)}, u32[]{:S(2)}, u32[]{:S(2)}) collective-permute-start(f32[24,768]{1,0:T(8,128)} %get-tuple-element.37), channel_id=1, source_target_pairs={{0,2},{1,3},{2,4},{3,5},{4,6},{5,7},{6,8},{7,9},{8,10},{9,11},{10,... | collective-permute-start | bytes 221192
  1060.4 58.8 %collective-permute-start.44 = (f32[24,768]{1,0:T(8,128)}, f32[24,768]{1,0:T(8,128)}, u32[]{:S(2)}, u32[]{:S(2)}) collective-permute-start(f32[24,768]{1,0:T(8,128)} %get-tuple-element.37), channel_id=1, source_target_pairs={{0,1},{1,2},{2,3},{3,4},{4,5},{5,6},{6,7},{7,8},{8,9},{9,10},{10,1... | collective-permute-start | bytes 221192
  (103 other events, 3360.5 us)
Sparse Core Ops, SparseCore 0:
  212.5 170.4 all-reduce.57
  385.9 654.9 reduce-scatter.6
where the time goes:
time: 1200 us; the launch traced here: 1180 us
  blocking collectives  619 us (52%)
  starting transfers between devices  248 us (21%)
  local copies, waits for them, and re-layouts  146 us (12%)
  other arithmetic  86.7 us (7%)
  matrix products  45.4 us (4%)
  between operations  22.3 us (2%)
  waiting for transfers between devices  14.5 us (1%)
    unnamed x2, blocking collectives  565 us
    unnamed x65, starting transfers between devices  215 us
    unnamed x190, local copies, waits for them, and re-layouts  119 us
    psum x1, blocking collectives, body(): lax.psum(jnp.sum(per_clip_loss(clip_stats, frame_total)), 'dp')  34.4 us
    ppermute x6, starting transfers between devices, extended_2(): lax.ppermute(lax.slice_in_dim(block, block.shape[dim] - width, None, axis...  24.9 us
    another operation x3, other arithmetic  24.5 us
  transfers between devices with their start and end apart: 78, of which 5 were waited for; matrix products, arithmetic and copies ran while one was open for 56% of the time, Pallas kernels for 0%

commit v1 on v0

v1 whole, which is shorter than its diff:
```python
import jax
import jax.numpy as jnp
import ml_dtypes
import numpy as np
from jax import lax
from jax.experimental import pallas as pl
from jax.experimental.pallas import tpu as pltpu
from jax.sharding import PartitionSpec as P

F32, BF16 = jnp.float32, jnp.bfloat16
MESH = pl.DeviceIdType.MESH
D, FF = 768, 2304
HOP, NFFT = 256, 1024
FRAMES, OWN, HALO = 1024, 128, 16
ROWS = OWN + 2 * HALO
CHUNKS1, CHUNKS2 = 5, 3
WIDE1, WIDE2 = CHUNKS1 * 256, CHUNKS2 * 256
CLIPS = 16
MB = 1 << 20
ORDERS = ("xyz", "yzx", "zxy")
HEAD_BLOCKS = ((0, 2), (2, 3), (5, 4))
PART_ROWS = (18 * 24 + 2 * 24, 6 * 72 + 3 * 24, 6 * 64 + 4 * 24)


def bf(array):
    return np.asarray(array, np.float32).astype(ml_dtypes.bfloat16)


def hann(length):
    return 0.5 - 0.5 * np.cos(2.0 * np.pi * np.arange(length) / length)


def angles(length):
    product = np.arange(length // 2 + 1)[:, None] * np.arange(length)[None, :] % length
    return 2.0 * np.pi * product / length


def interleave(real, imag, chunks):
    bins, width = real.shape
    out = np.zeros((chunks, 2, 128, width), np.float64)
    for half, part in enumerate((real, imag)):
        padded = np.zeros((chunks * 128, width), np.float64)
        padded[:bins] = part
        out[:, half] = padded.reshape(chunks, 128, width)
    return out.reshape(chunks * 256, width)


def make_constants():
    ang = angles(NFFT)
    bins = np.arange(NFFT // 2 + 1)
    factor = np.where((bins == 0) | (bins == NFFT // 2), 1.0, 2.0)[:, None] / NFFT
    window = hann(NFFT)[None, :]
    synthesis = bf(interleave(factor * np.cos(ang) * window, -factor * np.sin(ang) * window, CHUNKS1))
    analysis1 = bf(interleave(np.cos(ang), -np.sin(ang), CHUNKS1).T)
    ang = angles(NFFT // 2)
    analysis2 = bf(interleave(np.cos(ang), -np.sin(ang), CHUNKS2).T)
    win = np.zeros((8, NFFT), np.float32)
    win[0] = hann(NFFT)
    win[1] = hann(NFFT) ** 2
    win[2, : NFFT // 2] = hann(NFFT // 2)
    return synthesis, analysis1, analysis2, win


def device_index(x, y, z, core):
    return ((y * 2 + z // 2) * 2 + core) * 8 + x * 2 + z % 2


def shard_order(order, core):
    places = []
    for a in range(4):
        for b in range(4):
            for c in range(4):
                at = dict(zip(order, (a, b, c)))
                places.append(device_index(at["x"], at["y"], at["z"], core))
    return np.array(places)


def columns_of(order, core, each):
    return (shard_order(order, core)[:, None] * each + np.arange(each)[None, :]).reshape(-1)


def one_hot_columns(sources, size):
    out = np.zeros((size, sources.size), np.float32)
    out[sources, np.arange(sources.size)] = 1.0
    return bf(out)


def make_orders():
    pick_n = np.stack([one_hot_columns(columns_of(ORDERS[0], c, 6), D) for c in (0, 1)])
    half = [columns_of(ORDERS[1], c, 18)[: 4 * 4 * 2 * 18] for c in (0, 1)]
    pick_h = np.stack([one_hot_columns(h, FF // 2) for h in half])
    pick_k = np.stack([one_hot_columns(columns_of(ORDERS[2], c, 6), D) for c in (0, 1)])
    first = columns_of(ORDERS[0], 0, 6)
    where = {col: i for i, col in enumerate(first)}
    turns = []
    for k in (1, 2):
        sources = np.array([where[col] for col in columns_of(ORDERS[k], 0, 6)])
        turns.append(one_hot_columns(sources, 384))
    row_id = columns_of(ORDERS[2], 0, 16).astype(np.float32)[None, :]
    return pick_n, pick_h, pick_k, turns[0], turns[1], row_id


def mm(a, b):
    return jnp.dot(a, b, preferred_element_type=F32)


def mm_bt(a, b):
    return lax.dot_general(a, b, (((1,), (1,)), ((), ())), preferred_element_type=F32)


def mm_at(a, b):
    return lax.dot_general(a, b, (((0,), (0,)), ((), ())), preferred_element_type=F32)


def shift(values, by):
    by = by % values.shape[0]
    return values if by == 0 else pltpu.roll(values, by, 0)


def norm(values):
    centre = values - jnp.mean(values, axis=-1, keepdims=True)
    rstd = lax.rsqrt(jnp.mean(centre * centre, axis=-1, keepdims=True) + 1e-6)
    return centre * rstd, rstd


def norm_back(grad, y, rstd):
    mean_g = jnp.mean(grad, axis=-1, keepdims=True)
    mean_gy = jnp.mean(grad * y, axis=-1, keepdims=True)
    return rstd * (grad - mean_g - y * mean_gy)


def frame_places(comb):
    first = comb[HALO : HALO + 1, 258:259]
    rows = lax.broadcasted_iota(jnp.int32, (ROWS, 1), 0).astype(F32)
    return first + rows - float(HALO)


def inside(places):
    return (places >= 0.0) & (places < float(FRAMES))


def envelope(places, win):
    total = jnp.zeros((ROWS, HOP), F32)
    for p in range(4):
        total = total + jnp.where(inside(places + float(2 - p)), win[1:2, HOP * p : HOP * (p + 1)], 0.0)
    return jnp.where(inside(places), total, 1.0)


def spec(space):
    return pl.BlockSpec(memory_space=space)


def full(*shape, dtype=F32):
    return jax.ShapeDtypeStruct(shape, dtype)


def halo_kernel(comb, out, send, recv):
    tm = lax.axis_index("tm")
    right, left = lax.rem(tm + 1, 8), lax.rem(tm + 7, 8)
    barrier = pltpu.get_barrier_semaphore()
    for there in (left, right):
        pl.semaphore_signal(barrier, inc=1, device_id={"tm": there}, device_id_type=MESH)
    pl.semaphore_wait(barrier, 2)
    copies = []
    for i, (src, dst, there) in enumerate(
        ((OWN - HALO, 0, right), (0, OWN + HALO, left))
    ):
        copies.append(
            pltpu.make_async_remote_copy(
                src_ref=comb.at[pl.ds(src, HALO)],
                dst_ref=out.at[pl.ds(dst, HALO)],
                send_sem=send.at[i],
                recv_sem=recv.at[i],
                device_id={"tm": there},
                device_id_type=MESH,
            )
        )
    for copy in copies:
        copy.start()
    out[HALO : HALO + OWN, :] = comb[...]
    for copy in copies:
        copy.wait()


def halo_call(comb):
    return pl.pallas_call(
        halo_kernel,
        out_shape=full(ROWS, 384),
        in_specs=[spec(pltpu.VMEM)],
        out_specs=spec(pltpu.VMEM),
        scratch_shapes=[pltpu.SemaphoreType.DMA((2,)), pltpu.SemaphoreType.DMA((2,))],
        compiler_params=pltpu.CompilerParams(collective_id=0, has_side_effects=True),
        name="halo",
    )(comb)


def forward_kernel(
    comb, kern, scale, win, table_h, up_h, down_h, head_h, syn_h, a1_h, a2_h,
    sin_o, rstd_o, y1_o, gp_o, hid_o, down_o, y2_o, re_o, im_o, d1_o, q1_o, d2_o, q2_o, stat_o,
    table_v, up_v, down_v, head_v, syn_v, a1_v, a2_v, hid_v, spec_v, seg1, seg2, sems,
):
    pairs = (
        (table_h, table_v), (up_h, up_v), (down_h, down_v), (head_h, head_v),
        (syn_h, syn_v), (a1_h, a1_v), (a2_h, a2_v),
    )
    copies = [pltpu.make_async_copy(h, v, sems.at[i]) for i, (h, v) in enumerate(pairs)]
    for copy in copies:
        copy.start()
    places = frame_places(comb)
    valid = inside(places)
    lane = lax.broadcasted_iota(jnp.int32, (ROWS, 2 * FRAMES), 1).astype(F32)
    hot = (lane == comb[:, 256:257]) | (lane == comb[:, 257:258] + 1024.0)
    hot = jnp.where(hot, 1.0, 0.0).astype(BF16)
    copies[0].wait()
    y0, rstd0 = norm(mm(hot, table_v[...]))
    y0 = jnp.where(valid, y0, 0.0)
    sin_o[...] = y0
    mixture = kern[0:1, :] * shift(y0, 3)
    for k in range(1, 7):
        mixture = mixture + kern[k : k + 1, :] * shift(y0, 3 - k)
    y1, rstd1 = norm(mixture)
    y1_o[...] = y1
    normed = y1.astype(BF16)
    copies[1].wait()
    for c in range(FF // 256):
        at = slice(256 * c, 256 * (c + 1))
        up = mm(normed, up_v[:, at])
        cdf = 0.5 * (1.0 + lax.erf(up * 0.7071067811865476))
        hid_v[:, at] = (up * cdf).astype(BF16)
        gp_o[:, at] = cdf + up * (0.3989422804014327 * jnp.exp(-0.5 * up * up))
    hid_o[...] = hid_v[HALO : HALO + OWN, :]
    copies[2].wait()
    down = mm(hid_v[...], down_v[...])
    down_o[...] = down
    y2, rstd2 = norm(sin_o[...] + scale[...] * down)
    y2_o[...] = y2
    places128 = lax.broadcasted_iota(jnp.int32, (ROWS, 128), 1)
    rstd_o[...] = jnp.where(places128 == 0, rstd0, jnp.where(places128 == 1, rstd1, rstd2))
    onorm = y2.astype(BF16)
    copies[3].wait()
    for c in range(CHUNKS1):
        head = mm(onorm, head_v[:, 256 * c : 256 * (c + 1)])
        mag = jnp.exp(head[:, :128])
        phase = head[:, 128:]
        re, im = mag * jnp.cos(phase), mag * jnp.sin(phase)
        re_o[:, 128 * c : 128 * (c + 1)] = re
        im_o[:, 128 * c : 128 * (c + 1)] = im
        spec_v[:, 256 * c : 256 * c + 128] = re.astype(BF16)
        spec_v[:, 256 * c + 128 : 256 * (c + 1)] = im.astype(BF16)
    copies[4].wait()
    pred = jnp.zeros((ROWS, HOP), F32)
    for p in range(4):
        piece = jnp.where(valid, mm(spec_v[...], syn_v[:, HOP * p : HOP * (p + 1)]), 0.0)
        pred = pred + shift(piece, p - 2)
    pred = jnp.where(valid, pred / envelope(places, win), 0.0)
    goal = jnp.where(valid, comb[:, :HOP], 0.0)
    for s, x in enumerate((pred, goal)):
        r1 = slice(ROWS * s, ROWS * (s + 1))
        for p in range(4):
            at = slice(HOP * p, HOP * (p + 1))
            seg1[r1, at] = (shift(x, 2 - p) * win[0:1, at]).astype(BF16)
        even = slice(2 * ROWS * s, 2 * ROWS * s + ROWS)
        odd = slice(2 * ROWS * s + ROWS, 2 * ROWS * (s + 1))
        before, after = shift(x, 1), shift(x, -1)
        seg2[even, 0:256] = (before * win[2:3, 0:256]).astype(BF16)
        seg2[even, 256:512] = (x * win[2:3, 256:512]).astype(BF16)
        seg2[odd, 0:128] = (before[:, 128:] * win[2:3, 0:128]).astype(BF16)
        seg2[odd, 128:384] = (x * win[2:3, 128:384]).astype(BF16)
        seg2[odd, 384:512] = (after[:, :128] * win[2:3, 384:512]).astype(BF16)
    own = slice(HALO, HALO + OWN)
    for level in range(2):
        seg, table, chunks = ((seg1, a1_v, CHUNKS1), (seg2, a2_v, CHUNKS2))[level]
        d_o, q_o = ((d1_o, q1_o), (d2_o, q2_o))[level]
        copies[5 + level].wait()
        sums = [jnp.zeros((OWN, 128), F32) for _ in range(3)]
        for c in range(chunks):
            for sub in range(level + 1):
                rows_p = slice(ROWS * sub, ROWS * (sub + 1))
                base = ROWS * (level + 1)
                rows_g = slice(base + ROWS * sub, base + ROWS * (sub + 1))
                weights = table[:, 256 * c : 256 * (c + 1)]
                sp, sg = mm(seg[rows_p, :], weights), mm(seg[rows_g, :], weights)
                diff = sp - sg
                pr, pi, gr, gi = sp[:, :128], sp[:, 128:], sg[:, :128], sg[:, 128:]
                power_p, power_g = pr * pr + pi * pi, gr * gr + gi * gi
                gap = jnp.log1p(power_p) - jnp.log1p(power_g)
                slope = jnp.where(valid, 4.0 * gap / (1.0 + power_p), 0.0)
                d_o[rows_p, 256 * c : 256 * (c + 1)] = jnp.where(valid, diff, 0.0)
                q_o[rows_p, 256 * c : 256 * c + 128] = slope * pr
                q_o[rows_p, 256 * c + 128 : 256 * (c + 1)] = slope * pi
                dr, di = diff[own, :128], diff[own, 128:]
                sums[0] = sums[0] + dr * dr + di * di
                sums[1] = sums[1] + power_g[own]
                sums[2] = sums[2] + gap[own] * gap[own]
        for i in range(3):
            total = jnp.sum(jnp.sum(sums[i], axis=0, keepdims=True), axis=1, keepdims=True)
            stat_o[3 * level + i : 3 * level + i + 1, :] = jnp.broadcast_to(total, (1, 128))
    stat_o[6:8, :] = jnp.zeros((2, 128), F32)


def forward_call(comb, kern, scale, win, table, up_w, down_w, head_w, syn, a1, a2):
    outs = [
        full(ROWS, D), full(ROWS, 128), full(ROWS, D), full(ROWS, FF), full(OWN, FF, dtype=BF16),
        full(ROWS, D), full(ROWS, D), full(ROWS, CHUNKS1 * 128), full(ROWS, CHUNKS1 * 128),
        full(ROWS, WIDE1), full(ROWS, WIDE1), full(2 * ROWS, WIDE2), full(2 * ROWS, WIDE2),
        full(8, 128),
    ]
    big = (table, up_w, down_w, head_w, syn, a1, a2)
    return pl.pallas_call(
        forward_kernel,
        out_shape=outs,
        in_specs=[spec(pltpu.VMEM)] * 4 + [spec(pl.ANY)] * len(big),
        out_specs=[spec(pltpu.VMEM)] * len(outs),
        scratch_shapes=[pltpu.VMEM(a.shape, BF16) for a in big]
        + [
            pltpu.VMEM((ROWS, FF), BF16),
            pltpu.VMEM((ROWS, WIDE1), BF16),
            pltpu.VMEM((2 * ROWS, NFFT), BF16),
            pltpu.VMEM((4 * ROWS, NFFT // 2), BF16),
            pltpu.SemaphoreType.DMA((len(big),)),
        ],
        compiler_params=pltpu.CompilerParams(vmem_limit_bytes=56 * MB),
        name="forward",
    )(comb, kern, scale, win, *big)


def stat_kernel(stat, out, slots, send, recv):
    tm = lax.axis_index("tm")
    barrier = pltpu.get_barrier_semaphore()
    others = [lax.rem(tm + j, 8) for j in range(1, 8)]
    for there in others:
        pl.semaphore_signal(barrier, inc=1, device_id={"tm": there}, device_id_type=MESH)
    pl.semaphore_wait(barrier, 7)
    copies = []
    for j, there in enumerate(others):
        copies.append(
            pltpu.make_async_remote_copy(
                src_ref=stat,
                dst_ref=slots.at[tm],
                send_sem=send.at[j],
                recv_sem=recv.at[j],
                device_id={"tm": there},
                device_id_type=MESH,
            )
        )
    for copy in copies:
        copy.start()
    slots[tm] = stat[...]
    for copy in copies:
        copy.wait()
    total = slots[0]
    for j in range(1, 8):
        total = total + slots[j]
    out[...] = total


def stat_call(stat):
    return pl.pallas_call(
        stat_kernel,
        out_shape=full(8, 128),
        in_specs=[spec(pltpu.VMEM)],
        out_specs=spec(pltpu.VMEM),
        scratch_shapes=[
            pltpu.VMEM((8, 8, 128), F32),
            pltpu.SemaphoreType.DMA((7,)),
            pltpu.SemaphoreType.DMA((7,)),
        ],
        compiler_params=pltpu.CompilerParams(collective_id=1, has_side_effects=True),
        name="clip_sums",
    )(stat)


def backward_kernel(
    comb, kern, scale, win, stat, loss_scale,
    sin_i, rstd_i, y1_i, gp_i, hid_i, down_i, y2_i, re_i, im_i, d1_i, q1_i, d2_i, q2_i,
    a1_h, a2_h, syn_h, head_h, down_h, up_h, pick_n_h, pick_h_h, pick_k_h,
    nrm_o, hid_o, onm_o, dup_o, ddn_o, dhd_o, dem_o, ids_o, kg_o,
    a1_v, a2_v, syn_v, head_v, down_v, up_v, pick_n, pick_h, pick_k,
    dfr, dhead, dup, small, sems,
):
    pairs = (
        (a1_h, a1_v), (a2_h, a2_v), (syn_h, syn_v), (head_h, head_v), (down_h, down_v),
        (up_h, up_v), (pick_n_h, pick_n), (pick_h_h, pick_h), (pick_k_h, pick_k),
    )
    copies = [pltpu.make_async_copy(h, v, sems.at[i]) for i, (h, v) in enumerate(pairs)]
    for copy in copies:
        copy.start()
    own = slice(HALO, HALO + OWN)
    places = frame_places(comb)
    valid = inside(places)
    ids_o[...] = comb[own, 256:384]

    factor = loss_scale[...] * (0.5 / CLIPS)
    loss = jnp.zeros((1, 1), F32)
    cots = []
    for level in range(2):
        count = ((FRAMES * 513), (2 * FRAMES * 257))[level]
        sum_a = stat[3 * level : 3 * level + 1, 0:1]
        sum_b = stat[3 * level + 1 : 3 * level + 2, 0:1]
        sum_g = stat[3 * level + 2 : 3 * level + 3, 0:1]
        root_a, root_b = jnp.sqrt(sum_a + 1e-6), jnp.sqrt(sum_b + 1e-6)
        loss = loss + root_a / root_b + sum_g * (1.0 / count)
        cots.append((factor / (root_a * root_b), factor * (1.0 / count)))
    loss = jnp.where(comb[HALO : HALO + 1, 258:259] == 0.0, loss, 0.0)

    dx = jnp.zeros((ROWS, HOP), F32)
    copies[0].wait()
    ds1 = (cots[0][0] * d1_i[...] + cots[0][1] * q1_i[...]).astype(BF16)
    for p in range(4):
        at = slice(HOP * p, HOP * (p + 1))
        piece = mm_bt(ds1, a1_v[at, :]).astype(BF16).astype(F32) * win[0:1, at]
        dx = dx + shift(piece, p - 2)
    copies[1].wait()
    ds2 = (cots[1][0] * d2_i[...] + cots[1][1] * q2_i[...]).astype(BF16)
    dseg = mm_bt(ds2, a2_v[...]).astype(BF16).astype(F32) * win[2:3, : NFFT // 2]
    even, odd = dseg[:ROWS], dseg[ROWS:]
    dx = dx + shift(even[:, :256], -1) + even[:, 256:] + odd[:, 128:384]
    dx = dx + jnp.concatenate([shift(odd[:, 384:], 1), shift(odd[:, :128], -1)], axis=1)
    dx = jnp.where(valid, dx / envelope(places, win), 0.0)
    for p in range(4):
        piece = jnp.where(valid, shift(dx, 2 - p), 0.0)
        dfr[:, HOP * p : HOP * (p + 1)] = piece.astype(BF16)

    copies[2].wait()
    for c in range(CHUNKS1):
        dsp = mm_bt(dfr[...], syn_v[256 * c : 256 * (c + 1), :]).astype(BF16).astype(F32)
        dre, dim = dsp[:, :128], dsp[:, 128:]
        re, im = re_i[:, 128 * c : 128 * (c + 1)], im_i[:, 128 * c : 128 * (c + 1)]
        dlog, dph = dre * re + dim * im, dim * re - dre * im
        dhead[:, 256 * c : 256 * c + 128] = dlog.astype(BF16)
        dhead[:, 256 * c + 128 : 256 * (c + 1)] = dph.astype(BF16)
    dhd_o[:, :1024] = dhead[own, :1024].astype(F32)
    tail = dhead[own, 1024:1152].astype(F32) + pltpu.roll(dhead[own, 1152:1280].astype(F32), 1, 1)
    dhd_o[:, 1024:] = tail
    copies[3].wait()
    don = mm_bt(dhead[...], head_v[...]).astype(BF16).astype(F32)
    dstream = norm_back(don, y2_i[...], rstd_i[:, 2:3])

    scale_grad = jnp.sum(dstream[own] * down_i[own, :], axis=0, keepdims=True)
    ddn = (scale[...] * dstream).astype(BF16)
    ddn_o[...] = ddn[own].astype(F32)
    copies[4].wait()
    for c in range(FF // 256):
        at = slice(256 * c, 256 * (c + 1))
        dh = mm_bt(ddn, down_v[at, :]).astype(BF16).astype(F32)
        dup[:, at] = (dh * gp_i[:, at]).astype(BF16)
    dup_o[...] = dup[own, :].astype(F32)
    copies[5].wait()
    dnorm = mm_bt(dup[...], up_v[...]).astype(BF16).astype(F32)
    dmix = norm_back(dnorm, y1_i[...], rstd_i[:, 1:2])
    dmix = jnp.where(valid, dmix, 0.0)
    y0 = sin_i[...]
    dsin = dstream
    small[...] = jnp.zeros((128, D), F32)
    for k in range(7):
        dsin = dsin + kern[k : k + 1, :] * shift(dmix, k - 3)
        taps = dmix * shift(y0, 3 - k)
        small[2 + k : 3 + k, :] = jnp.sum(taps[own], axis=0, keepdims=True)
    demb = norm_back(dsin, y0, rstd_i[:, 0:1])
    dem_o[...] = demb[own].astype(BF16).astype(F32)

    small[9:10, :] = scale_grad
    rest = loss
    for i, grid in enumerate((65536.0, 1.0, 1.0 / 65536.0, 1.0 / 65536.0 / 65536.0)):
        piece = jnp.floor(rest * (1.0 / grid)) * grid
        rest = rest - piece
        small[10 + i : 11 + i, :] = jnp.broadcast_to(piece, (1, D))

    for i in (6, 7, 8):
        copies[i].wait()
    normed = y1_i[own, :].astype(BF16)
    onorm = y2_i[own, :].astype(BF16)
    small0 = small[...].astype(BF16)
    left = small[...] - small0.astype(F32)
    small1 = left.astype(BF16)
    small2 = (left - small1.astype(F32)).astype(BF16)
    for c in range(2):
        nrm_o[c] = mm(normed, pick_n[c])
        onm_o[c] = mm(onorm, pick_n[c])
        for h in range(2):
            out = slice(576 * h, 576 * (h + 1))
            hid_o[c, :, out] = mm(hid_i[:, 1152 * h : 1152 * (h + 1)], pick_h[c])
        kg_o[c] = sum(
            lax.dot_general(pick_k[c], s, (((0,), (1,)), ((), ())), preferred_element_type=F32)
            for s in (small0, small1, small2)
        )


def backward_call(comb, kern, scale, win, stat, loss_scale, saved, big):
    outs = [
        full(2, OWN, 384), full(2, OWN, 1152), full(2, OWN, 384), full(OWN, FF), full(OWN, D),
        full(OWN, 1152), full(OWN, D), full(OWN, 128), full(2, 384, 128),
    ]
    return pl.pallas_call(
        backward_kernel,
        out_shape=outs,
        in_specs=[spec(pltpu.VMEM)] * (6 + len(saved)) + [spec(pl.ANY)] * len(big),
        out_specs=[spec(pltpu.VMEM)] * len(outs),
        scratch_shapes=[pltpu.VMEM(a.shape, BF16) for a in big]
        + [
            pltpu.VMEM((ROWS, NFFT), BF16),
            pltpu.VMEM((ROWS, WIDE1), BF16),
            pltpu.VMEM((ROWS, FF), BF16),
            pltpu.VMEM((128, D), F32),
            pltpu.SemaphoreType.DMA((len(big),)),
        ],
        compiler_params=pltpu.CompilerParams(vmem_limit_bytes=56 * MB),
        name="backward",
    )(comb, kern, scale, win, stat, loss_scale, *saved, *big)


PICKED = (True, True, True, False, False, False, False, False, True)


def pair_kernel(*refs):
    count = len(PICKED)
    ins, outs = refs[:count], refs[count : 2 * count]
    send, recv, local = refs[2 * count :]
    dp = lax.axis_index("dp")
    core = lax.rem(dp, 2)
    partner = dp + 1 - 2 * core
    barrier = pltpu.get_barrier_semaphore()
    pl.semaphore_signal(barrier, inc=1, device_id={"dp": partner}, device_id_type=MESH)
    pl.semaphore_wait(barrier, 1)
    copies = []
    for i, picked in enumerate(PICKED):
        rows = outs[i].shape[0] // 2
        copy = pltpu.make_async_remote_copy(
            src_ref=ins[i].at[1 - core] if picked else ins[i],
            dst_ref=outs[i].at[pl.ds(rows, rows)],
            send_sem=send.at[i],
            recv_sem=recv.at[i],
            device_id={"dp": partner},
            device_id_type=MESH,
        )
        copy.start()
        copies.append(copy)
    for i, picked in enumerate(PICKED):
        rows = outs[i].shape[0] // 2
        copy = pltpu.make_async_copy(
            ins[i].at[core] if picked else ins[i], outs[i].at[pl.ds(0, rows)], local.at[i]
        )
        copy.start()
        copies.append(copy)
    for copy in copies:
        copy.wait()


def pair_call(arrays):
    count = len(arrays)
    outs = [full(2 * a.shape[-2], a.shape[-1]) for a in arrays]
    return pl.pallas_call(
        pair_kernel,
        out_shape=outs,
        in_specs=[spec(pl.ANY)] * count,
        out_specs=[spec(pl.ANY)] * count,
        scratch_shapes=[pltpu.SemaphoreType.DMA((count,))] * 3,
        compiler_params=pltpu.CompilerParams(collective_id=2, has_side_effects=True),
        name="core_pair",
    )(*arrays)


def put(out, first, values, rows):
    for block in range(values.shape[1] // 128):
        part = values[:, 128 * block : 128 * (block + 1)].reshape(4, 4, rows, 128)
        out[:, :, first + rows * block : first + rows * (block + 1), :] = part


def weight_kernel(nrm, hid, onm, dup, ddn, dhd, dem, ids, kg, turn1, turn2, row_id, p0, p1, p2):
    onorm = [onm[...].astype(BF16)]
    for turn in (turn1, turn2):
        onorm.append(mm(onorm[0], turn[...]).astype(BF16))
    normed = nrm[...].astype(BF16)
    for c in range(FF // 256):
        put(p0, 48 * c, mm_at(normed, dup[:, 256 * c : 256 * (c + 1)].astype(BF16)), 24)
    hidden = hid[...].astype(BF16)
    for c in range(3):
        put(p1, 144 * c, mm_at(hidden, ddn[:, 256 * c : 256 * (c + 1)].astype(BF16)), 72)
    core = ids[0:1, 3:4]
    rows = row_id[...] + 128.0 * core
    hot = (rows == ids[:, 0:1]) | (rows == ids[:, 1:2] + 1024.0)
    hot = jnp.where(hot, 1.0, 0.0).astype(BF16)
    for c in range(3):
        put(p2, 128 * c, mm_at(hot, dem[:, 256 * c : 256 * (c + 1)].astype(BF16)), 64)
    for k, (out, first) in enumerate(((p0, 432), (p1, 432), (p2, 384))):
        start, blocks = HEAD_BLOCKS[k]
        for b in range(blocks):
            at = slice(128 * (start + b), 128 * (start + b + 1))
            values = mm_at(onorm[k], dhd[:, at].astype(BF16))
            if start + b == 8:
                values = values + kg[:384, :] + kg[384:, :]
            put(out, first + 24 * b, values, 24)


def weight_call(arrays, turn1, turn2, row_id):
    outs = [full(4, 4, n, 128) for n in PART_ROWS]
    return pl.pallas_call(
        weight_kernel,
        out_shape=outs,
        in_specs=[spec(pltpu.VMEM)] * (len(arrays) + 3),
        out_specs=[spec(pltpu.VMEM)] * 3,
        compiler_params=pltpu.CompilerParams(vmem_limit_bytes=56 * MB),
        name="weight_grads",
    )(*arrays, turn1, turn2, row_id)


LAST_ROWS = (120, 128, 120)


def scatter_kernel(*refs):
    parts, (up_o, down_o, table_o, head_o) = refs[0:3], refs[3:7]
    scratch = refs[7:]
    mine, to_right, to_left = scratch[0:3], scratch[3:6], scratch[6:9]
    got1, got2a, got2b = scratch[9:12], scratch[12:15], scratch[15:18]
    last, got3 = scratch[18:21], scratch[21:24]
    send, recv, local = scratch[24:]

    dp, tm = lax.axis_index("dp"), lax.axis_index("tm")
    at = {"x": tm // 2, "y": dp // 4, "z": lax.rem(dp // 2, 2) * 2 + lax.rem(tm, 2)}
    core = lax.rem(dp, 2)

    def device(axis, by):
        to = dict(at)
        to[axis] = lax.rem(at[axis] + by, 4)
        return {
            "dp": (to["y"] * 2 + to["z"] // 2) * 2 + core,
            "tm": to["x"] * 2 + lax.rem(to["z"], 2),
        }

    barrier = pltpu.get_barrier_semaphore()
    for axis in "xyz":
        for by in (1, 2, 3):
            pl.semaphore_signal(barrier, inc=1, device_id=device(axis, by), device_id_type=MESH)
    pl.semaphore_wait(barrier, 9)

    def remote(src, dst, k, slot, axis, by):
        return pltpu.make_async_remote_copy(
            src_ref=src,
            dst_ref=dst,
            send_sem=send.at[k, slot],
            recv_sem=recv.at[k, slot],
            device_id=device(axis, by),
            device_id_type=MESH,
        )

    first, second = pl.ds(0, 2), pl.ds(2, 2)
    sent = []
    loads = []
    for k in range(3):
        axis, p, g = ORDERS[k][0], parts[k], got1[k]
        i = at[axis]
        right, opposite, left = lax.rem(i + 1, 4), lax.rem(i + 2, 4), lax.rem(i + 3, 4)
        copies = [
            remote(p.at[opposite, first], g.at[0], k, 0, axis, 1),
            remote(p.at[opposite, second], g.at[1], k, 1, axis, 3),
            remote(p.at[right, second], g.at[3], k, 3, axis, 1),
            remote(p.at[left, first], g.at[4], k, 4, axis, 3),
        ]
        here = [
            pltpu.make_async_copy(p.at[right, first], to_right[k], local.at[k, 0]),
            pltpu.make_async_copy(p.at[left, second], to_left[k], local.at[k, 1]),
            pltpu.make_async_copy(p.at[i], mine[k], local.at[k, 2]),
        ]
        for copy in copies + here:
            copy.start()
        sent.append(copies)
        loads.append(here)
    for k in range(3):
        axis, g = ORDERS[k][0], got1[k]
        loads[k][0].wait()
        sent[k][0].wait_recv()
        to_right[k][...] += g[0]
        sent[k].append(remote(to_right[k], g.at[2], k, 2, axis, 1))
        sent[k][-1].start()
        loads[k][1].wait()
        sent[k][1].wait_recv()
        to_left[k][...] += g[1]
        sent[k].append(remote(to_left[k], g.at[5], k, 5, axis, 3))
        sent[k][-1].start()
    for k in range(3):
        g, m = got1[k], mine[k]
        loads[k][2].wait()
        sent[k][2].wait_recv()
        sent[k][3].wait_recv()
        sent[k][4].wait_recv()
        sent[k][5].wait_recv()
        m[0:2] += g[2] + g[4]
        m[2:4] += g[3] + g[5]
        axis = ORDERS[k][1]
        i = at[axis]
        right, opposite, left = lax.rem(i + 1, 4), lax.rem(i + 2, 4), lax.rem(i + 3, 4)
        n = PART_ROWS[k]
        cut = (n // 2 + 7) // 8 * 8
        upper, lower = pl.ds(0, cut), pl.ds(cut, n - cut)
        a, b = got2a[k], got2b[k]
        copies = [
            remote(m.at[opposite, upper], a.at[0], k, 6, axis, 1),
            remote(m.at[opposite, lower], b.at[0], k, 7, axis, 3),
            remote(m.at[right, lower], b.at[1], k, 8, axis, 1),
            remote(m.at[left, upper], a.at[1], k, 9, axis, 3),
        ]
        for copy in copies:
            copy.start()
        sent[k] = sent[k] + copies
    for k in range(3):
        axis = ORDERS[k][1]
        i = at[axis]
        right, left = lax.rem(i + 1, 4), lax.rem(i + 3, 4)
        n = PART_ROWS[k]
        cut = (n // 2 + 7) // 8 * 8
        upper, lower = pl.ds(0, cut), pl.ds(cut, n - cut)
        m, a, b = mine[k], got2a[k], got2b[k]
        sent[k][6].wait_recv()
        m[right, upper] += a[0]
        sent[k].append(remote(m.at[right, upper], a.at[2], k, 10, axis, 1))
        sent[k][-1].start()
        sent[k][7].wait_recv()
        m[left, lower] += b[0]
        sent[k].append(remote(m.at[left, lower], b.at[2], k, 11, axis, 3))
        sent[k][-1].start()
    for k in range(3):
        axis = ORDERS[k][1]
        i = at[axis]
        n = PART_ROWS[k]
        cut = (n // 2 + 7) // 8 * 8
        upper, lower = pl.ds(0, cut), pl.ds(cut, n - cut)
        m, a, b, out = mine[k], got2a[k], got2b[k], last[k]
        for j in (8, 9, 10, 11):
            sent[k][j].wait_recv()
        m[i, upper] += a[1] + a[2]
        m[i, lower] += b[1] + b[2]
        blocks = (((18, 24), (2, 24)), ((6, 72), (3, 24)), ((6, 64), (4, 24)))[k]
        start, place = 0, 0
        for count, rows in blocks:
            each = rows // 4
            for _ in range(count):
                for d in range(4):
                    out[d, pl.ds(place, each)] = m[i, pl.ds(start + d * each, each)]
                start += rows
                place += each
        if place < LAST_ROWS[k]:
            for d in range(4):
                out[d, pl.ds(place, LAST_ROWS[k] - place)] = jnp.zeros(
                    (LAST_ROWS[k] - place, 128), F32
                )
        axis = ORDERS[k][2]
        i = at[axis]
        for by in (1, 2, 3):
            copy = remote(
                out.at[lax.rem(i + by, 4)], got3[k].at[by - 1], k, 11 + by, axis, by
            )
            copy.start()
            sent[k].append(copy)
    for k in range(3):
        for j in (12, 13, 14):
            sent[k][j].wait_recv()
        total = last[k][at[ORDERS[k][2]]] + got3[k][0] + got3[k][1] + got3[k][2]
        out, count, each = ((up_o, 18, 6), (down_o, 6, 18), (table_o, 6, 16))[k]
        for c in range(count):
            out[:, 128 * c : 128 * (c + 1)] = total[each * c : each * (c + 1)]
        start, blocks = HEAD_BLOCKS[k]
        for c in range(blocks):
            rows = count * each + 6 * c
            head_o[:, 128 * (start + c) : 128 * (start + c + 1)] = total[rows : rows + 6]
    for k in range(3):
        for copy in sent[k]:
            copy.wait_send()


def scatter_call(parts):
    def each(make):
        return [make(k) for k in range(3)]

    rows = PART_ROWS
    cuts = [(n // 2 + 7) // 8 * 8 for n in rows]
    return pl.pallas_call(
        scatter_kernel,
        out_shape=[full(6, FF), full(18, D), full(16, D), full(6, 1152)],
        in_specs=[spec(pl.ANY)] * 3,
        out_specs=[spec(pltpu.VMEM)] * 4,
        scratch_shapes=each(lambda k: pltpu.VMEM((4, rows[k], 128), F32))
        + each(lambda k: pltpu.VMEM((2, rows[k], 128), F32))
        + each(lambda k: pltpu.VMEM((2, rows[k], 128), F32))
        + each(lambda k: pltpu.VMEM((6, 2, rows[k], 128), F32))
        + each(lambda k: pltpu.VMEM((3, cuts[k], 128), F32))
        + each(lambda k: pltpu.VMEM((3, rows[k] - cuts[k], 128), F32))
        + each(lambda k: pltpu.VMEM((4, LAST_ROWS[k], 128), F32))
        + each(lambda k: pltpu.VMEM((3, LAST_ROWS[k], 128), F32))
        + [
            pltpu.SemaphoreType.DMA((3, 15)),
            pltpu.SemaphoreType.DMA((3, 15)),
            pltpu.SemaphoreType.DMA((3, 3)),
        ],
        compiler_params=pltpu.CompilerParams(
            collective_id=3, has_side_effects=True, vmem_limit_bytes=48 * MB
        ),
        name="reduce_scatter",
    )(*parts)


def lay_out_head(head_weight):
    def halves(part):
        padded = jnp.pad(part, ((0, 0), (0, CHUNKS1 * 128 - part.shape[1])))
        return padded.reshape(D, CHUNKS1, 128)

    both = jnp.stack([halves(head_weight[:, :513]), halves(head_weight[:, 513:])], axis=2)
    return both.reshape(D, WIDE1)


def assemble(up, down, table, head):
    mags = [head[:, 256 * c : 256 * c + 128] for c in range(4)] + [head[:, 1024:1025]]
    phases = [head[:, 256 * c + 128 : 256 * (c + 1)] for c in range(4)] + [head[:, 1025:1026]]
    head_grad = jnp.concatenate(mags + phases, axis=1)
    loss = (head[0, 1034] + head[0, 1035] + (head[0, 1036] + head[0, 1037])) * (0.5 / CLIPS)
    return loss, table, head[:, 1026:1033].T, up, down, head[:, 1033], head_grad


def body(
    code_ids, code_table, kernel, up_weight, down_weight, layer_scale, head_weight, target, loss_scale
):
    syn, a1, a2, win = make_constants()
    pick_n, pick_h, pick_k, turn1, turn2, row_id = make_orders()
    place = jnp.stack(
        [
            (lax.axis_index("tm") * OWN).astype(F32),
            lax.rem(lax.axis_index("dp"), 2).astype(F32),
        ]
    )
    comb = jnp.concatenate(
        [
            target.reshape(OWN, HOP),
            code_ids.reshape(OWN, 2).astype(F32),
            jnp.broadcast_to(place[None, :], (OWN, 2)),
            jnp.zeros((OWN, 124), F32),
        ],
        axis=1,
    )
    comb = halo_call(comb)
    kern = jnp.pad(kernel, ((0, 1), (0, 0)))
    scale = layer_scale.reshape(1, D)
    head_w = lay_out_head(head_weight)
    saved = forward_call(
        comb, kern, scale, win, code_table, up_weight, down_weight, head_w, syn, a1, a2
    )
    stat = stat_call(saved[-1])
    operands = backward_call(
        comb, kern, scale, win, stat, loss_scale.reshape(1, 1), saved[:-1],
        (a1, a2, syn, head_w, down_weight, up_weight, pick_n, pick_h, pick_k),
    )
    parts = weight_call(pair_call(operands), turn1, turn2, row_id)
    return assemble(*scatter_call(parts))


def solution(mesh):
    in_specs = (P("dp", "tm", None), P(), P(), P(), P(), P(), P(), P("dp", "tm"), P())
    out_specs = (
        P(),
        P(("dp", "tm"), None),
        P(None, ("dp", "tm")),
        P(("dp", "tm"), None),
        P(("dp", "tm"), None),
        P(("dp", "tm")),
        P(("dp", "tm"), None),
    )
    return jax.shard_map(body, mesh=mesh, in_specs=in_specs, out_specs=out_specs, check_vma=False)
```

time: 1200 us -> 272 us (0.23); the launches traced: 1180 us -> 271 us
  blocking collectives: 619 us -> 0 us
  starting transfers between devices: 248 us -> 0 us
  Pallas kernels: 0 us -> 234 us
  local copies, waits for them, and re-layouts: 146 us -> 21.2 us
  other arithmetic: 86.7 us -> 10.9 us
  matrix products: 45.4 us -> 0 us
  between operations: 22.3 us -> 5.27 us
  waiting for transfers between devices: 14.5 us -> 0 us
    unnamed x2 -> x0, blocking collectives: 565 us -> none
    pallas_call x0 -> x7, Pallas kernels: none -> 234 us  [the longest x1 117 us: pair_call(): pl.pallas_call(pair_kernel, out_shape=outs, in_specs=[spec(pl.ANY)] * cou...]
    unnamed x65 -> x0, starting transfers between devices: 215 us -> none
    unnamed x190 -> x12, local copies, waits for them, and re-layouts: 119 us -> 5.99 us
    psum x2 -> x0, blocking collectives: 54 us -> none  [the longest x1 34.4 us: body(): lax.psum(jnp.sum(per_clip_loss(clip_stats, frame_total)), 'dp')]
    dot_general x19 -> x0, matrix products: 45.4 us -> none  [the longest x4 15.5 us: weight_grad(): return jnp.dot(left_side.T, right_side, preferred_element_type=jnp.float32)]
    div x12 -> x0, other arithmetic: 34.5 us -> none  [the longest x1 17 us: body(): add_ends(outputs[1], rim_ext[:, :half_frame], rim_ext[:, -half_frame:])]
    ppermute x12 -> x0, starting transfers between devices: 33 us -> none  [the longest x6 24.9 us: extended_2(): lax.ppermute(lax.slice_in_dim(block, block.shape[dim] - width, None, axis...]
  transfers between devices with their start and end apart: 78 -> 0, of which waited for: 5 -> 0; matrix products, arithmetic and copies ran while one was open for 56% -> 0% of each run, Pallas kernels for 0% -> 0%
where the time goes in v1:
time: 272 us; the launch traced here: 271 us
  Pallas kernels  234 us (86%)
  local copies, waits for them, and re-layouts  21.2 us (8%)
  other arithmetic  10.9 us (4%)
  between operations  5.27 us (2%)
    pallas_call x1, Pallas kernels, pair_call(): pl.pallas_call(pair_kernel, out_shape=outs, in_specs=[spec(pl.ANY)] * cou...  117 us
    pallas_call x1, Pallas kernels, scatter_call(): pl.pallas_call(scatter_kernel, out_shape=[full(6, FF), full(18, D), full(...  59.7 us
    pallas_call x1, Pallas kernels, backward_call(): pl.pallas_call(backward_kernel, out_shape=outs, in_specs=[spec(pltpu.VMEM...  17.5 us
    pallas_call x1, Pallas kernels, forward_call(): pl.pallas_call(forward_kernel, out_shape=outs, in_specs=[spec(pltpu.VMEM)...  13.9 us
    pallas_call x1, Pallas kernels, weight_call(): pl.pallas_call(weight_kernel, out_shape=outs, in_specs=[spec(pltpu.VMEM)]...  9.54 us
    pallas_call x1, Pallas kernels, stat_call(): pl.pallas_call(stat_kernel, out_shape=full(8, 128), in_specs=[spec(pltpu....  8.64 us
    pallas_call x1, Pallas kernels, halo_call(): pl.pallas_call(halo_kernel, out_shape=full(ROWS, 384), in_specs=[spec(plt...  7.77 us
    another operation x1, other arithmetic, lay_out_head(): jnp.stack([halves(head_weight[:, :513]), halves(head_weight[:, 513:])], a...  6.9 us

profile of v1, /device:TPU:0, one launch (start us, length us, event | category | flops | bytes accessed | tf_op | source)
XLA Modules:
  0.0 271.1 jit_solution(2853543471302063450)
XLA Ops:
  0.6 0.0 copy-start.1
  1.4 0.1 pad_maximum_fusion.1
  1.5 0.1 pad.19.clone
  1.6 1.3 reshape.35.scale
  2.8 1.3 pad.11.kern
  4.2 0.8 copy.30
  5.0 0.5 broadcast.24
  5.5 1.9 reduce.5
  7.4 0.7 maximum_maximum_fusion.comb
  8.1 7.8 %halo.1.comb = f32[160,384]{1,0:T(8,128)} custom-call(f32[128,384]{1,0:T(8,128)} %maximum_maximum_fusion.comb), custom_call_target="tpu_custom_call" | custom-call | tf_op jit(solution)/shard_map/halo/pallas_call | solution.py:186
  15.9 0.0 copy-done.1
  15.9 0.2 slice.56
  16.1 0.0 copy-start.2
  16.1 0.1 pad.13
  16.2 1.4 copy.32
  17.6 0.0 copy-done.2
  17.6 1.4 slice_select_fusion
  19.0 3.2 %copy.31 = bf16[768,5,1,128]{3,2,1,0:T(2,128)(2,1)} copy(bf16[768,5,1,128]{0,3,1,2:T(8,128)(2,1)S(1)} %bitcast.11) | data formatting | bytes 1966080 | tf_op jit(solution)/shard_map/stack;reshape | solution.py:806
  22.1 6.9 %pad_maximum_fusion = bf16[768,5,2,128]{3,2,1,0:T(2,128)(2,1)} fusion(bf16[768,5,1,128]{3,2,1,0:T(2,128)(2,1)S(1)} %copy.32, bf16[768,5,1,128]{3,2,1,0:T(2,128)(2,1)} %copy.31), kind=kLoop, calls=%fused_computation | loop fusion | flops 3932160 | bytes 3932160 | tf_op jit(solution)/shard_map/stack | solution.py:806
  29.0 5.6 %reshape.36.head_h = bf16[768,1280]{1,0:T(8,128)(2,1)} reshape(bf16[768,5,2,128]{3,2,1,0:T(2,128)(2,1)} %pad_maximum_fusion) | data formatting | bytes 3932160 | tf_op jit(solution)/shard_map/reshape | solution.py:807
  34.6 13.9 %forward.1 = (f32[160,768]{1,0:T(8,128)}, f32[160,128]{1,0:T(8,128)}, f32[160,768]{1,0:T(8,128)}, f32[160,2304]{1,0:T(8,128)}, bf16[128,2304]{1,0:T(8,128)(2,1)}...) custom-call(f32[160,384]{1,0:T(8,128)} %halo.1.comb, ...), custom_call_target="tpu_custom_call" | custom-call | tf_op jit(solution)/shard_map/forward/pallas_call | solution.py:309
  48.5 8.6 %clip_sums.1.stat = f32[8,128]{1,0:T(8,128)} custom-call(f32[8,128]{1,0:T(8,128)} %get-tuple-element.46.stat), custom_call_target="tpu_custom_call" | custom-call | tf_op jit(solution)/shard_map/clip_sums/pallas_call | solution.py:358
  57.2 17.5 %backward.1 = (f32[2,128,384]{2,1,0:T(8,128)}, f32[2,128,1152]{2,1,0:T(8,128)}, f32[2,128,384]{2,1,0:T(8,128)}, f32[128,2304]{1,0:T(8,128)}, f32[128,768]{1,0:T(...) custom-call(f32[160,384]{1,0:T(8,128)} %halo.1.comb, ...), custom_call_target="tpu_custom_call" | custom-call | tf_op jit(solution)/shard_map/backward/pallas_call | solution.py:494
  74.7 116.7 %core_pair.1 = (f32[256,384]{1,0:T(8,128)}, f32[256,1152]{1,0:T(8,128)}, f32[256,384]{1,0:T(8,128)}, f32[256,2304]{1,0:T(8,128)}, f32[256,768]{1,0:T(8,128)}, /*...) custom-call(f32[2,128,384]{2,1,0:T(8,128)} %get-tuple-element.60.refs_0_, ...), custom_call_target="tpu_custom_call" | custom-call | tf_op jit(solution)/shard_map/core_pair/pallas_call | solution.py:552
  191.4 9.5 %weight_grads.1 = (f32[4,4,480,128]{3,2,1,0:T(8,128)}, f32[4,4,504,128]{3,2,1,0:T(8,128)}, f32[4,4,480,128]{3,2,1,0:T(8,128)}) custom-call(f32[256,384]{1,0:T(8,128)} %get-tuple-element.69.nrm, f32[256,1152]{1,0:T(8,128)} %get-tuple-element.70.hid, f32[256,384]{1,0:T(8,128)} %get-tuple-element.71.onm, f32[256,2304]{1,0:T(8,128)} %get-tuple-element.72.dup, ...), custom_call_target="tpu_custom_call" | custom-call | tf_op jit(solution)/shard_map/weight_grads/pallas_call | solution.py:597
  200.9 0.0 copy-start
  200.9 2.1 copy-done
  203.0 59.7 %reduce_scatter.1 = (f32[6,2304]{1,0:T(8,128)S(1)}, f32[18,768]{1,0:T(8,128)S(1)}, f32[16,768]{1,0:T(8,128)S(1)}, f32[6,1152]{1,0:T(8,128)S(1)}) custom-call(f32[4,4,480,128]{3,2,1,0:T(8,128)S(1)} %copy-done, f32[4,4,504,128]{3,2,1,0:T(8,128)} %get-tuple-element.79.refs_1_, f32[4,4,480,128]{3,2,1,0:T(8,128)} %get-tuple-element.80.refs_2_), custom_call_target="tpu_custom_call" | custom-call | tf_op jit(solution)/shard_map/reduce_scatter/pallas_call | solution.py:776
  262.8 0.6 fusion.2
  265.9 0.1 slice_bitcast_fusion
  266.0 0.7 copy.33
  266.7 0.7 fusion
  267.4 0.7 concatenate.7
  268.1 0.6 copy.38
  268.7 0.6 copy.39
  269.3 0.6 copy.40
  (4 shorter events, 0.1 us)
Async XLA Ops:
  0.6 15.3 %copy-start.1 = (bf16[768,1026]{0,1:T(8,128)(2,1)S(1)}, bf16[768,1026]{0,1:T(8,128)(2,1)}, u32[]{:S(2)}) copy-start(bf16[768,1026]{0,1:T(8,128)(2,1)} %param.25) | copy-start | bytes 4727812
  16.1 1.5 copy-start.2
  200.9 2.1 copy-start

commit v2 on v1

--- a/solution.py
+++ b/solution.py
@@ -154,8 +154,13 @@
     return jax.ShapeDtypeStruct(shape, dtype)
 
 
-def halo_kernel(comb, out, send, recv):
+def halo_kernel(target, ids, out, comb, send, recv):
     tm = lax.axis_index("tm")
+    lane = lax.broadcasted_iota(jnp.int32, (OWN, 128), 1)
+    marks = jnp.where(lane == 2, tm * OWN, lax.rem(lax.axis_index("dp"), 2))
+    marks = jnp.where(lane == 0, ids[:, 0:1], jnp.where(lane == 1, ids[:, 1:2], marks))
+    comb[:, :HOP] = target[...]
+    comb[:, HOP:] = marks.astype(F32)
     right, left = lax.rem(tm + 1, 8), lax.rem(tm + 7, 8)
     barrier = pltpu.get_barrier_semaphore()
     for there in (left, right):
@@ -182,22 +187,26 @@
         copy.wait()
 
 
-def halo_call(comb):
+def halo_call(target, ids):
     return pl.pallas_call(
         halo_kernel,
         out_shape=full(ROWS, 384),
-        in_specs=[spec(pltpu.VMEM)],
+        in_specs=[spec(pltpu.VMEM)] * 2,
         out_specs=spec(pltpu.VMEM),
-        scratch_shapes=[pltpu.SemaphoreType.DMA((2,)), pltpu.SemaphoreType.DMA((2,))],
+        scratch_shapes=[
+            pltpu.VMEM((OWN, 384), F32),
+            pltpu.SemaphoreType.DMA((2,)),
+            pltpu.SemaphoreType.DMA((2,)),
+        ],
         compiler_params=pltpu.CompilerParams(collective_id=0, has_side_effects=True),
         name="halo",
-    )(comb)
+    )(target, ids)
 
 
 def forward_kernel(
     comb, kern, scale, win, table_h, up_h, down_h, head_h, syn_h, a1_h, a2_h,
     sin_o, rstd_o, y1_o, gp_o, hid_o, down_o, y2_o, re_o, im_o, d1_o, q1_o, d2_o, q2_o, stat_o,
-    table_v, up_v, down_v, head_v, syn_v, a1_v, a2_v, hid_v, spec_v, seg1, seg2, sems,
+    table_v, up_v, down_v, head_v, syn_v, a1_v, a2_v, hid_v, head_s, spec_v, seg1, seg2, sems,
 ):
     pairs = (
         (table_h, table_v), (up_h, up_v), (down_h, down_v), (head_h, head_v),
@@ -238,10 +247,17 @@
     rstd_o[...] = jnp.where(places128 == 0, rstd0, jnp.where(places128 == 1, rstd1, rstd2))
     onorm = y2.astype(BF16)
     copies[3].wait()
+    head_s[:, 1024:] = jnp.zeros((ROWS, 128), F32)
+    for c in range(4):
+        head_s[:, 256 * c : 256 * (c + 1)] = mm(onorm, head_v[:, 256 * c : 256 * (c + 1)])
+    head_s[:, 1024:1026] = mm(onorm, head_v[:, 1024:1026])
+    phases = pltpu.roll(head_s[:, 512:], CHUNKS1 * 128 - 1, 1)
     for c in range(CHUNKS1):
-        head = mm(onorm, head_v[:, 256 * c : 256 * (c + 1)])
-        mag = jnp.exp(head[:, :128])
-        phase = head[:, 128:]
+        logmag = head_s[:, 128 * c : 128 * (c + 1)]
+        if c == 4:
+            logmag = jnp.where(places128 == 0, logmag, 0.0)
+        mag = jnp.exp(logmag)
+        phase = phases[:, 128 * c : 128 * (c + 1)]
         re, im = mag * jnp.cos(phase), mag * jnp.sin(phase)
         re_o[:, 128 * c : 128 * (c + 1)] = re
         im_o[:, 128 * c : 128 * (c + 1)] = im
@@ -314,6 +330,7 @@
         scratch_shapes=[pltpu.VMEM(a.shape, BF16) for a in big]
         + [
             pltpu.VMEM((ROWS, FF), BF16),
+            pltpu.VMEM((ROWS, 1152), F32),
             pltpu.VMEM((ROWS, WIDE1), BF16),
             pltpu.VMEM((2 * ROWS, NFFT), BF16),
             pltpu.VMEM((4 * ROWS, NFFT // 2), BF16),
@@ -376,7 +393,7 @@
     a1_h, a2_h, syn_h, head_h, down_h, up_h, pick_n_h, pick_h_h, pick_k_h,
     nrm_o, hid_o, onm_o, dup_o, ddn_o, dhd_o, dem_o, ids_o, kg_o,
     a1_v, a2_v, syn_v, head_v, down_v, up_v, pick_n, pick_h, pick_k,
-    dfr, dhead, dup, small, sems,
+    dfr, dphase, dhead, dup, small, sems,
 ):
     pairs = (
         (a1_h, a1_v), (a2_h, a2_v), (syn_h, syn_v), (head_h, head_v), (down_h, down_v),
@@ -427,13 +444,15 @@
         dre, dim = dsp[:, :128], dsp[:, 128:]
         re, im = re_i[:, 128 * c : 128 * (c + 1)], im_i[:, 128 * c : 128 * (c + 1)]
         dlog, dph = dre * re + dim * im, dim * re - dre * im
-        dhead[:, 256 * c : 256 * c + 128] = dlog.astype(BF16)
-        dhead[:, 256 * c + 128 : 256 * (c + 1)] = dph.astype(BF16)
-    dhd_o[:, :1024] = dhead[own, :1024].astype(F32)
-    tail = dhead[own, 1024:1152].astype(F32) + pltpu.roll(dhead[own, 1152:1280].astype(F32), 1, 1)
-    dhd_o[:, 1024:] = tail
+        if c < 4:
+            dhead[:, 128 * c : 128 * (c + 1)] = dlog.astype(BF16)
+        dphase[:, 128 * c : 128 * (c + 1)] = dph
+    moved = pltpu.roll(dphase[...], 1, 1)
+    dhead[:, 512:640] = (moved[:, :128] + dlog).astype(BF16)
+    dhead[:, 640:] = moved[:, 128:].astype(BF16)
+    dhd_o[...] = dhead[own, :].astype(F32)
     copies[3].wait()
-    don = mm_bt(dhead[...], head_v[...]).astype(BF16).astype(F32)
+    don = mm_bt(dhead[:, :1026], head_v[...]).astype(BF16).astype(F32)
     dstream = norm_back(don, y2_i[...], rstd_i[:, 2:3])
 
     scale_grad = jnp.sum(dstream[own] * down_i[own, :], axis=0, keepdims=True)
@@ -499,7 +518,8 @@
         scratch_shapes=[pltpu.VMEM(a.shape, BF16) for a in big]
         + [
             pltpu.VMEM((ROWS, NFFT), BF16),
-            pltpu.VMEM((ROWS, WIDE1), BF16),
+            pltpu.VMEM((ROWS, CHUNKS1 * 128), F32),
+            pltpu.VMEM((ROWS, 1152), BF16),
             pltpu.VMEM((ROWS, FF), BF16),
             pltpu.VMEM((128, D), F32),
             pltpu.SemaphoreType.DMA((len(big),)),
@@ -509,13 +529,10 @@
     )(comb, kern, scale, win, stat, loss_scale, *saved, *big)
 
 
-PICKED = (True, True, True, False, False, False, False, False, True)
-
-
 def pair_kernel(*refs):
-    count = len(PICKED)
+    count = len(refs) // 2 - 1
     ins, outs = refs[:count], refs[count : 2 * count]
-    send, recv, local = refs[2 * count :]
+    send, recv = refs[2 * count :]
     dp = lax.axis_index("dp")
     core = lax.rem(dp, 2)
     partner = dp + 1 - 2 * core
@@ -523,11 +540,10 @@
     pl.semaphore_signal(barrier, inc=1, device_id={"dp": partner}, device_id_type=MESH)
     pl.semaphore_wait(barrier, 1)
     copies = []
-    for i, picked in enumerate(PICKED):
-        rows = outs[i].shape[0] // 2
+    for i in range(count):
         copy = pltpu.make_async_remote_copy(
-            src_ref=ins[i].at[1 - core] if picked else ins[i],
-            dst_ref=outs[i].at[pl.ds(rows, rows)],
+            src_ref=ins[i].at[1 - core] if len(ins[i].shape) == 3 else ins[i],
+            dst_ref=outs[i],
             send_sem=send.at[i],
             recv_sem=recv.at[i],
             device_id={"dp": partner},
@@ -535,26 +551,18 @@
         )
         copy.start()
         copies.append(copy)
-    for i, picked in enumerate(PICKED):
-        rows = outs[i].shape[0] // 2
-        copy = pltpu.make_async_copy(
-            ins[i].at[core] if picked else ins[i], outs[i].at[pl.ds(0, rows)], local.at[i]
-        )
-        copy.start()
-        copies.append(copy)
     for copy in copies:
         copy.wait()
 
 
 def pair_call(arrays):
     count = len(arrays)
-    outs = [full(2 * a.shape[-2], a.shape[-1]) for a in arrays]
     return pl.pallas_call(
         pair_kernel,
-        out_shape=outs,
+        out_shape=[full(*a.shape[-2:]) for a in arrays],
         in_specs=[spec(pl.ANY)] * count,
         out_specs=[spec(pl.ANY)] * count,
-        scratch_shapes=[pltpu.SemaphoreType.DMA((count,))] * 3,
+        scratch_shapes=[pltpu.SemaphoreType.DMA((count,))] * 2,
         compiler_params=pltpu.CompilerParams(collective_id=2, has_side_effects=True),
         name="core_pair",
     )(*arrays)
@@ -566,42 +574,50 @@
         out[:, :, first + rows * block : first + rows * (block + 1), :] = part
 
 
-def weight_kernel(nrm, hid, onm, dup, ddn, dhd, dem, ids, kg, turn1, turn2, row_id, p0, p1, p2):
-    onorm = [onm[...].astype(BF16)]
+def weight_kernel(*refs):
+    here, there = refs[0:9], refs[9:18]
+    turn1, turn2, row_id, p0, p1, p2 = refs[18:]
+    core = lax.rem(lax.axis_index("dp"), 2)
+
+    def both(i, cols=slice(None)):
+        mine = here[i][core, :, cols] if len(here[i].shape) == 3 else here[i][:, cols]
+        return jnp.concatenate([mine, there[i][:, cols]], axis=0)
+
+    onorm = [both(2).astype(BF16)]
     for turn in (turn1, turn2):
         onorm.append(mm(onorm[0], turn[...]).astype(BF16))
-    normed = nrm[...].astype(BF16)
+    normed = both(0).astype(BF16)
     for c in range(FF // 256):
-        put(p0, 48 * c, mm_at(normed, dup[:, 256 * c : 256 * (c + 1)].astype(BF16)), 24)
-    hidden = hid[...].astype(BF16)
+        put(p0, 48 * c, mm_at(normed, both(3, slice(256 * c, 256 * (c + 1))).astype(BF16)), 24)
+    hidden = both(1).astype(BF16)
     for c in range(3):
-        put(p1, 144 * c, mm_at(hidden, ddn[:, 256 * c : 256 * (c + 1)].astype(BF16)), 72)
-    core = ids[0:1, 3:4]
-    rows = row_id[...] + 128.0 * core
+        put(p1, 144 * c, mm_at(hidden, both(4, slice(256 * c, 256 * (c + 1))).astype(BF16)), 72)
+    ids = both(7)
+    rows = row_id[...] + 128.0 * ids[0:1, 3:4]
     hot = (rows == ids[:, 0:1]) | (rows == ids[:, 1:2] + 1024.0)
     hot = jnp.where(hot, 1.0, 0.0).astype(BF16)
     for c in range(3):
-        put(p2, 128 * c, mm_at(hot, dem[:, 256 * c : 256 * (c + 1)].astype(BF16)), 64)
+        put(p2, 128 * c, mm_at(hot, both(6, slice(256 * c, 256 * (c + 1))).astype(BF16)), 64)
     for k, (out, first) in enumerate(((p0, 432), (p1, 432), (p2, 384))):
         start, blocks = HEAD_BLOCKS[k]
         for b in range(blocks):
             at = slice(128 * (start + b), 128 * (start + b + 1))
-            values = mm_at(onorm[k], dhd[:, at].astype(BF16))
+            values = mm_at(onorm[k], both(5, at).astype(BF16))
             if start + b == 8:
-                values = values + kg[:384, :] + kg[384:, :]
+                values = values + here[8][core] + there[8][...]
             put(out, first + 24 * b, values, 24)
 
 
-def weight_call(arrays, turn1, turn2, row_id):
+def weight_call(here, there, turn1, turn2, row_id):
     outs = [full(4, 4, n, 128) for n in PART_ROWS]
     return pl.pallas_call(
         weight_kernel,
         out_shape=outs,
-        in_specs=[spec(pltpu.VMEM)] * (len(arrays) + 3),
+        in_specs=[spec(pltpu.VMEM)] * 21,
         out_specs=[spec(pltpu.VMEM)] * 3,
         compiler_params=pltpu.CompilerParams(vmem_limit_bytes=56 * MB),
         name="weight_grads",
-    )(*arrays, turn1, turn2, row_id)
+    )(*here, *there, turn1, turn2, row_id)
 
 
 LAST_ROWS = (120, 128, 120)
@@ -798,21 +814,9 @@
     )(*parts)
 
 
-def lay_out_head(head_weight):
-    def halves(part):
-        padded = jnp.pad(part, ((0, 0), (0, CHUNKS1 * 128 - part.shape[1])))
-        return padded.reshape(D, CHUNKS1, 128)
-
-    both = jnp.stack([halves(head_weight[:, :513]), halves(head_weight[:, 513:])], axis=2)
-    return both.reshape(D, WIDE1)
-
-
 def assemble(up, down, table, head):
-    mags = [head[:, 256 * c : 256 * c + 128] for c in range(4)] + [head[:, 1024:1025]]
-    phases = [head[:, 256 * c + 128 : 256 * (c + 1)] for c in range(4)] + [head[:, 1025:1026]]
-    head_grad = jnp.concatenate(mags + phases, axis=1)
     loss = (head[0, 1034] + head[0, 1035] + (head[0, 1036] + head[0, 1037])) * (0.5 / CLIPS)
-    return loss, table, head[:, 1026:1033].T, up, down, head[:, 1033], head_grad
+    return loss, table, head[:, 1026:1033].T, up, down, head[:, 1033], head[:, :1026]
 
 
 def body(
@@ -820,34 +824,17 @@
 ):
     syn, a1, a2, win = make_constants()
     pick_n, pick_h, pick_k, turn1, turn2, row_id = make_orders()
-    place = jnp.stack(
-        [
-            (lax.axis_index("tm") * OWN).astype(F32),
-            lax.rem(lax.axis_index("dp"), 2).astype(F32),
-        ]
-    )
-    comb = jnp.concatenate(
-        [
-            target.reshape(OWN, HOP),
-            code_ids.reshape(OWN, 2).astype(F32),
-            jnp.broadcast_to(place[None, :], (OWN, 2)),
-            jnp.zeros((OWN, 124), F32),
-        ],
-        axis=1,
-    )
-    comb = halo_call(comb)
-    kern = jnp.pad(kernel, ((0, 1), (0, 0)))
+    comb = halo_call(target.reshape(OWN, HOP), code_ids.reshape(OWN, 2))
     scale = layer_scale.reshape(1, D)
-    head_w = lay_out_head(head_weight)
     saved = forward_call(
-        comb, kern, scale, win, code_table, up_weight, down_weight, head_w, syn, a1, a2
+        comb, kernel, scale, win, code_table, up_weight, down_weight, head_weight, syn, a1, a2
     )
     stat = stat_call(saved[-1])
     operands = backward_call(
-        comb, kern, scale, win, stat, loss_scale.reshape(1, 1), saved[:-1],
-        (a1, a2, syn, head_w, down_weight, up_weight, pick_n, pick_h, pick_k),
+        comb, kernel, scale, win, stat, loss_scale.reshape(1, 1), saved[:-1],
+        (a1, a2, syn, head_weight, down_weight, up_weight, pick_n, pick_h, pick_k),
     )
-    parts = weight_call(pair_call(operands), turn1, turn2, row_id)
+    parts = weight_call(operands, pair_call(operands), turn1, turn2, row_id)
     return assemble(*scatter_call(parts))
 
 

time: 272 us -> 147 us (0.54)
  Pallas kernels: 234 us -> 125 us
  other arithmetic: 10.9 us -> 1.86 us
  local copies, waits for them, and re-layouts: 21.2 us -> 14.3 us
    pallas_call x1, Pallas kernels: 117 us -> 7.19 us  [pair_call(): pl.pallas_call(pair_kernel, out_shape=[full(*a.shape[-2:]) for a in array...]
    another operation x2 -> x0, other arithmetic: 6.97 us -> none  [the longest x1 6.9 us: lay_out_head(): jnp.stack([halves(head_weight[:, :513]), halves(head_weight[:, 513:])], a...]
    unnamed x12 -> x10, local copies, waits for them, and re-layouts: 5.99 us -> 11 us
    reshape x2 -> x1, local copies, waits for them, and re-layouts: 5.6 us -> 0.67 us  [body(): comb = halo_call(target.reshape(OWN, HOP), code_ids.reshape(OWN, 2))]
    another operation x2 -> x0, local copies, waits for them, and re-layouts: 4.57 us -> none  [lay_out_head(): jnp.stack([halves(head_weight[:, :513]), halves(head_weight[:, 513:])], a...]
where the time goes in v2:
time: 147 us
  Pallas kernels  125 us (85%)
  local copies, waits for them, and re-layouts  14.3 us (10%)
  between operations  5.07 us (3%)
  other arithmetic  1.86 us (1%)
    pallas_call x1, Pallas kernels, scatter_call(): pl.pallas_call(scatter_kernel, out_shape=[full(6, FF), full(18, D), full(...  60.1 us
    pallas_call x1, Pallas kernels, backward_call(): pl.pallas_call(backward_kernel, out_shape=outs, in_specs=[spec(pltpu.VMEM...  17.4 us
    pallas_call x1, Pallas kernels, forward_call(): pl.pallas_call(forward_kernel, out_shape=outs, in_specs=[spec(pltpu.VMEM)...  14.2 us
    unnamed x10, local copies, waits for them, and re-layouts  11 us
    pallas_call x1, Pallas kernels, weight_call(): pl.pallas_call(weight_kernel, out_shape=outs, in_specs=[spec(pltpu.VMEM)]...  9.98 us
    pallas_call x1, Pallas kernels, stat_call(): pl.pallas_call(stat_kernel, out_shape=full(8, 128), in_specs=[spec(pltpu....  8.64 us
    pallas_call x1, Pallas kernels, halo_call(): pl.pallas_call(halo_kernel, out_shape=full(ROWS, 384), in_specs=[spec(plt...  7.84 us
    pallas_call x1, Pallas kernels, pair_call(): pl.pallas_call(pair_kernel, out_shape=[full(*a.shape[-2:]) for a in array...  7.19 us

profile of v2, /device:TPU:0, one launch (start us, length us, event | category | flops | bytes accessed | tf_op | source)
XLA Modules:
  0.0 146.6 jit_solution(11372103223127712847)
XLA Ops:
  1.3 1.3 reshape.33.scale
  2.5 1.4 copy.30
  4.0 0.5 broadcast.4
  4.5 1.9 %reduce.5 = f32[32768]{0:T(1024)S(1)} reduce(f32[1,32768]{1,0:T(1,128)} %param.26, f32[]{:T(128)} %broadcast.4), dimensions={0}, to_apply=%param.26.reduce_sub_computation.3 | reduce | bytes 262148 | tf_op args[7]
  6.3 0.7 reshape.31.target
  7.0 7.8 %halo.1.comb = f32[160,384]{1,0:T(8,128)} custom-call(f32[128,256]{1,0:T(8,128)} %reshape.31.target, s32[128,2]{1,0:T(8,128)} %bitcast.8), custom_call_target="tpu_custom_call" | custom-call | tf_op jit(solution)/shard_map/halo/pallas_call | solution.py:191
  14.9 3.8 %copy.31.head_h = bf16[768,1026]{1,0:T(8,128)(2,1)} copy(bf16[768,1026]{0,1:T(8,128)(2,1)} %param.25) | data formatting | bytes 3151872 | tf_op args[6]
  18.7 14.2 %forward.1 = (f32[160,768]{1,0:T(8,128)}, f32[160,128]{1,0:T(8,128)}, f32[160,768]{1,0:T(8,128)}, f32[160,2304]{1,0:T(8,128)}, bf16[128,2304]{1,0:T(8,128)(2,1)}...) custom-call(f32[160,384]{1,0:T(8,128)} %halo.1.comb, ...), custom_call_target="tpu_custom_call" | custom-call | tf_op jit(solution)/shard_map/forward/pallas_call | solution.py:325
  32.9 8.6 %clip_sums.1.stat = f32[8,128]{1,0:T(8,128)} custom-call(f32[8,128]{1,0:T(8,128)} %get-tuple-element.46.stat), custom_call_target="tpu_custom_call" | custom-call | tf_op jit(solution)/shard_map/clip_sums/pallas_call | solution.py:375
  41.5 17.4 %backward.1 = (f32[2,128,384]{2,1,0:T(8,128)}, f32[2,128,1152]{2,1,0:T(8,128)}, f32[2,128,384]{2,1,0:T(8,128)}, f32[128,2304]{1,0:T(8,128)}, f32[128,768]{1,0:T(...) custom-call(f32[160,384]{1,0:T(8,128)} %halo.1.comb, ...), custom_call_target="tpu_custom_call" | custom-call | tf_op jit(solution)/shard_map/backward/pallas_call | solution.py:513
  59.0 7.2 %core_pair.1 = (f32[128,384]{1,0:T(8,128)}, f32[128,1152]{1,0:T(8,128)}, f32[128,384]{1,0:T(8,128)}, f32[128,2304]{1,0:T(8,128)}, f32[128,768]{1,0:T(8,128)}, /*...) custom-call(f32[2,128,384]{2,1,0:T(8,128)} %get-tuple-element.60.refs_0_, ...), custom_call_target="tpu_custom_call" | custom-call | tf_op jit(solution)/shard_map/core_pair/pallas_call | solution.py:560
  66.2 10.0 %weight_grads.1 = (f32[4,4,480,128]{3,2,1,0:T(8,128)}, f32[4,4,504,128]{3,2,1,0:T(8,128)}, f32[4,4,480,128]{3,2,1,0:T(8,128)}) custom-call(f32[2,128,384]{2,1,0:T(8,128)} %get-tuple-element.60.refs_0_, f32[2,128,1152]{2,1,0:T(8,128)} %get-tuple-element.61.refs_1_, f32[2,128,384]{2,1,0:T(8,128)} %get-tuple-element.62.refs_2_, ...), custom_call_target="tpu_custom_call" | custom-call | tf_op jit(solution)/shard_map/weight_grads/pallas_call | solution.py:613
  76.1 0.0 copy-start
  76.1 2.1 %copy-done = f32[4,4,480,128]{3,2,1,0:T(8,128)S(1)} copy-done((f32[4,4,480,128]{3,2,1,0:T(8,128)S(1)}, f32[4,4,480,128]{3,2,1,0:T(8,128)}, u32[]{:S(2)}) %copy-start) | copy-done | bytes 3932184
  78.2 60.1 %reduce_scatter.1 = (f32[6,2304]{1,0:T(8,128)S(1)}, f32[18,768]{1,0:T(8,128)S(1)}, f32[16,768]{1,0:T(8,128)S(1)}, f32[6,1152]{1,0:T(8,128)S(1)}) custom-call(f32[4,4,480,128]{3,2,1,0:T(8,128)S(1)} %copy-done, f32[4,4,504,128]{3,2,1,0:T(8,128)} %get-tuple-element.79.refs_1_, f32[4,4,480,128]{3,2,1,0:T(8,128)} %get-tuple-element.80.refs_2_), custom_call_target="tpu_custom_call" | custom-call | tf_op jit(solution)/shard_map/reduce_scatter/pallas_call | solution.py:792
  138.3 0.7 slice_reduce_fusion
  139.0 0.6 fusion
  142.2 0.1 slice_bitcast_fusion
  142.3 0.7 copy.33
  142.9 0.6 copy.39
  143.6 0.6 copy.40
  144.2 0.6 copy.41
  144.8 0.6 copy.42
Async XLA Ops:
  76.1 2.1 %copy-start = (f32[4,4,480,128]{3,2,1,0:T(8,128)S(1)}, f32[4,4,480,128]{3,2,1,0:T(8,128)}, u32[]{:S(2)}) copy-start(f32[4,4,480,128]{3,2,1,0:T(8,128)} %get-tuple-element.78.refs_0_) | copy-start | bytes 11796484

commit v3 on v2

--- a/solution.py
+++ b/solution.py
@@ -96,7 +96,7 @@
     for k in (1, 2):
         sources = np.array([where[col] for col in columns_of(ORDERS[k], 0, 6)])
         turns.append(one_hot_columns(sources, 384))
-    row_id = columns_of(ORDERS[2], 0, 16).astype(np.float32)[None, :]
+    row_id = columns_of(ORDERS[2], 0, 16).astype(np.int32)[:, None]
     return pick_n, pick_h, pick_k, turns[0], turns[1], row_id
 
 
@@ -129,10 +129,9 @@
     return rstd * (grad - mean_g - y * mean_gy)
 
 
-def frame_places(comb):
-    first = comb[HALO : HALO + 1, 258:259]
-    rows = lax.broadcasted_iota(jnp.int32, (ROWS, 1), 0).astype(F32)
-    return first + rows - float(HALO)
+def frame_places():
+    first = lax.axis_index("tm") * OWN - HALO
+    return (lax.broadcasted_iota(jnp.int32, (ROWS, 1), 0) + first).astype(F32)
 
 
 def inside(places):
@@ -154,26 +153,27 @@
     return jax.ShapeDtypeStruct(shape, dtype)
 
 
-def halo_kernel(target, ids, out, comb, send, recv):
+def halo_kernel(target, ids, left_t, right_t, left_i, right_i, send, recv):
     tm = lax.axis_index("tm")
-    lane = lax.broadcasted_iota(jnp.int32, (OWN, 128), 1)
-    marks = jnp.where(lane == 2, tm * OWN, lax.rem(lax.axis_index("dp"), 2))
-    marks = jnp.where(lane == 0, ids[:, 0:1], jnp.where(lane == 1, ids[:, 1:2], marks))
-    comb[:, :HOP] = target[...]
-    comb[:, HOP:] = marks.astype(F32)
     right, left = lax.rem(tm + 1, 8), lax.rem(tm + 7, 8)
     barrier = pltpu.get_barrier_semaphore()
     for there in (left, right):
         pl.semaphore_signal(barrier, inc=1, device_id={"tm": there}, device_id_type=MESH)
     pl.semaphore_wait(barrier, 2)
+    edge = HALO * HOP
     copies = []
     for i, (src, dst, there) in enumerate(
-        ((OWN - HALO, 0, right), (0, OWN + HALO, left))
+        (
+            (target.at[:, pl.ds(OWN * HOP - edge, edge)], left_t, right),
+            (target.at[:, pl.ds(0, edge)], right_t, left),
+            (ids, left_i, right),
+            (ids, right_i, left),
+        )
     ):
         copies.append(
             pltpu.make_async_remote_copy(
-                src_ref=comb.at[pl.ds(src, HALO)],
-                dst_ref=out.at[pl.ds(dst, HALO)],
+                src_ref=src,
+                dst_ref=dst,
                 send_sem=send.at[i],
                 recv_sem=recv.at[i],
                 device_id={"tm": there},
@@ -182,32 +182,41 @@
         )
     for copy in copies:
         copy.start()
-    out[HALO : HALO + OWN, :] = comb[...]
     for copy in copies:
         copy.wait()
 
 
 def halo_call(target, ids):
+    edge = full(1, HALO * HOP)
+    around = full(2, OWN, dtype=jnp.int32)
     return pl.pallas_call(
         halo_kernel,
-        out_shape=full(ROWS, 384),
+        out_shape=[edge, edge, around, around],
         in_specs=[spec(pltpu.VMEM)] * 2,
-        out_specs=spec(pltpu.VMEM),
-        scratch_shapes=[
-            pltpu.VMEM((OWN, 384), F32),
-            pltpu.SemaphoreType.DMA((2,)),
-            pltpu.SemaphoreType.DMA((2,)),
-        ],
+        out_specs=[spec(pltpu.VMEM)] * 4,
+        scratch_shapes=[pltpu.SemaphoreType.DMA((4,)), pltpu.SemaphoreType.DMA((4,))],
         compiler_params=pltpu.CompilerParams(collective_id=0, has_side_effects=True),
         name="halo",
     )(target, ids)
 
 
+def ids_column(ids):
+    padded = jnp.concatenate([ids.astype(F32), jnp.zeros((126, OWN), F32)], axis=0)
+    return jnp.transpose(padded)[:, :2]
+
+
 def forward_kernel(
-    comb, kern, scale, win, table_h, up_h, down_h, head_h, syn_h, a1_h, a2_h,
-    sin_o, rstd_o, y1_o, gp_o, hid_o, down_o, y2_o, re_o, im_o, d1_o, q1_o, d2_o, q2_o, stat_o,
-    table_v, up_v, down_v, head_v, syn_v, a1_v, a2_v, hid_v, head_s, spec_v, seg1, seg2, sems,
+    target, left_t, right_t, ids, left_i, right_i, kern, scale_i, win,
+    table_h, up_h, down_h, head_h, syn_h, a1_h, a2_h, *refs,
 ):
+    outs, stat_o, refs = refs[: len(SAVED)], refs[len(SAVED)], refs[len(SAVED) + 1 :]
+    (sin_o, rstd_o, y1_o, gp_o, hid_o, down_o, y2_o, re_o, im_o, d1_o, q1_o, d2_o, q2_o) = refs[
+        : len(SAVED)
+    ]
+    kept = refs[: len(SAVED)]
+    refs = refs[len(SAVED) :]
+    (table_v, up_v, down_v, head_v, syn_v, a1_v, a2_v) = refs[:7]
+    goal, codes, hid_v, head_s, spec_v, seg1, seg2, sems, out_sems = refs[7:]
     pairs = (
         (table_h, table_v), (up_h, up_v), (down_h, down_v), (head_h, head_v),
         (syn_h, syn_v), (a1_h, a1_v), (a2_h, a2_v),
@@ -215,20 +224,32 @@
     copies = [pltpu.make_async_copy(h, v, sems.at[i]) for i, (h, v) in enumerate(pairs)]
     for copy in copies:
         copy.start()
-    places = frame_places(comb)
+    saves = [pltpu.make_async_copy(v, h, out_sems.at[i]) for i, (v, h) in enumerate(zip(kept, outs))]
+    scale = scale_i[...].reshape(1, D)
+    for source, first, count, skip in (
+        (left_t, 0, HALO, 0), (target, HALO, OWN, 0), (right_t, HALO + OWN, HALO, 0),
+    ):
+        for r in range(count):
+            goal[first + r : first + r + 1, :] = source[:, HOP * r : HOP * (r + 1)]
+    codes[0:HALO, :] = ids_column(left_i[...])[OWN - HALO :]
+    codes[HALO : HALO + OWN, :] = ids_column(ids[...])
+    codes[HALO + OWN :, :] = ids_column(right_i[...])[:HALO]
+    places = frame_places()
     valid = inside(places)
     lane = lax.broadcasted_iota(jnp.int32, (ROWS, 2 * FRAMES), 1).astype(F32)
-    hot = (lane == comb[:, 256:257]) | (lane == comb[:, 257:258] + 1024.0)
+    hot = (lane == codes[:, 0:1]) | (lane == codes[:, 1:2] + 1024.0)
     hot = jnp.where(hot, 1.0, 0.0).astype(BF16)
     copies[0].wait()
     y0, rstd0 = norm(mm(hot, table_v[...]))
     y0 = jnp.where(valid, y0, 0.0)
     sin_o[...] = y0
+    saves[0].start()
     mixture = kern[0:1, :] * shift(y0, 3)
     for k in range(1, 7):
         mixture = mixture + kern[k : k + 1, :] * shift(y0, 3 - k)
     y1, rstd1 = norm(mixture)
     y1_o[...] = y1
+    saves[2].start()
     normed = y1.astype(BF16)
     copies[1].wait()
     for c in range(FF // 256):
@@ -238,19 +259,24 @@
         hid_v[:, at] = (up * cdf).astype(BF16)
         gp_o[:, at] = cdf + up * (0.3989422804014327 * jnp.exp(-0.5 * up * up))
     hid_o[...] = hid_v[HALO : HALO + OWN, :]
+    saves[3].start()
+    saves[4].start()
     copies[2].wait()
     down = mm(hid_v[...], down_v[...])
     down_o[...] = down
-    y2, rstd2 = norm(sin_o[...] + scale[...] * down)
+    saves[5].start()
+    y2, rstd2 = norm(y0 + scale * down)
     y2_o[...] = y2
+    saves[6].start()
     places128 = lax.broadcasted_iota(jnp.int32, (ROWS, 128), 1)
     rstd_o[...] = jnp.where(places128 == 0, rstd0, jnp.where(places128 == 1, rstd1, rstd2))
+    saves[1].start()
     onorm = y2.astype(BF16)
     copies[3].wait()
     head_s[:, 1024:] = jnp.zeros((ROWS, 128), F32)
     for c in range(4):
-        head_s[:, 256 * c : 256 * (c + 1)] = mm(onorm, head_v[:, 256 * c : 256 * (c + 1)])
-    head_s[:, 1024:1026] = mm(onorm, head_v[:, 1024:1026])
+        head_s[:, 256 * c : 256 * (c + 1)] = mm_bt(onorm, head_v[256 * c : 256 * (c + 1), :])
+    head_s[:, 1024:1026] = mm_bt(onorm, head_v[1024:1026, :])
     phases = pltpu.roll(head_s[:, 512:], CHUNKS1 * 128 - 1, 1)
     for c in range(CHUNKS1):
         logmag = head_s[:, 128 * c : 128 * (c + 1)]
@@ -263,14 +289,15 @@
         im_o[:, 128 * c : 128 * (c + 1)] = im
         spec_v[:, 256 * c : 256 * c + 128] = re.astype(BF16)
         spec_v[:, 256 * c + 128 : 256 * (c + 1)] = im.astype(BF16)
+    saves[7].start()
+    saves[8].start()
     copies[4].wait()
     pred = jnp.zeros((ROWS, HOP), F32)
     for p in range(4):
         piece = jnp.where(valid, mm(spec_v[...], syn_v[:, HOP * p : HOP * (p + 1)]), 0.0)
         pred = pred + shift(piece, p - 2)
     pred = jnp.where(valid, pred / envelope(places, win), 0.0)
-    goal = jnp.where(valid, comb[:, :HOP], 0.0)
-    for s, x in enumerate((pred, goal)):
+    for s, x in enumerate((pred, jnp.where(valid, goal[...], 0.0))):
         r1 = slice(ROWS * s, ROWS * (s + 1))
         for p in range(4):
             at = slice(HOP * p, HOP * (p + 1))
@@ -308,37 +335,50 @@
                 sums[0] = sums[0] + dr * dr + di * di
                 sums[1] = sums[1] + power_g[own]
                 sums[2] = sums[2] + gap[own] * gap[own]
+        saves[9 + 2 * level].start()
+        saves[10 + 2 * level].start()
         for i in range(3):
             total = jnp.sum(jnp.sum(sums[i], axis=0, keepdims=True), axis=1, keepdims=True)
             stat_o[3 * level + i : 3 * level + i + 1, :] = jnp.broadcast_to(total, (1, 128))
     stat_o[6:8, :] = jnp.zeros((2, 128), F32)
-
-
-def forward_call(comb, kern, scale, win, table, up_w, down_w, head_w, syn, a1, a2):
-    outs = [
-        full(ROWS, D), full(ROWS, 128), full(ROWS, D), full(ROWS, FF), full(OWN, FF, dtype=BF16),
-        full(ROWS, D), full(ROWS, D), full(ROWS, CHUNKS1 * 128), full(ROWS, CHUNKS1 * 128),
-        full(ROWS, WIDE1), full(ROWS, WIDE1), full(2 * ROWS, WIDE2), full(2 * ROWS, WIDE2),
-        full(8, 128),
-    ]
-    big = (table, up_w, down_w, head_w, syn, a1, a2)
+    for save in saves:
+        save.wait()
+
+
+SAVED = (
+    full(ROWS, D), full(ROWS, 128), full(ROWS, D), full(ROWS, FF), full(OWN, FF, dtype=BF16),
+    full(ROWS, D), full(ROWS, D), full(ROWS, CHUNKS1 * 128), full(ROWS, CHUNKS1 * 128),
+    full(ROWS, WIDE1), full(ROWS, WIDE1), full(2 * ROWS, WIDE2), full(2 * ROWS, WIDE2),
+)
+
+
+def vmem(shapes):
+    return [pltpu.VMEM(a.shape, a.dtype) for a in shapes]
+
+
+def forward_call(small, big):
+    outs = list(SAVED) + [full(8, 128)]
     return pl.pallas_call(
         forward_kernel,
         out_shape=outs,
-        in_specs=[spec(pltpu.VMEM)] * 4 + [spec(pl.ANY)] * len(big),
-        out_specs=[spec(pltpu.VMEM)] * len(outs),
-        scratch_shapes=[pltpu.VMEM(a.shape, BF16) for a in big]
+        in_specs=[spec(pltpu.VMEM)] * len(small) + [spec(pl.ANY)] * len(big),
+        out_specs=[spec(pl.ANY)] * len(SAVED) + [spec(pltpu.VMEM)],
+        scratch_shapes=vmem(SAVED)
+        + vmem(big)
         + [
+            pltpu.VMEM((ROWS, HOP), F32),
+            pltpu.VMEM((ROWS, 2), F32),
             pltpu.VMEM((ROWS, FF), BF16),
             pltpu.VMEM((ROWS, 1152), F32),
             pltpu.VMEM((ROWS, WIDE1), BF16),
             pltpu.VMEM((2 * ROWS, NFFT), BF16),
             pltpu.VMEM((4 * ROWS, NFFT // 2), BF16),
             pltpu.SemaphoreType.DMA((len(big),)),
+            pltpu.SemaphoreType.DMA((len(SAVED),)),
         ],
-        compiler_params=pltpu.CompilerParams(vmem_limit_bytes=56 * MB),
+        compiler_params=pltpu.CompilerParams(vmem_limit_bytes=60 * MB),
         name="forward",
-    )(comb, kern, scale, win, *big)
+    )(*small, *big)
 
 
 def stat_kernel(stat, out, slots, send, recv):
@@ -387,25 +427,37 @@
     )(stat)
 
 
-def backward_kernel(
-    comb, kern, scale, win, stat, loss_scale,
-    sin_i, rstd_i, y1_i, gp_i, hid_i, down_i, y2_i, re_i, im_i, d1_i, q1_i, d2_i, q2_i,
-    a1_h, a2_h, syn_h, head_h, down_h, up_h, pick_n_h, pick_h_h, pick_k_h,
-    nrm_o, hid_o, onm_o, dup_o, ddn_o, dhd_o, dem_o, ids_o, kg_o,
-    a1_v, a2_v, syn_v, head_v, down_v, up_v, pick_n, pick_h, pick_k,
-    dfr, dphase, dhead, dup, small, sems,
-):
-    pairs = (
-        (a1_h, a1_v), (a2_h, a2_v), (syn_h, syn_v), (head_h, head_v), (down_h, down_v),
-        (up_h, up_v), (pick_n_h, pick_n), (pick_h_h, pick_h), (pick_k_h, pick_k),
-    )
-    copies = [pltpu.make_async_copy(h, v, sems.at[i]) for i, (h, v) in enumerate(pairs)]
-    for copy in copies:
+def backward_kernel(kern, scale_i, win, stat, loss_scale, *refs):
+    count = len(SAVED)
+    saved_h, refs = refs[:count], refs[count:]
+    big_h, refs = refs[:9], refs[9:]
+    outs, refs = refs[:8], refs[8:]
+    saved, refs = refs[:count], refs[count:]
+    (sin_i, rstd_i, y1_i, gp_i, hid_i, down_i, y2_i, re_i, im_i, d1_i, q1_i, d2_i, q2_i) = saved
+    (a1_v, a2_v, syn_v, head_v, down_v, up_v, pick_n, pick_h, pick_k), refs = refs[:9], refs[9:]
+    (nrm_o, hid_o, onm_o, dup_o, ddn_o, dhd_o, dem_o, kg_o), refs = refs[:8], refs[8:]
+    kept = (nrm_o, hid_o, onm_o, dup_o, ddn_o, dhd_o, dem_o, kg_o)
+    dfr, dphase, dhead, dup, small, sems, saved_sems, out_sems = refs
+    loads = [
+        pltpu.make_async_copy(h, v, saved_sems.at[i]) for i, (h, v) in enumerate(zip(saved_h, saved))
+    ]
+    copies = [
+        pltpu.make_async_copy(h, v, sems.at[i])
+        for i, (h, v) in enumerate(
+            zip(big_h, (a1_v, a2_v, syn_v, head_v, down_v, up_v, pick_n, pick_h, pick_k))
+        )
+    ]
+    saves = [pltpu.make_async_copy(v, h, out_sems.at[i]) for i, (v, h) in enumerate(zip(kept, outs))]
+    for copy in (
+        loads[9], loads[10], copies[0], loads[11], loads[12], copies[1], copies[2], loads[7],
+        loads[8], copies[3], loads[1], loads[6], loads[5], copies[4], loads[3], copies[5],
+        loads[2], loads[0], copies[6], loads[4], copies[7], copies[8],
+    ):
         copy.start()
+    scale = scale_i[...].reshape(1, D)
     own = slice(HALO, HALO + OWN)
-    places = frame_places(comb)
+    places = frame_places()
     valid = inside(places)
-    ids_o[...] = comb[own, 256:384]
 
     factor = loss_scale[...] * (0.5 / CLIPS)
     loss = jnp.zeros((1, 1), F32)
@@ -418,15 +470,19 @@
         root_a, root_b = jnp.sqrt(sum_a + 1e-6), jnp.sqrt(sum_b + 1e-6)
         loss = loss + root_a / root_b + sum_g * (1.0 / count)
         cots.append((factor / (root_a * root_b), factor * (1.0 / count)))
-    loss = jnp.where(comb[HALO : HALO + 1, 258:259] == 0.0, loss, 0.0)
+    loss = jnp.where(lax.axis_index("tm") == 0, loss, 0.0)
 
     dx = jnp.zeros((ROWS, HOP), F32)
+    loads[9].wait()
+    loads[10].wait()
     copies[0].wait()
     ds1 = (cots[0][0] * d1_i[...] + cots[0][1] * q1_i[...]).astype(BF16)
     for p in range(4):
         at = slice(HOP * p, HOP * (p + 1))
         piece = mm_bt(ds1, a1_v[at, :]).astype(BF16).astype(F32) * win[0:1, at]
         dx = dx + shift(piece, p - 2)
+    loads[11].wait()
+    loads[12].wait()
     copies[1].wait()
     ds2 = (cots[1][0] * d2_i[...] + cots[1][1] * q2_i[...]).astype(BF16)
     dseg = mm_bt(ds2, a2_v[...]).astype(BF16).astype(F32) * win[2:3, : NFFT // 2]
@@ -439,6 +495,8 @@
         dfr[:, HOP * p : HOP * (p + 1)] = piece.astype(BF16)
 
     copies[2].wait()
+    loads[7].wait()
+    loads[8].wait()
     for c in range(CHUNKS1):
         dsp = mm_bt(dfr[...], syn_v[256 * c : 256 * (c + 1), :]).astype(BF16).astype(F32)
         dre, dim = dsp[:, :128], dsp[:, 128:]
@@ -451,20 +509,28 @@
     dhead[:, 512:640] = (moved[:, :128] + dlog).astype(BF16)
     dhead[:, 640:] = moved[:, 128:].astype(BF16)
     dhd_o[...] = dhead[own, :].astype(F32)
+    saves[5].start()
     copies[3].wait()
-    don = mm_bt(dhead[:, :1026], head_v[...]).astype(BF16).astype(F32)
+    don = mm(dhead[:, :1026], head_v[...]).astype(BF16).astype(F32)
+    for i in (1, 6, 5):
+        loads[i].wait()
     dstream = norm_back(don, y2_i[...], rstd_i[:, 2:3])
 
     scale_grad = jnp.sum(dstream[own] * down_i[own, :], axis=0, keepdims=True)
-    ddn = (scale[...] * dstream).astype(BF16)
+    ddn = (scale * dstream).astype(BF16)
     ddn_o[...] = ddn[own].astype(F32)
+    saves[4].start()
     copies[4].wait()
+    loads[3].wait()
     for c in range(FF // 256):
         at = slice(256 * c, 256 * (c + 1))
         dh = mm_bt(ddn, down_v[at, :]).astype(BF16).astype(F32)
         dup[:, at] = (dh * gp_i[:, at]).astype(BF16)
     dup_o[...] = dup[own, :].astype(F32)
+    saves[3].start()
     copies[5].wait()
+    loads[2].wait()
+    loads[0].wait()
     dnorm = mm_bt(dup[...], up_v[...]).astype(BF16).astype(F32)
     dmix = norm_back(dnorm, y1_i[...], rstd_i[:, 1:2])
     dmix = jnp.where(valid, dmix, 0.0)
@@ -477,6 +543,7 @@
         small[2 + k : 3 + k, :] = jnp.sum(taps[own], axis=0, keepdims=True)
     demb = norm_back(dsin, y0, rstd_i[:, 0:1])
     dem_o[...] = demb[own].astype(BF16).astype(F32)
+    saves[6].start()
 
     small[9:10, :] = scale_grad
     rest = loss
@@ -485,8 +552,8 @@
         rest = rest - piece
         small[10 + i : 11 + i, :] = jnp.broadcast_to(piece, (1, D))
 
-    for i in (6, 7, 8):
-        copies[i].wait()
+    for copy in (copies[6], copies[7], copies[8], loads[4]):
+        copy.wait()
     normed = y1_i[own, :].astype(BF16)
     onorm = y2_i[own, :].astype(BF16)
     small0 = small[...].astype(BF16)
@@ -503,19 +570,25 @@
             lax.dot_general(pick_k[c], s, (((0,), (1,)), ((), ())), preferred_element_type=F32)
             for s in (small0, small1, small2)
         )
-
-
-def backward_call(comb, kern, scale, win, stat, loss_scale, saved, big):
+    for i in (0, 1, 2, 7):
+        saves[i].start()
+    for save in saves:
+        save.wait()
+
+
+def backward_call(small, saved, big):
     outs = [
         full(2, OWN, 384), full(2, OWN, 1152), full(2, OWN, 384), full(OWN, FF), full(OWN, D),
-        full(OWN, 1152), full(OWN, D), full(OWN, 128), full(2, 384, 128),
+        full(OWN, 1152), full(OWN, D), full(2, 384, 128),
     ]
     return pl.pallas_call(
         backward_kernel,
         out_shape=outs,
-        in_specs=[spec(pltpu.VMEM)] * (6 + len(saved)) + [spec(pl.ANY)] * len(big),
-        out_specs=[spec(pltpu.VMEM)] * len(outs),
-        scratch_shapes=[pltpu.VMEM(a.shape, BF16) for a in big]
+        in_specs=[spec(pltpu.VMEM)] * len(small) + [spec(pl.ANY)] * (len(saved) + len(big)),
+        out_specs=[spec(pl.ANY)] * len(outs),
+        scratch_shapes=vmem(saved)
+        + vmem(big)
+        + vmem(outs)
         + [
             pltpu.VMEM((ROWS, NFFT), BF16),
             pltpu.VMEM((ROWS, CHUNKS1 * 128), F32),
@@ -523,10 +596,12 @@
             pltpu.VMEM((ROWS, FF), BF16),
             pltpu.VMEM((128, D), F32),
             pltpu.SemaphoreType.DMA((len(big),)),
+            pltpu.SemaphoreType.DMA((len(saved),)),
+            pltpu.SemaphoreType.DMA((len(outs),)),
         ],
-        compiler_params=pltpu.CompilerParams(vmem_limit_bytes=56 * MB),
+        compiler_params=pltpu.CompilerParams(vmem_limit_bytes=60 * MB),
         name="backward",
-    )(comb, kern, scale, win, stat, loss_scale, *saved, *big)
+    )(*small, *saved, *big)
 
 
 def pair_kernel(*refs):
@@ -559,7 +634,7 @@
     count = len(arrays)
     return pl.pallas_call(
         pair_kernel,
-        out_shape=[full(*a.shape[-2:]) for a in arrays],
+        out_shape=[full(*a.shape[-2:], dtype=a.dtype) for a in arrays],
         in_specs=[spec(pl.ANY)] * count,
         out_specs=[spec(pl.ANY)] * count,
         scratch_shapes=[pltpu.SemaphoreType.DMA((count,))] * 2,
@@ -592,19 +667,19 @@
     hidden = both(1).astype(BF16)
     for c in range(3):
         put(p1, 144 * c, mm_at(hidden, both(4, slice(256 * c, 256 * (c + 1))).astype(BF16)), 72)
-    ids = both(7)
-    rows = row_id[...] + 128.0 * ids[0:1, 3:4]
-    hot = (rows == ids[:, 0:1]) | (rows == ids[:, 1:2] + 1024.0)
+    ids = jnp.concatenate([here[8][...], there[8][...]], axis=1)
+    rows = row_id[...] + OWN * core
+    hot = (rows == ids[0:1, :]) | (rows == ids[1:2, :] + 1024)
     hot = jnp.where(hot, 1.0, 0.0).astype(BF16)
     for c in range(3):
-        put(p2, 128 * c, mm_at(hot, both(6, slice(256 * c, 256 * (c + 1))).astype(BF16)), 64)
+        put(p2, 128 * c, mm(hot, both(6, slice(256 * c, 256 * (c + 1))).astype(BF16)), 64)
     for k, (out, first) in enumerate(((p0, 432), (p1, 432), (p2, 384))):
         start, blocks = HEAD_BLOCKS[k]
         for b in range(blocks):
             at = slice(128 * (start + b), 128 * (start + b + 1))
             values = mm_at(onorm[k], both(5, at).astype(BF16))
             if start + b == 8:
-                values = values + here[8][core] + there[8][...]
+                values = values + here[7][core] + there[7][...]
             put(out, first + 24 * b, values, 24)
 
 
@@ -624,8 +699,8 @@
 
 
 def scatter_kernel(*refs):
-    parts, (up_o, down_o, table_o, head_o) = refs[0:3], refs[3:7]
-    scratch = refs[7:]
+    parts, outs = refs[0:3], refs[3:6]
+    scratch = refs[6:]
     mine, to_right, to_left = scratch[0:3], scratch[3:6], scratch[6:9]
     got1, got2a, got2b = scratch[9:12], scratch[12:15], scratch[15:18]
     last, got3 = scratch[18:21], scratch[21:24]
@@ -770,14 +845,7 @@
     for k in range(3):
         for j in (12, 13, 14):
             sent[k][j].wait_recv()
-        total = last[k][at[ORDERS[k][2]]] + got3[k][0] + got3[k][1] + got3[k][2]
-        out, count, each = ((up_o, 18, 6), (down_o, 6, 18), (table_o, 6, 16))[k]
-        for c in range(count):
-            out[:, 128 * c : 128 * (c + 1)] = total[each * c : each * (c + 1)]
-        start, blocks = HEAD_BLOCKS[k]
-        for c in range(blocks):
-            rows = count * each + 6 * c
-            head_o[:, 128 * (start + c) : 128 * (start + c + 1)] = total[rows : rows + 6]
+        outs[k][...] = last[k][at[ORDERS[k][2]]] + got3[k][0] + got3[k][1] + got3[k][2]
     for k in range(3):
         for copy in sent[k]:
             copy.wait_send()
@@ -791,9 +859,9 @@
     cuts = [(n // 2 + 7) // 8 * 8 for n in rows]
     return pl.pallas_call(
         scatter_kernel,
-        out_shape=[full(6, FF), full(18, D), full(16, D), full(6, 1152)],
+        out_shape=[full(n, 128) for n in LAST_ROWS],
         in_specs=[spec(pl.ANY)] * 3,
-        out_specs=[spec(pltpu.VMEM)] * 4,
+        out_specs=[spec(pltpu.VMEM)] * 3,
         scratch_shapes=each(lambda k: pltpu.VMEM((4, rows[k], 128), F32))
         + each(lambda k: pltpu.VMEM((2, rows[k], 128), F32))
         + each(lambda k: pltpu.VMEM((2, rows[k], 128), F32))
@@ -814,9 +882,37 @@
     )(*parts)
 
 
-def assemble(up, down, table, head):
-    loss = (head[0, 1034] + head[0, 1035] + (head[0, 1036] + head[0, 1037])) * (0.5 / CLIPS)
-    return loss, table, head[:, 1026:1033].T, up, down, head[:, 1033], head[:, :1026]
+def finish_kernel(s0, s1, s2, loss_o, table_o, kern_o, up_o, down_o, scale_o, head_o):
+    sources = (s0, s1, s2)
+    for k, (out, count, each) in enumerate(((up_o, 18, 6), (down_o, 6, 18), (table_o, 6, 16))):
+        for c in range(count):
+            out[:, 128 * c : 128 * (c + 1)] = sources[k][each * c : each * (c + 1), :]
+        start, blocks = HEAD_BLOCKS[k]
+        for c in range(blocks):
+            rows = count * each + 6 * c
+            values = sources[k][rows : rows + 6, :]
+            if start + c < 8:
+                head_o[:, 128 * (start + c) : 128 * (start + c + 1)] = values
+            else:
+                head_o[:, 1024:1026] = values[:, 0:2]
+                tail = jnp.transpose(jnp.concatenate([values, jnp.zeros((122, 128), F32)], axis=0))
+                kern_o[...] = tail[2:9, 0:6]
+                scale_o[...] = tail[9:10, 0:6]
+                pieces = values[0:1, 10:14]
+                loss_o[...] = jnp.sum(pieces, axis=1, keepdims=True) * (0.5 / CLIPS)
+
+
+def finish_call(sums):
+    loss, table, kern, up, down, scale, head = pl.pallas_call(
+        finish_kernel,
+        out_shape=[
+            full(1, 1), full(16, D), full(7, 6), full(6, FF), full(18, D), full(1, 6), full(6, 1026),
+        ],
+        in_specs=[spec(pltpu.VMEM)] * 3,
+        out_specs=[spec(pltpu.VMEM)] * 7,
+        name="finish",
+    )(*sums)
+    return loss.reshape(()), table, kern, up, down, scale.reshape(6), head
 
 
 def body(
@@ -824,18 +920,21 @@
 ):
     syn, a1, a2, win = make_constants()
     pick_n, pick_h, pick_k, turn1, turn2, row_id = make_orders()
-    comb = halo_call(target.reshape(OWN, HOP), code_ids.reshape(OWN, 2))
-    scale = layer_scale.reshape(1, D)
-    saved = forward_call(
-        comb, kernel, scale, win, code_table, up_weight, down_weight, head_weight, syn, a1, a2
+    ids = jnp.swapaxes(code_ids, 1, 2).reshape(2, OWN)
+    head_t = head_weight.T
+    left_t, right_t, left_i, right_i = halo_call(target, ids)
+    *saved, stat = forward_call(
+        (target, left_t, right_t, ids, left_i, right_i, kernel, layer_scale, win),
+        (code_table, up_weight, down_weight, head_t, syn, a1, a2),
     )
-    stat = stat_call(saved[-1])
     operands = backward_call(
-        comb, kernel, scale, win, stat, loss_scale.reshape(1, 1), saved[:-1],
-        (a1, a2, syn, head_weight, down_weight, up_weight, pick_n, pick_h, pick_k),
+        (kernel, layer_scale, win, stat_call(stat), loss_scale.reshape(1, 1)),
+        saved,
+        (a1, a2, syn, head_t, down_weight, up_weight, pick_n, pick_h, pick_k),
     )
-    parts = weight_call(operands, pair_call(operands), turn1, turn2, row_id)
-    return assemble(*scatter_call(parts))
+    here = [*operands, ids]
+    parts = weight_call(here, pair_call(here), turn1, turn2, row_id)
+    return finish_call(scatter_call(parts))
 
 
 def solution(mesh):

time: 147 us -> 131 us (0.89)
  local copies, waits for them, and re-layouts: 14.3 us -> 3.97 us
  between operations: 5.07 us -> 1.34 us
  other arithmetic: 1.86 us -> 0 us
    unnamed x10 -> x8, local copies, waits for them, and re-layouts: 11 us -> 3.97 us
    reshape x2 -> x0, local copies, waits for them, and re-layouts: 1.94 us -> none  [the longest x1 1.27 us: body(): scale = layer_scale.reshape(1, D)]
    unnamed x1 -> x0, other arithmetic: 1.86 us -> none
    pallas_call x1, Pallas kernels: 17.4 us -> 15.8 us  [backward_call(): pl.pallas_call(backward_kernel, out_shape=outs, in_specs=[spec(pltpu.VMEM...]
    pallas_call x3 -> x4, Pallas kernels: 75.1 us -> 76.4 us  [the longest x1 60 us: scatter_call(): pl.pallas_call(scatter_kernel, out_shape=[full(n, 128) for n in LAST_ROWS...]
where the time goes in v3:
time: 131 us; the launch traced here: 130 us
  Pallas kernels  125 us (95%)
  local copies, waits for them, and re-layouts  3.97 us (3%)
  between operations  1.34 us (1%)
    pallas_call x1, Pallas kernels, scatter_call(): pl.pallas_call(scatter_kernel, out_shape=[full(n, 128) for n in LAST_ROWS...  60 us
    pallas_call x1, Pallas kernels, backward_call(): pl.pallas_call(backward_kernel, out_shape=outs, in_specs=[spec(pltpu.VMEM...  15.8 us
    pallas_call x1, Pallas kernels, forward_call(): pl.pallas_call(forward_kernel, out_shape=outs, in_specs=[spec(pltpu.VMEM)...  14 us
    pallas_call x1, Pallas kernels, weight_call(): pl.pallas_call(weight_kernel, out_shape=outs, in_specs=[spec(pltpu.VMEM)]...  10.1 us
    pallas_call x1, Pallas kernels, stat_call(): pl.pallas_call(stat_kernel, out_shape=full(8, 128), in_specs=[spec(pltpu....  8.65 us
    pallas_call x1, Pallas kernels, halo_call(): pl.pallas_call(halo_kernel, out_shape=[edge, edge, around, around], in_sp...  7.73 us
    pallas_call x1, Pallas kernels, pair_call(): pl.pallas_call(pair_kernel, out_shape=[full(*a.shape[-2:], dtype=a.dtype)...  7.1 us
    unnamed x8, local copies, waits for them, and re-layouts  3.97 us

profile of v3, /device:TPU:0, one launch (start us, length us, event | category | flops | bytes accessed | tf_op | source)
XLA Modules:
  0.0 130.3 jit_solution(17059042329508869996)
XLA Ops:
  1.3 7.7 %halo.1 = (f32[1,4096]{1,0:T(1,128)}, f32[1,4096]{1,0:T(1,128)}, s32[2,128]{1,0:T(2,128)}, s32[2,128]{1,0:T(2,128)}) custom-call(f32[1,32768]{1,0:T(1,128)} %target.3, s32[2,128]{1,0:T(2,128)} %bitcast.10), custom_call_target="tpu_custom_call" | custom-call | tf_op jit(solution)/shard_map/halo/pallas_call | solution.py:192
  9.0 14.0 %forward.1 = (f32[160,768]{1,0:T(8,128)}, f32[160,128]{1,0:T(8,128)}, f32[160,768]{1,0:T(8,128)}, f32[160,2304]{1,0:T(8,128)}, bf16[128,2304]{1,0:T(8,128)(2,1)}...) custom-call(f32[1,32768]{1,0:T(1,128)} %target.3, ...), custom_call_target="tpu_custom_call" | custom-call | tf_op jit(solution)/shard_map/forward/pallas_call | solution.py:361
  23.0 8.6 %clip_sums.1.stat = f32[8,128]{1,0:T(8,128)} custom-call(f32[8,128]{1,0:T(8,128)} %get-tuple-element.59.stat), custom_call_target="tpu_custom_call" | custom-call | tf_op jit(solution)/shard_map/clip_sums/pallas_call | solution.py:415
  31.7 15.8 %backward.1 = (f32[2,128,384]{2,1,0:T(8,128)}, f32[2,128,1152]{2,1,0:T(8,128)}, f32[2,128,384]{2,1,0:T(8,128)}, f32[128,2304]{1,0:T(8,128)}, f32[128,768]{1,0:T(...) custom-call(f32[7,768]{1,0:T(8,128)} %kern.3, f32[768]{0:T(1024)} %scale_i.3, ...), custom_call_target="tpu_custom_call" | custom-call | tf_op jit(solution)/shard_map/backward/pallas_call | solution.py:584
  47.5 7.1 %core_pair.1 = (f32[128,384]{1,0:T(8,128)}, f32[128,1152]{1,0:T(8,128)}, f32[128,384]{1,0:T(8,128)}, f32[128,2304]{1,0:T(8,128)}, f32[128,768]{1,0:T(8,128)}, /*...) custom-call(f32[2,128,384]{2,1,0:T(8,128)} %get-tuple-element.73.refs_0_, ...), custom_call_target="tpu_custom_call" | custom-call | tf_op jit(solution)/shard_map/core_pair/pallas_call | solution.py:635
  54.6 10.1 %weight_grads.1 = (f32[4,4,480,128]{3,2,1,0:T(8,128)}, f32[4,4,504,128]{3,2,1,0:T(8,128)}, f32[4,4,480,128]{3,2,1,0:T(8,128)}) custom-call(f32[2,128,384]{2,1,0:T(8,128)} %get-tuple-element.73.refs_0_, f32[2,128,1152]{2,1,0:T(8,128)} %get-tuple-element.74.refs_1_, f32[2,128,384]{2,1,0:T(8,128)} %get-tuple-element.75.refs_2_, ...), custom_call_target="tpu_custom_call" | custom-call | tf_op jit(solution)/shard_map/weight_grads/pallas_call | solution.py:688
  64.7 0.0 copy-start
  64.7 2.1 %copy-done = f32[4,4,480,128]{3,2,1,0:T(8,128)S(1)} copy-done((f32[4,4,480,128]{3,2,1,0:T(8,128)S(1)}, f32[4,4,480,128]{3,2,1,0:T(8,128)}, u32[]{:S(2)}) %copy-start) | copy-done | bytes 3932184
  66.8 60.0 %reduce_scatter.1 = (f32[120,128]{1,0:T(8,128)S(1)}, f32[128,128]{1,0:T(8,128)S(1)}, f32[120,128]{1,0:T(8,128)S(1)}) custom-call(f32[4,4,480,128]{3,2,1,0:T(8,128)S(1)} %copy-done, f32[4,4,504,128]{3,2,1,0:T(8,128)} %get-tuple-element.91.refs_1_, f32[4,4,480,128]{3,2,1,0:T(8,128)} %get-tuple-element.92.refs_2_), custom_call_target="tpu_custom_call" | custom-call | tf_op jit(solution)/shard_map/reduce_scatter/pallas_call | solution.py:860
  126.8 0.0 copy-start.1
  126.8 0.6 copy-done.1
  127.4 0.0 copy-start.2
  127.4 0.6 copy-done.2
  128.1 0.0 copy-start.3
  128.1 0.6 copy-done.3
  128.7 1.6 %finish.1 = (f32[1,1]{1,0:T(1,128)}, f32[16,768]{1,0:T(8,128)}, f32[7,6]{1,0:T(8,128)}, f32[6,2304]{1,0:T(8,128)}, f32[18,768]{1,0:T(8,128)}, /*index=5*/f32[1,6]{1,0:T(1,128)}, f32[6,1026]{1,0:T(8,128)}) custom-call(f32[120,128]{1,0:T(8,128)} %copy-done.2, f32[128,128]{1,0:T(8,128)} %copy-done.1, f32[120,128]{1,0:T(8,128)} %copy-done.3), custom_call_target="tpu_custom_call" | custom-call | tf_op jit(solution)/shard_map/finish/pallas_call | solution.py:906
Async XLA Ops:
  64.7 2.1 %copy-start = (f32[4,4,480,128]{3,2,1,0:T(8,128)S(1)}, f32[4,4,480,128]{3,2,1,0:T(8,128)}, u32[]{:S(2)}) copy-start(f32[4,4,480,128]{3,2,1,0:T(8,128)} %get-tuple-element.90.refs_0_) | copy-start | bytes 11796484
  126.8 0.6 copy-start.1
  127.4 0.6 copy-start.2
  128.1 0.6 copy-start.3

commit v4 on v3

--- a/solution.py
+++ b/solution.py
@@ -132,6 +132,23 @@
 def frame_places():
     first = lax.axis_index("tm") * OWN - HALO
     return (lax.broadcasted_iota(jnp.int32, (ROWS, 1), 0) + first).astype(F32)
+
+
+def sin_cos(x):
+    turns = jnp.round(x * 0.6366197723675814)
+    r = x - turns * 1.5703125
+    r = r - turns * 4.837512969970703125e-4
+    r = r - turns * 7.549789954891882e-8
+    z = r * r
+    sine = r + r * z * (-1.6666654611e-1 + z * (8.3321608736e-3 + z * -1.9515295891e-4))
+    cosine = (4.166664568298827e-2 + z * (-1.388731625493765e-3 + z * 2.443315711809948e-5)) * (z * z)
+    cosine = cosine - 0.5 * z + 1.0
+    quarter = turns.astype(jnp.int32)
+    odd = (quarter & 1) == 1
+    first, second = jnp.where(odd, cosine, sine), jnp.where(odd, sine, cosine)
+    first = jnp.where((quarter & 2) == 2, -first, first)
+    second = jnp.where(((quarter + 1) & 2) == 2, -second, second)
+    return first, second
 
 
 def inside(places):
@@ -222,8 +239,8 @@
         (syn_h, syn_v), (a1_h, a1_v), (a2_h, a2_v),
     )
     copies = [pltpu.make_async_copy(h, v, sems.at[i]) for i, (h, v) in enumerate(pairs)]
-    for copy in copies:
-        copy.start()
+    copies[0].start()
+    copies[1].start()
     saves = [pltpu.make_async_copy(v, h, out_sems.at[i]) for i, (v, h) in enumerate(zip(kept, outs))]
     scale = scale_i[...].reshape(1, D)
     for source, first, count, skip in (
@@ -240,6 +257,7 @@
     hot = (lane == codes[:, 0:1]) | (lane == codes[:, 1:2] + 1024.0)
     hot = jnp.where(hot, 1.0, 0.0).astype(BF16)
     copies[0].wait()
+    copies[2].start()
     y0, rstd0 = norm(mm(hot, table_v[...]))
     y0 = jnp.where(valid, y0, 0.0)
     sin_o[...] = y0
@@ -252,6 +270,8 @@
     saves[2].start()
     normed = y1.astype(BF16)
     copies[1].wait()
+    copies[3].start()
+    copies[4].start()
     for c in range(FF // 256):
         at = slice(256 * c, 256 * (c + 1))
         up = mm(normed, up_v[:, at])
@@ -262,6 +282,8 @@
     saves[3].start()
     saves[4].start()
     copies[2].wait()
+    copies[5].start()
+    copies[6].start()
     down = mm(hid_v[...], down_v[...])
     down_o[...] = down
     saves[5].start()
@@ -284,7 +306,8 @@
             logmag = jnp.where(places128 == 0, logmag, 0.0)
         mag = jnp.exp(logmag)
         phase = phases[:, 128 * c : 128 * (c + 1)]
-        re, im = mag * jnp.cos(phase), mag * jnp.sin(phase)
+        sine, cosine = sin_cos(phase)
+        re, im = mag * cosine, mag * sine
         re_o[:, 128 * c : 128 * (c + 1)] = re
         im_o[:, 128 * c : 128 * (c + 1)] = im
         spec_v[:, 256 * c : 256 * c + 128] = re.astype(BF16)
@@ -448,11 +471,7 @@
         )
     ]
     saves = [pltpu.make_async_copy(v, h, out_sems.at[i]) for i, (v, h) in enumerate(zip(kept, outs))]
-    for copy in (
-        loads[9], loads[10], copies[0], loads[11], loads[12], copies[1], copies[2], loads[7],
-        loads[8], copies[3], loads[1], loads[6], loads[5], copies[4], loads[3], copies[5],
-        loads[2], loads[0], copies[6], loads[4], copies[7], copies[8],
-    ):
+    for copy in (loads[9], loads[10], copies[0]):
         copy.start()
     scale = scale_i[...].reshape(1, D)
     own = slice(HALO, HALO + OWN)
@@ -476,6 +495,8 @@
     loads[9].wait()
     loads[10].wait()
     copies[0].wait()
+    for copy in (loads[11], loads[12], copies[1], copies[2], loads[7], loads[8]):
+        copy.start()
     ds1 = (cots[0][0] * d1_i[...] + cots[0][1] * q1_i[...]).astype(BF16)
     for p in range(4):
         at = slice(HOP * p, HOP * (p + 1))
@@ -484,6 +505,8 @@
     loads[11].wait()
     loads[12].wait()
     copies[1].wait()
+    for copy in (copies[3], loads[1], loads[6], loads[5]):
+        copy.start()
     ds2 = (cots[1][0] * d2_i[...] + cots[1][1] * q2_i[...]).astype(BF16)
     dseg = mm_bt(ds2, a2_v[...]).astype(BF16).astype(F32) * win[2:3, : NFFT // 2]
     even, odd = dseg[:ROWS], dseg[ROWS:]
@@ -497,6 +520,8 @@
     copies[2].wait()
     loads[7].wait()
     loads[8].wait()
+    copies[4].start()
+    loads[3].start()
     for c in range(CHUNKS1):
         dsp = mm_bt(dfr[...], syn_v[256 * c : 256 * (c + 1), :]).astype(BF16).astype(F32)
         dre, dim = dsp[:, :128], dsp[:, 128:]
@@ -511,6 +536,8 @@
     dhd_o[...] = dhead[own, :].astype(F32)
     saves[5].start()
     copies[3].wait()
+    for copy in (copies[5], loads[2], loads[0]):
+        copy.start()
     don = mm(dhead[:, :1026], head_v[...]).astype(BF16).astype(F32)
     for i in (1, 6, 5):
         loads[i].wait()
@@ -522,6 +549,8 @@
     saves[4].start()
     copies[4].wait()
     loads[3].wait()
+    for copy in (copies[6], loads[4], copies[7], copies[8]):
+        copy.start()
     for c in range(FF // 256):
         at = slice(256 * c, 256 * (c + 1))
         dh = mm_bt(ddn, down_v[at, :]).astype(BF16).astype(F32)
@@ -604,43 +633,12 @@
     )(*small, *saved, *big)
 
 
-def pair_kernel(*refs):
-    count = len(refs) // 2 - 1
-    ins, outs = refs[:count], refs[count : 2 * count]
-    send, recv = refs[2 * count :]
-    dp = lax.axis_index("dp")
-    core = lax.rem(dp, 2)
-    partner = dp + 1 - 2 * core
-    barrier = pltpu.get_barrier_semaphore()
-    pl.semaphore_signal(barrier, inc=1, device_id={"dp": partner}, device_id_type=MESH)
-    pl.semaphore_wait(barrier, 1)
-    copies = []
-    for i in range(count):
-        copy = pltpu.make_async_remote_copy(
-            src_ref=ins[i].at[1 - core] if len(ins[i].shape) == 3 else ins[i],
-            dst_ref=outs[i],
-            send_sem=send.at[i],
-            recv_sem=recv.at[i],
-            device_id={"dp": partner},
-            device_id_type=MESH,
-        )
-        copy.start()
-        copies.append(copy)
-    for copy in copies:
-        copy.wait()
-
-
-def pair_call(arrays):
-    count = len(arrays)
-    return pl.pallas_call(
-        pair_kernel,
-        out_shape=[full(*a.shape[-2:], dtype=a.dtype) for a in arrays],
-        in_specs=[spec(pl.ANY)] * count,
-        out_specs=[spec(pl.ANY)] * count,
-        scratch_shapes=[pltpu.SemaphoreType.DMA((count,))] * 2,
-        compiler_params=pltpu.CompilerParams(collective_id=2, has_side_effects=True),
-        name="core_pair",
-    )(*arrays)
+LAST_ROWS = (120, 128, 120)
+FIRST_ROWS = (0, 120, 248)
+OPERANDS = (
+    full(OWN, 384), full(OWN, 1152), full(OWN, 384), full(OWN, FF), full(OWN, D),
+    full(OWN, 1152), full(OWN, D), full(384, 128), full(2, OWN, dtype=jnp.int32),
+)
 
 
 def put(out, first, values, rows):
@@ -649,66 +647,22 @@
         out[:, :, first + rows * block : first + rows * (block + 1), :] = part
 
 
-def weight_kernel(*refs):
-    here, there = refs[0:9], refs[9:18]
-    turn1, turn2, row_id, p0, p1, p2 = refs[18:]
-    core = lax.rem(lax.axis_index("dp"), 2)
-
-    def both(i, cols=slice(None)):
-        mine = here[i][core, :, cols] if len(here[i].shape) == 3 else here[i][:, cols]
-        return jnp.concatenate([mine, there[i][:, cols]], axis=0)
-
-    onorm = [both(2).astype(BF16)]
-    for turn in (turn1, turn2):
-        onorm.append(mm(onorm[0], turn[...]).astype(BF16))
-    normed = both(0).astype(BF16)
-    for c in range(FF // 256):
-        put(p0, 48 * c, mm_at(normed, both(3, slice(256 * c, 256 * (c + 1))).astype(BF16)), 24)
-    hidden = both(1).astype(BF16)
-    for c in range(3):
-        put(p1, 144 * c, mm_at(hidden, both(4, slice(256 * c, 256 * (c + 1))).astype(BF16)), 72)
-    ids = jnp.concatenate([here[8][...], there[8][...]], axis=1)
-    rows = row_id[...] + OWN * core
-    hot = (rows == ids[0:1, :]) | (rows == ids[1:2, :] + 1024)
-    hot = jnp.where(hot, 1.0, 0.0).astype(BF16)
-    for c in range(3):
-        put(p2, 128 * c, mm(hot, both(6, slice(256 * c, 256 * (c + 1))).astype(BF16)), 64)
-    for k, (out, first) in enumerate(((p0, 432), (p1, 432), (p2, 384))):
-        start, blocks = HEAD_BLOCKS[k]
-        for b in range(blocks):
-            at = slice(128 * (start + b), 128 * (start + b + 1))
-            values = mm_at(onorm[k], both(5, at).astype(BF16))
-            if start + b == 8:
-                values = values + here[7][core] + there[7][...]
-            put(out, first + 24 * b, values, 24)
-
-
-def weight_call(here, there, turn1, turn2, row_id):
-    outs = [full(4, 4, n, 128) for n in PART_ROWS]
-    return pl.pallas_call(
-        weight_kernel,
-        out_shape=outs,
-        in_specs=[spec(pltpu.VMEM)] * 21,
-        out_specs=[spec(pltpu.VMEM)] * 3,
-        compiler_params=pltpu.CompilerParams(vmem_limit_bytes=56 * MB),
-        name="weight_grads",
-    )(*here, *there, turn1, turn2, row_id)
-
-
-LAST_ROWS = (120, 128, 120)
+def halves_of(rows):
+    upper = (rows // 2 + 7) // 8 * 8
+    return pl.ds(0, upper), pl.ds(upper, rows - upper)
 
 
 def scatter_kernel(*refs):
-    parts, outs = refs[0:3], refs[3:6]
-    scratch = refs[6:]
-    mine, to_right, to_left = scratch[0:3], scratch[3:6], scratch[6:9]
-    got1, got2a, got2b = scratch[9:12], scratch[12:15], scratch[15:18]
-    last, got3 = scratch[18:21], scratch[21:24]
-    send, recv, local = scratch[24:]
+    here_h, (turn1, turn2, row_id), out_o, scratch = refs[0:9], refs[9:12], refs[12], refs[13:]
+    here, there = scratch[0:9], scratch[9:18]
+    parts, through, from_left, from_right = (scratch[18 + 3 * i : 21 + 3 * i] for i in range(4))
+    got2a, got2b, last, got3 = (scratch[30 + 3 * i : 33 + 3 * i] for i in range(4))
+    send, recv, pair_send, pair_recv, load = scratch[42:]
 
     dp, tm = lax.axis_index("dp"), lax.axis_index("tm")
     at = {"x": tm // 2, "y": dp // 4, "z": lax.rem(dp // 2, 2) * 2 + lax.rem(tm, 2)}
     core = lax.rem(dp, 2)
+    partner = {"dp": dp + 1 - 2 * core, "tm": tm}
 
     def device(axis, by):
         to = dict(at)
@@ -719,13 +673,40 @@
         }
 
     barrier = pltpu.get_barrier_semaphore()
+    pl.semaphore_signal(barrier, inc=1, device_id=partner, device_id_type=MESH)
     for axis in "xyz":
         for by in (1, 2, 3):
             pl.semaphore_signal(barrier, inc=1, device_id=device(axis, by), device_id_type=MESH)
-    pl.semaphore_wait(barrier, 9)
+    order = (0, 3, 2, 5, 1, 4, 8, 6, 7)
+    loads, pairs = {}, {}
+    for i in order:
+        picked = len(here_h[i].shape) == 3
+        loads[i] = pltpu.make_async_copy(
+            here_h[i].at[core] if picked else here_h[i], here[i], load.at[i]
+        )
+        pairs[i] = pltpu.make_async_remote_copy(
+            src_ref=here_h[i].at[1 - core] if picked else here_h[i],
+            dst_ref=there[i],
+            send_sem=pair_send.at[i],
+            recv_sem=pair_recv.at[i],
+            device_id=partner,
+            device_id_type=MESH,
+        )
+        loads[i].start()
+    pl.semaphore_wait(barrier, 10)
+    for i in order:
+        pairs[i].start()
+
+    def need(*which):
+        for i in which:
+            loads[i].wait()
+            pairs[i].wait_recv()
+
+    def both(i, cols=slice(None)):
+        return jnp.concatenate([here[i][:, cols], there[i][:, cols]], axis=0).astype(BF16)
 
     def remote(src, dst, k, slot, axis, by):
-        return pltpu.make_async_remote_copy(
+        copy = pltpu.make_async_remote_copy(
             src_ref=src,
             dst_ref=dst,
             send_sem=send.at[k, slot],
@@ -733,100 +714,112 @@
             device_id=device(axis, by),
             device_id_type=MESH,
         )
-
-    first, second = pl.ds(0, 2), pl.ds(2, 2)
+        copy.start()
+        return copy
+
+    def around(axis):
+        i = at[axis]
+        return i, lax.rem(i + 1, 4), lax.rem(i + 2, 4), lax.rem(i + 3, 4)
+
+    def head_part(k, first, onorm):
+        start, blocks = HEAD_BLOCKS[k]
+        for b in range(blocks):
+            cols = slice(128 * (start + b), 128 * (start + b + 1))
+            values = mm_at(onorm, both(5, cols))
+            if start + b == 8:
+                values = values + here[7][...] + there[7][...]
+            put(parts[k], first + 24 * b, values, 24)
+
+    low, high = pl.ds(0, 2), pl.ds(2, 2)
     sent = []
-    loads = []
+
+    def phase1(k):
+        axis, p = ORDERS[k][0], parts[k]
+        i, right, opposite, left = around(axis)
+        sent.append(
+            [
+                remote(p.at[opposite, low], through[k].at[0], k, 0, axis, 1),
+                remote(p.at[opposite, high], through[k].at[1], k, 1, axis, 3),
+                remote(p.at[right, high], from_left[k].at[high], k, 2, axis, 1),
+                remote(p.at[left, low], from_right[k].at[low], k, 3, axis, 3),
+            ]
+        )
+
+    need(0, 3)
+    normed = both(0)
+    for c in range(FF // 256):
+        put(parts[0], 48 * c, mm_at(normed, both(3, slice(256 * c, 256 * (c + 1)))), 24)
+    need(2, 5)
+    onorm = both(2)
+    head_part(0, 432, onorm)
+    phase1(0)
+    need(1, 4)
+    hidden = both(1)
+    for c in range(3):
+        put(parts[1], 144 * c, mm_at(hidden, both(4, slice(256 * c, 256 * (c + 1)))), 72)
+    head_part(1, 432, mm(onorm, turn1[...]).astype(BF16))
+    phase1(1)
+    need(8, 6, 7)
+    ids = jnp.concatenate([here[8][...], there[8][...]], axis=1)
+    rows = row_id[...] + OWN * core
+    hot = (rows == ids[0:1, :]) | (rows == ids[1:2, :] + 1024)
+    hot = jnp.where(hot, 1.0, 0.0).astype(BF16)
+    for c in range(3):
+        put(parts[2], 128 * c, mm(hot, both(6, slice(256 * c, 256 * (c + 1)))), 64)
+    head_part(2, 384, mm(onorm, turn2[...]).astype(BF16))
+    phase1(2)
+
     for k in range(3):
-        axis, p, g = ORDERS[k][0], parts[k], got1[k]
-        i = at[axis]
-        right, opposite, left = lax.rem(i + 1, 4), lax.rem(i + 2, 4), lax.rem(i + 3, 4)
-        copies = [
-            remote(p.at[opposite, first], g.at[0], k, 0, axis, 1),
-            remote(p.at[opposite, second], g.at[1], k, 1, axis, 3),
-            remote(p.at[right, second], g.at[3], k, 3, axis, 1),
-            remote(p.at[left, first], g.at[4], k, 4, axis, 3),
-        ]
-        here = [
-            pltpu.make_async_copy(p.at[right, first], to_right[k], local.at[k, 0]),
-            pltpu.make_async_copy(p.at[left, second], to_left[k], local.at[k, 1]),
-            pltpu.make_async_copy(p.at[i], mine[k], local.at[k, 2]),
-        ]
-        for copy in copies + here:
-            copy.start()
-        sent.append(copies)
-        loads.append(here)
+        axis, p = ORDERS[k][0], parts[k]
+        i, right, opposite, left = around(axis)
+        sent[k][0].wait_recv()
+        p[right, low] += through[k][0]
+        sent[k].append(remote(p.at[right, low], from_left[k].at[low], k, 4, axis, 1))
+        sent[k][1].wait_recv()
+        p[left, high] += through[k][1]
+        sent[k].append(remote(p.at[left, high], from_right[k].at[high], k, 5, axis, 3))
     for k in range(3):
-        axis, g = ORDERS[k][0], got1[k]
-        loads[k][0].wait()
-        sent[k][0].wait_recv()
-        to_right[k][...] += g[0]
-        sent[k].append(remote(to_right[k], g.at[2], k, 2, axis, 1))
-        sent[k][-1].start()
-        loads[k][1].wait()
-        sent[k][1].wait_recv()
-        to_left[k][...] += g[1]
-        sent[k].append(remote(to_left[k], g.at[5], k, 5, axis, 3))
-        sent[k][-1].start()
+        mine = at[ORDERS[k][0]]
+        axis, p, a, b = ORDERS[k][1], parts[k], got2a[k], got2b[k]
+        i, right, opposite, left = around(axis)
+        upper, lower = halves_of(PART_ROWS[k])
+        for j in (2, 3, 4, 5):
+            sent[k][j].wait_recv()
+        p[mine, opposite] += from_left[k][opposite] + from_right[k][opposite]
+        sent[k].append(remote(p.at[mine, opposite, upper], a.at[0], k, 6, axis, 1))
+        sent[k].append(remote(p.at[mine, opposite, lower], b.at[0], k, 7, axis, 3))
+        p[mine, right] += from_left[k][right] + from_right[k][right]
+        sent[k].append(remote(p.at[mine, right, lower], b.at[1], k, 8, axis, 1))
+        p[mine, left] += from_left[k][left] + from_right[k][left]
+        sent[k].append(remote(p.at[mine, left, upper], a.at[1], k, 9, axis, 3))
+        p[mine, i] += from_left[k][i] + from_right[k][i]
     for k in range(3):
-        g, m = got1[k], mine[k]
-        loads[k][2].wait()
-        sent[k][2].wait_recv()
-        sent[k][3].wait_recv()
-        sent[k][4].wait_recv()
-        sent[k][5].wait_recv()
-        m[0:2] += g[2] + g[4]
-        m[2:4] += g[3] + g[5]
-        axis = ORDERS[k][1]
-        i = at[axis]
-        right, opposite, left = lax.rem(i + 1, 4), lax.rem(i + 2, 4), lax.rem(i + 3, 4)
-        n = PART_ROWS[k]
-        cut = (n // 2 + 7) // 8 * 8
-        upper, lower = pl.ds(0, cut), pl.ds(cut, n - cut)
-        a, b = got2a[k], got2b[k]
-        copies = [
-            remote(m.at[opposite, upper], a.at[0], k, 6, axis, 1),
-            remote(m.at[opposite, lower], b.at[0], k, 7, axis, 3),
-            remote(m.at[right, lower], b.at[1], k, 8, axis, 1),
-            remote(m.at[left, upper], a.at[1], k, 9, axis, 3),
-        ]
-        for copy in copies:
-            copy.start()
-        sent[k] = sent[k] + copies
+        mine = at[ORDERS[k][0]]
+        axis, p, a, b = ORDERS[k][1], parts[k], got2a[k], got2b[k]
+        i, right, opposite, left = around(axis)
+        upper, lower = halves_of(PART_ROWS[k])
+        sent[k][6].wait_recv()
+        p[mine, right, upper] += a[0]
+        sent[k].append(remote(p.at[mine, right, upper], a.at[2], k, 10, axis, 1))
+        sent[k][7].wait_recv()
+        p[mine, left, lower] += b[0]
+        sent[k].append(remote(p.at[mine, left, lower], b.at[2], k, 11, axis, 3))
     for k in range(3):
-        axis = ORDERS[k][1]
-        i = at[axis]
-        right, left = lax.rem(i + 1, 4), lax.rem(i + 3, 4)
-        n = PART_ROWS[k]
-        cut = (n // 2 + 7) // 8 * 8
-        upper, lower = pl.ds(0, cut), pl.ds(cut, n - cut)
-        m, a, b = mine[k], got2a[k], got2b[k]
-        sent[k][6].wait_recv()
-        m[right, upper] += a[0]
-        sent[k].append(remote(m.at[right, upper], a.at[2], k, 10, axis, 1))
-        sent[k][-1].start()
-        sent[k][7].wait_recv()
-        m[left, lower] += b[0]
-        sent[k].append(remote(m.at[left, lower], b.at[2], k, 11, axis, 3))
-        sent[k][-1].start()
-    for k in range(3):
-        axis = ORDERS[k][1]
-        i = at[axis]
-        n = PART_ROWS[k]
-        cut = (n // 2 + 7) // 8 * 8
-        upper, lower = pl.ds(0, cut), pl.ds(cut, n - cut)
-        m, a, b, out = mine[k], got2a[k], got2b[k], last[k]
+        mine = at[ORDERS[k][0]]
+        i = at[ORDERS[k][1]]
+        p, a, b, out = parts[k], got2a[k], got2b[k], last[k]
+        upper, lower = halves_of(PART_ROWS[k])
         for j in (8, 9, 10, 11):
             sent[k][j].wait_recv()
-        m[i, upper] += a[1] + a[2]
-        m[i, lower] += b[1] + b[2]
+        p[mine, i, upper] += a[1] + a[2]
+        p[mine, i, lower] += b[1] + b[2]
         blocks = (((18, 24), (2, 24)), ((6, 72), (3, 24)), ((6, 64), (4, 24)))[k]
         start, place = 0, 0
         for count, rows in blocks:
             each = rows // 4
             for _ in range(count):
                 for d in range(4):
-                    out[d, pl.ds(place, each)] = m[i, pl.ds(start + d * each, each)]
+                    out[d, pl.ds(place, each)] = p[mine, i, pl.ds(start + d * each, each)]
                 start += rows
                 place += each
         if place < LAST_ROWS[k]:
@@ -835,55 +828,58 @@
                     (LAST_ROWS[k] - place, 128), F32
                 )
         axis = ORDERS[k][2]
-        i = at[axis]
         for by in (1, 2, 3):
-            copy = remote(
-                out.at[lax.rem(i + by, 4)], got3[k].at[by - 1], k, 11 + by, axis, by
-            )
-            copy.start()
-            sent[k].append(copy)
+            to = lax.rem(at[axis] + by, 4)
+            sent[k].append(remote(out.at[to], got3[k].at[by - 1], k, 11 + by, axis, by))
     for k in range(3):
         for j in (12, 13, 14):
             sent[k][j].wait_recv()
-        outs[k][...] = last[k][at[ORDERS[k][2]]] + got3[k][0] + got3[k][1] + got3[k][2]
+        total = last[k][at[ORDERS[k][2]]] + got3[k][0] + got3[k][1] + got3[k][2]
+        out_o[pl.ds(FIRST_ROWS[k], LAST_ROWS[k]), :] = total
+    for i in order:
+        pairs[i].wait_send()
     for k in range(3):
         for copy in sent[k]:
             copy.wait_send()
 
 
-def scatter_call(parts):
+def scatter_call(operands, turn1, turn2, row_id):
     def each(make):
-        return [make(k) for k in range(3)]
+        return [pltpu.VMEM(make(k), F32) for k in range(3)]
 
     rows = PART_ROWS
-    cuts = [(n // 2 + 7) // 8 * 8 for n in rows]
+    cuts = [halves_of(n)[0].size for n in rows]
     return pl.pallas_call(
         scatter_kernel,
-        out_shape=[full(n, 128) for n in LAST_ROWS],
-        in_specs=[spec(pl.ANY)] * 3,
-        out_specs=[spec(pltpu.VMEM)] * 3,
-        scratch_shapes=each(lambda k: pltpu.VMEM((4, rows[k], 128), F32))
-        + each(lambda k: pltpu.VMEM((2, rows[k], 128), F32))
-        + each(lambda k: pltpu.VMEM((2, rows[k], 128), F32))
-        + each(lambda k: pltpu.VMEM((6, 2, rows[k], 128), F32))
-        + each(lambda k: pltpu.VMEM((3, cuts[k], 128), F32))
-        + each(lambda k: pltpu.VMEM((3, rows[k] - cuts[k], 128), F32))
-        + each(lambda k: pltpu.VMEM((4, LAST_ROWS[k], 128), F32))
-        + each(lambda k: pltpu.VMEM((3, LAST_ROWS[k], 128), F32))
+        out_shape=full(sum(LAST_ROWS), 128),
+        in_specs=[spec(pl.ANY)] * 9 + [spec(pltpu.VMEM)] * 3,
+        out_specs=spec(pltpu.VMEM),
+        scratch_shapes=vmem(OPERANDS)
+        + vmem(OPERANDS)
+        + each(lambda k: (4, 4, rows[k], 128))
+        + each(lambda k: (2, 2, rows[k], 128))
+        + each(lambda k: (4, rows[k], 128))
+        + each(lambda k: (4, rows[k], 128))
+        + each(lambda k: (3, cuts[k], 128))
+        + each(lambda k: (3, rows[k] - cuts[k], 128))
+        + each(lambda k: (4, LAST_ROWS[k], 128))
+        + each(lambda k: (3, LAST_ROWS[k], 128))
         + [
             pltpu.SemaphoreType.DMA((3, 15)),
             pltpu.SemaphoreType.DMA((3, 15)),
-            pltpu.SemaphoreType.DMA((3, 3)),
+            pltpu.SemaphoreType.DMA((9,)),
+            pltpu.SemaphoreType.DMA((9,)),
+            pltpu.SemaphoreType.DMA((9,)),
         ],
         compiler_params=pltpu.CompilerParams(
-            collective_id=3, has_side_effects=True, vmem_limit_bytes=48 * MB
+            collective_id=3, has_side_effects=True, vmem_limit_bytes=60 * MB
         ),
-        name="reduce_scatter",
-    )(*parts)
-
-
-def finish_kernel(s0, s1, s2, loss_o, table_o, kern_o, up_o, down_o, scale_o, head_o):
-    sources = (s0, s1, s2)
+        name="weight_grads_scatter",
+    )(*operands, turn1, turn2, row_id)
+
+
+def finish_kernel(sums, loss_o, table_o, kern_o, up_o, down_o, scale_o, head_o):
+    sources = [sums.at[pl.ds(FIRST_ROWS[k], LAST_ROWS[k])] for k in range(3)]
     for k, (out, count, each) in enumerate(((up_o, 18, 6), (down_o, 6, 18), (table_o, 6, 16))):
         for c in range(count):
             out[:, 128 * c : 128 * (c + 1)] = sources[k][each * c : each * (c + 1), :]
@@ -908,10 +904,10 @@
         out_shape=[
             full(1, 1), full(16, D), full(7, 6), full(6, FF), full(18, D), full(1, 6), full(6, 1026),
         ],
-        in_specs=[spec(pltpu.VMEM)] * 3,
+        in_specs=[spec(pltpu.VMEM)],
         out_specs=[spec(pltpu.VMEM)] * 7,
         name="finish",
-    )(*sums)
+    )(sums)
     return loss.reshape(()), table, kern, up, down, scale.reshape(6), head
 
 
@@ -932,9 +928,7 @@
         saved,
         (a1, a2, syn, head_t, down_weight, up_weight, pick_n, pick_h, pick_k),
     )
-    here = [*operands, ids]
-    parts = weight_call(here, pair_call(here), turn1, turn2, row_id)
-    return finish_call(scatter_call(parts))
+    return finish_call(scatter_call([*operands, ids], turn1, turn2, row_id))
 
 
 def solution(mesh):

time: 131 us -> 118 us (0.901)
  Pallas kernels: 125 us -> 115 us
  local copies, waits for them, and re-layouts: 3.97 us -> 0 us
    pallas_call x3 -> x1, Pallas kernels: 77.2 us -> 66.8 us  [scatter_call(): pl.pallas_call(scatter_kernel, out_shape=full(sum(LAST_ROWS), 128), in_sp...]
    unnamed x8 -> x0, local copies, waits for them, and re-layouts: 3.97 us -> none
where the time goes in v4:
time: 118 us; the launch traced here: 116 us
  Pallas kernels  115 us (97%)
  between operations  1.32 us (1%)
    pallas_call x1, Pallas kernels, scatter_call(): pl.pallas_call(scatter_kernel, out_shape=full(sum(LAST_ROWS), 128), in_sp...  66.8 us
    pallas_call x1, Pallas kernels, backward_call(): pl.pallas_call(backward_kernel, out_shape=outs, in_specs=[spec(pltpu.VMEM...  16.9 us
    pallas_call x1, Pallas kernels, forward_call(): pl.pallas_call(forward_kernel, out_shape=outs, in_specs=[spec(pltpu.VMEM)...  13.3 us
    pallas_call x1, Pallas kernels, stat_call(): pl.pallas_call(stat_kernel, out_shape=full(8, 128), in_specs=[spec(pltpu....  8.64 us
    pallas_call x1, Pallas kernels, halo_call(): pl.pallas_call(halo_kernel, out_shape=[edge, edge, around, around], in_sp...  7.73 us

profile of v4, /device:TPU:0, one launch (start us, length us, event | category | flops | bytes accessed | tf_op | source)
XLA Modules:
  0.0 116.3 jit_solution(12676903382859648752)
XLA Ops:
  1.3 7.7 %halo.1 = (f32[1,4096]{1,0:T(1,128)}, f32[1,4096]{1,0:T(1,128)}, s32[2,128]{1,0:T(2,128)}, s32[2,128]{1,0:T(2,128)}) custom-call(f32[1,32768]{1,0:T(1,128)} %target.3, s32[2,128]{1,0:T(2,128)} %bitcast.10), custom_call_target="tpu_custom_call" | custom-call | tf_op jit(solution)/shard_map/halo/pallas_call | solution.py:209
  9.0 13.3 %forward.1 = (f32[160,768]{1,0:T(8,128)}, f32[160,128]{1,0:T(8,128)}, f32[160,768]{1,0:T(8,128)}, f32[160,2304]{1,0:T(8,128)}, bf16[128,2304]{1,0:T(8,128)(2,1)}...) custom-call(f32[1,32768]{1,0:T(1,128)} %target.3, ...), custom_call_target="tpu_custom_call" | custom-call | tf_op jit(solution)/shard_map/forward/pallas_call | solution.py:384
  22.3 8.6 %clip_sums.1.stat = f32[8,128]{1,0:T(8,128)} custom-call(f32[8,128]{1,0:T(8,128)} %get-tuple-element.44.stat), custom_call_target="tpu_custom_call" | custom-call | tf_op jit(solution)/shard_map/clip_sums/pallas_call | solution.py:438
  31.0 16.9 %backward.1 = (f32[2,128,384]{2,1,0:T(8,128)}, f32[2,128,1152]{2,1,0:T(8,128)}, f32[2,128,384]{2,1,0:T(8,128)}, f32[128,2304]{1,0:T(8,128)}, f32[128,768]{1,0:T(...) custom-call(f32[7,768]{1,0:T(8,128)} %kern.3, f32[768]{0:T(1024)} %scale_i.3, ...), custom_call_target="tpu_custom_call" | custom-call | tf_op jit(solution)/shard_map/backward/pallas_call | solution.py:613
  47.9 66.8 %weight_grads_scatter.1.sums = f32[368,128]{1,0:T(8,128)} custom-call(f32[2,128,384]{2,1,0:T(8,128)} %get-tuple-element.58.refs_0_, f32[2,128,1152]{2,1,0:T(8,128)} %get-tuple-element.59.refs_1_, f32[2,128,384]{2,1,0:T(8,128)} %get-tuple-element.60.refs_2_, f32[128,2304]{1,0:T(8,128)} %get-tuple-element.61.refs_3_, f32[128,768]{1,0:T(8,128)} %get-tuple-element.62.refs_4_, ...), custom_call_target="tpu_custom_call" | custom-call | tf_op jit(solution)/shard_map/weight_grads_scatter/pallas_call | solution.py:852
  114.7 1.6 %finish.1 = (f32[1,1]{1,0:T(1,128)}, f32[16,768]{1,0:T(8,128)}, f32[7,6]{1,0:T(8,128)}, f32[6,2304]{1,0:T(8,128)}, f32[18,768]{1,0:T(8,128)}, /*index=5*/f32[1,6]{1,0:T(1,128)}, f32[6,1026]{1,0:T(8,128)}) custom-call(f32[368,128]{1,0:T(8,128)} %weight_grads_scatter.1.sums), custom_call_target="tpu_custom_call" | custom-call | tf_op jit(solution)/shard_map/finish/pallas_call | solution.py:902

commit v5 on v4

--- a/solution.py
+++ b/solution.py
@@ -170,86 +170,99 @@
     return jax.ShapeDtypeStruct(shape, dtype)
 
 
-def halo_kernel(target, ids, left_t, right_t, left_i, right_i, send, recv):
-    tm = lax.axis_index("tm")
-    right, left = lax.rem(tm + 1, 8), lax.rem(tm + 7, 8)
-    barrier = pltpu.get_barrier_semaphore()
-    for there in (left, right):
-        pl.semaphore_signal(barrier, inc=1, device_id={"tm": there}, device_id_type=MESH)
-    pl.semaphore_wait(barrier, 2)
-    edge = HALO * HOP
-    copies = []
-    for i, (src, dst, there) in enumerate(
-        (
-            (target.at[:, pl.ds(OWN * HOP - edge, edge)], left_t, right),
-            (target.at[:, pl.ds(0, edge)], right_t, left),
-            (ids, left_i, right),
-            (ids, right_i, left),
-        )
-    ):
-        copies.append(
-            pltpu.make_async_remote_copy(
-                src_ref=src,
-                dst_ref=dst,
-                send_sem=send.at[i],
-                recv_sem=recv.at[i],
-                device_id={"tm": there},
-                device_id_type=MESH,
-            )
-        )
-    for copy in copies:
-        copy.start()
-    for copy in copies:
-        copy.wait()
-
-
-def halo_call(target, ids):
-    edge = full(1, HALO * HOP)
-    around = full(2, OWN, dtype=jnp.int32)
-    return pl.pallas_call(
-        halo_kernel,
-        out_shape=[edge, edge, around, around],
-        in_specs=[spec(pltpu.VMEM)] * 2,
-        out_specs=[spec(pltpu.VMEM)] * 4,
-        scratch_shapes=[pltpu.SemaphoreType.DMA((4,)), pltpu.SemaphoreType.DMA((4,))],
-        compiler_params=pltpu.CompilerParams(collective_id=0, has_side_effects=True),
-        name="halo",
-    )(target, ids)
-
-
 def ids_column(ids):
     padded = jnp.concatenate([ids.astype(F32), jnp.zeros((126, OWN), F32)], axis=0)
     return jnp.transpose(padded)[:, :2]
 
 
-def forward_kernel(
-    target, left_t, right_t, ids, left_i, right_i, kern, scale_i, win,
-    table_h, up_h, down_h, head_h, syn_h, a1_h, a2_h, *refs,
-):
-    outs, stat_o, refs = refs[: len(SAVED)], refs[len(SAVED)], refs[len(SAVED) + 1 :]
-    (sin_o, rstd_o, y1_o, gp_o, hid_o, down_o, y2_o, re_o, im_o, d1_o, q1_o, d2_o, q2_o) = refs[
-        : len(SAVED)
+OPERANDS = (
+    full(OWN, 384), full(OWN, 1152), full(OWN, 384), full(OWN, FF), full(OWN, D),
+    full(OWN, 1152), full(OWN, D), full(384, 128),
+)
+PICKED = (True, True, True, False, False, False, False, True)
+IDS = full(2, OWN, dtype=jnp.int32)
+SAVED = (
+    full(ROWS, D), full(ROWS, 128), full(ROWS, D), full(ROWS, FF),
+    full(ROWS, D), full(ROWS, D), full(ROWS, CHUNKS1 * 128), full(ROWS, CHUNKS1 * 128),
+    full(ROWS, WIDE1), full(ROWS, WIDE1), full(2 * ROWS, WIDE2), full(2 * ROWS, WIDE2),
+)
+
+
+def vmem(shapes):
+    return [pltpu.VMEM(a.shape, a.dtype) for a in shapes]
+
+
+def step_kernel(target, ids, kern, scale_i, win, loss_scale, *refs):
+    big_h, refs = refs[:10], refs[10:]
+    here_h, refs = refs[:8], refs[8:]
+    there_h, refs = refs[:9], refs[9:]
+    big_v, refs = refs[:10], refs[10:]
+    (table_v, up_v, down_v, head_v, syn_v, a1_v, a2_v, pick_n, pick_h, pick_k) = big_v
+    (sin_o, rstd_o, y1_o, gp_o, down_o, y2_o, re_o, im_o, d1_o, q1_o, d2_o, q2_o) = refs[:12]
+    refs = refs[12:]
+    kept, refs = refs[:8], refs[8:]
+    (nrm_o, hid_o, onm_o, dup_o, ddn_o, dhd_o, dem_o, kg_o) = kept
+    (left_t, right_t, left_i, right_i, goal, codes, hid_v, head_s, spec_v, seg1, seg2), refs = (
+        refs[:11], refs[11:],
+    )
+    (stat_o, slots, dfr, dphase, dhead, dup, small), refs = refs[:7], refs[7:]
+    sems, halo_send, halo_recv, stat_send, stat_recv, pair_send, pair_recv, save_sems = refs
+
+    dp, tm = lax.axis_index("dp"), lax.axis_index("tm")
+    core = lax.rem(dp, 2)
+    partner = {"dp": dp + 1 - 2 * core, "tm": tm}
+    others = [{"dp": dp, "tm": lax.rem(tm + j, 8)} for j in range(1, 8)]
+    barrier = pltpu.get_barrier_semaphore()
+    for there in others + [partner]:
+        pl.semaphore_signal(barrier, inc=1, device_id=there, device_id_type=MESH)
+    copies = [pltpu.make_async_copy(h, v, sems.at[i]) for i, (h, v) in enumerate(zip(big_h, big_v))]
+    for copy in copies:
+        copy.start()
+
+    def remote(src, dst, send, recv, there):
+        copy = pltpu.make_async_remote_copy(
+            src_ref=src, dst_ref=dst, send_sem=send, recv_sem=recv,
+            device_id=there, device_id_type=MESH,
+        )
+        copy.start()
+        return copy
+
+    edge = HALO * HOP
+    right, left = others[0], others[6]
+    pl.semaphore_wait(barrier, 8)
+    halo = [
+        remote(src, dst, halo_send.at[i], halo_recv.at[i], there)
+        for i, (src, dst, there) in enumerate(
+            (
+                (ids, left_i, right),
+                (ids, right_i, left),
+                (target.at[:, pl.ds(OWN * HOP - edge, edge)], left_t, right),
+                (target.at[:, pl.ds(0, edge)], right_t, left),
+            )
+        )
     ]
-    kept = refs[: len(SAVED)]
-    refs = refs[len(SAVED) :]
-    (table_v, up_v, down_v, head_v, syn_v, a1_v, a2_v) = refs[:7]
-    goal, codes, hid_v, head_s, spec_v, seg1, seg2, sems, out_sems = refs[7:]
-    pairs = (
-        (table_h, table_v), (up_h, up_v), (down_h, down_v), (head_h, head_v),
-        (syn_h, syn_v), (a1_h, a1_v), (a2_h, a2_v),
-    )
-    copies = [pltpu.make_async_copy(h, v, sems.at[i]) for i, (h, v) in enumerate(pairs)]
-    copies[0].start()
-    copies[1].start()
-    saves = [pltpu.make_async_copy(v, h, out_sems.at[i]) for i, (v, h) in enumerate(zip(kept, outs))]
+    pairs = [remote(ids, there_h[8], pair_send.at[8], pair_recv.at[8], partner)]
+    saves = [
+        pltpu.make_async_copy(v.at[core] if p else v, h, save_sems.at[i])
+        for i, (v, h, p) in enumerate(zip(kept, here_h, PICKED))
+    ]
+
+    def give(i):
+        saves[i].start()
+        source = kept[i].at[1 - core] if PICKED[i] else kept[i]
+        pairs.append(remote(source, there_h[i], pair_send.at[i], pair_recv.at[i], partner))
+
     scale = scale_i[...].reshape(1, D)
-    for source, first, count, skip in (
-        (left_t, 0, HALO, 0), (target, HALO, OWN, 0), (right_t, HALO + OWN, HALO, 0),
+    codes[HALO : HALO + OWN, :] = ids_column(ids[...])
+    for source, first, count in (
+        (target, HALO, OWN), (left_t, 0, HALO), (right_t, HALO + OWN, HALO),
     ):
+        if source is left_t:
+            for copy in halo:
+                copy.wait_recv()
         for r in range(count):
             goal[first + r : first + r + 1, :] = source[:, HOP * r : HOP * (r + 1)]
     codes[0:HALO, :] = ids_column(left_i[...])[OWN - HALO :]
-    codes[HALO : HALO + OWN, :] = ids_column(ids[...])
     codes[HALO + OWN :, :] = ids_column(right_i[...])[:HALO]
     places = frame_places()
     valid = inside(places)
@@ -257,42 +270,29 @@
     hot = (lane == codes[:, 0:1]) | (lane == codes[:, 1:2] + 1024.0)
     hot = jnp.where(hot, 1.0, 0.0).astype(BF16)
     copies[0].wait()
-    copies[2].start()
     y0, rstd0 = norm(mm(hot, table_v[...]))
     y0 = jnp.where(valid, y0, 0.0)
     sin_o[...] = y0
-    saves[0].start()
     mixture = kern[0:1, :] * shift(y0, 3)
     for k in range(1, 7):
         mixture = mixture + kern[k : k + 1, :] * shift(y0, 3 - k)
     y1, rstd1 = norm(mixture)
     y1_o[...] = y1
-    saves[2].start()
     normed = y1.astype(BF16)
     copies[1].wait()
-    copies[3].start()
-    copies[4].start()
     for c in range(FF // 256):
         at = slice(256 * c, 256 * (c + 1))
         up = mm(normed, up_v[:, at])
         cdf = 0.5 * (1.0 + lax.erf(up * 0.7071067811865476))
         hid_v[:, at] = (up * cdf).astype(BF16)
         gp_o[:, at] = cdf + up * (0.3989422804014327 * jnp.exp(-0.5 * up * up))
-    hid_o[...] = hid_v[HALO : HALO + OWN, :]
-    saves[3].start()
-    saves[4].start()
     copies[2].wait()
-    copies[5].start()
-    copies[6].start()
     down = mm(hid_v[...], down_v[...])
     down_o[...] = down
-    saves[5].start()
     y2, rstd2 = norm(y0 + scale * down)
     y2_o[...] = y2
-    saves[6].start()
     places128 = lax.broadcasted_iota(jnp.int32, (ROWS, 128), 1)
     rstd_o[...] = jnp.where(places128 == 0, rstd0, jnp.where(places128 == 1, rstd1, rstd2))
-    saves[1].start()
     onorm = y2.astype(BF16)
     copies[3].wait()
     head_s[:, 1024:] = jnp.zeros((ROWS, 128), F32)
@@ -312,8 +312,6 @@
         im_o[:, 128 * c : 128 * (c + 1)] = im
         spec_v[:, 256 * c : 256 * c + 128] = re.astype(BF16)
         spec_v[:, 256 * c + 128 : 256 * (c + 1)] = im.astype(BF16)
-    saves[7].start()
-    saves[8].start()
     copies[4].wait()
     pred = jnp.zeros((ROWS, HOP), F32)
     for p in range(4):
@@ -358,36 +356,142 @@
                 sums[0] = sums[0] + dr * dr + di * di
                 sums[1] = sums[1] + power_g[own]
                 sums[2] = sums[2] + gap[own] * gap[own]
-        saves[9 + 2 * level].start()
-        saves[10 + 2 * level].start()
         for i in range(3):
             total = jnp.sum(jnp.sum(sums[i], axis=0, keepdims=True), axis=1, keepdims=True)
             stat_o[3 * level + i : 3 * level + i + 1, :] = jnp.broadcast_to(total, (1, 128))
     stat_o[6:8, :] = jnp.zeros((2, 128), F32)
-    for save in saves:
-        save.wait()
-
-
-SAVED = (
-    full(ROWS, D), full(ROWS, 128), full(ROWS, D), full(ROWS, FF), full(OWN, FF, dtype=BF16),
-    full(ROWS, D), full(ROWS, D), full(ROWS, CHUNKS1 * 128), full(ROWS, CHUNKS1 * 128),
-    full(ROWS, WIDE1), full(ROWS, WIDE1), full(2 * ROWS, WIDE2), full(2 * ROWS, WIDE2),
-)
-
-
-def vmem(shapes):
-    return [pltpu.VMEM(a.shape, a.dtype) for a in shapes]
-
-
-def forward_call(small, big):
-    outs = list(SAVED) + [full(8, 128)]
+    shares = [
+        remote(stat_o, slots.at[tm], stat_send.at[j], stat_recv.at[j], there)
+        for j, there in enumerate(others)
+    ]
+    slots[tm] = stat_o[...]
+
+    copies[7].wait()
+    copies[8].wait()
+    normed = y1_o[own, :].astype(BF16)
+    onorm = y2_o[own, :].astype(BF16)
+    for c in range(2):
+        nrm_o[c] = mm(normed, pick_n[c])
+        onm_o[c] = mm(onorm, pick_n[c])
+        for h in range(2):
+            out = slice(576 * h, 576 * (h + 1))
+            hid_o[c, :, out] = mm(hid_v[own, 1152 * h : 1152 * (h + 1)], pick_h[c])
+    for i in (0, 2, 1):
+        give(i)
+
+    for share in shares:
+        share.wait_recv()
+    total = slots[0]
+    for j in range(1, 8):
+        total = total + slots[j]
+
+    factor = loss_scale[...] * (0.5 / CLIPS)
+    loss = jnp.zeros((1, 1), F32)
+    cots = []
+    for level in range(2):
+        count = ((FRAMES * 513), (2 * FRAMES * 257))[level]
+        sum_a = total[3 * level : 3 * level + 1, 0:1]
+        sum_b = total[3 * level + 1 : 3 * level + 2, 0:1]
+        sum_g = total[3 * level + 2 : 3 * level + 3, 0:1]
+        root_a, root_b = jnp.sqrt(sum_a + 1e-6), jnp.sqrt(sum_b + 1e-6)
+        loss = loss + root_a / root_b + sum_g * (1.0 / count)
+        cots.append((factor / (root_a * root_b), factor * (1.0 / count)))
+    loss = jnp.where(lax.axis_index("tm") == 0, loss, 0.0)
+
+    dx = jnp.zeros((ROWS, HOP), F32)
+    ds1 = (cots[0][0] * d1_o[...] + cots[0][1] * q1_o[...]).astype(BF16)
+    for p in range(4):
+        at = slice(HOP * p, HOP * (p + 1))
+        piece = mm_bt(ds1, a1_v[at, :]).astype(BF16).astype(F32) * win[0:1, at]
+        dx = dx + shift(piece, p - 2)
+    ds2 = (cots[1][0] * d2_o[...] + cots[1][1] * q2_o[...]).astype(BF16)
+    dseg = mm_bt(ds2, a2_v[...]).astype(BF16).astype(F32) * win[2:3, : NFFT // 2]
+    even, odd = dseg[:ROWS], dseg[ROWS:]
+    dx = dx + shift(even[:, :256], -1) + even[:, 256:] + odd[:, 128:384]
+    dx = dx + jnp.concatenate([shift(odd[:, 384:], 1), shift(odd[:, :128], -1)], axis=1)
+    dx = jnp.where(valid, dx / envelope(places, win), 0.0)
+    for p in range(4):
+        piece = jnp.where(valid, shift(dx, 2 - p), 0.0)
+        dfr[:, HOP * p : HOP * (p + 1)] = piece.astype(BF16)
+
+    for c in range(CHUNKS1):
+        dsp = mm_bt(dfr[...], syn_v[256 * c : 256 * (c + 1), :]).astype(BF16).astype(F32)
+        dre, dim = dsp[:, :128], dsp[:, 128:]
+        re, im = re_o[:, 128 * c : 128 * (c + 1)], im_o[:, 128 * c : 128 * (c + 1)]
+        dlog, dph = dre * re + dim * im, dim * re - dre * im
+        if c < 4:
+            dhead[:, 128 * c : 128 * (c + 1)] = dlog.astype(BF16)
+        dphase[:, 128 * c : 128 * (c + 1)] = dph
+    moved = pltpu.roll(dphase[...], 1, 1)
+    dhead[:, 512:640] = (moved[:, :128] + dlog).astype(BF16)
+    dhead[:, 640:] = moved[:, 128:].astype(BF16)
+    dhd_o[...] = dhead[own, :].astype(F32)
+    give(5)
+    don = mm(dhead[:, :1026], head_v[...]).astype(BF16).astype(F32)
+    dstream = norm_back(don, y2_o[...], rstd_o[:, 2:3])
+
+    scale_grad = jnp.sum(dstream[own] * down_o[own, :], axis=0, keepdims=True)
+    ddn = (scale * dstream).astype(BF16)
+    ddn_o[...] = ddn[own].astype(F32)
+    give(4)
+    for c in range(FF // 256):
+        at = slice(256 * c, 256 * (c + 1))
+        dh = mm_bt(ddn, down_v[at, :]).astype(BF16).astype(F32)
+        dup[:, at] = (dh * gp_o[:, at]).astype(BF16)
+    dup_o[...] = dup[own, :].astype(F32)
+    give(3)
+    dnorm = mm_bt(dup[...], up_v[...]).astype(BF16).astype(F32)
+    dmix = norm_back(dnorm, y1_o[...], rstd_o[:, 1:2])
+    dmix = jnp.where(valid, dmix, 0.0)
+    y0 = sin_o[...]
+    dsin = dstream
+    small[...] = jnp.zeros((128, D), F32)
+    for k in range(7):
+        dsin = dsin + kern[k : k + 1, :] * shift(dmix, k - 3)
+        taps = dmix * shift(y0, 3 - k)
+        small[2 + k : 3 + k, :] = jnp.sum(taps[own], axis=0, keepdims=True)
+    demb = norm_back(dsin, y0, rstd_o[:, 0:1])
+    dem_o[...] = demb[own].astype(BF16).astype(F32)
+    give(6)
+
+    small[9:10, :] = scale_grad
+    rest = loss
+    for i, grid in enumerate((65536.0, 1.0, 1.0 / 65536.0, 1.0 / 65536.0 / 65536.0)):
+        piece = jnp.floor(rest * (1.0 / grid)) * grid
+        rest = rest - piece
+        small[10 + i : 11 + i, :] = jnp.broadcast_to(piece, (1, D))
+
+    copies[9].wait()
+    small0 = small[...].astype(BF16)
+    left = small[...] - small0.astype(F32)
+    small1 = left.astype(BF16)
+    small2 = (left - small1.astype(F32)).astype(BF16)
+    for c in range(2):
+        kg_o[c] = sum(
+            lax.dot_general(pick_k[c], s, (((0,), (1,)), ((), ())), preferred_element_type=F32)
+            for s in (small0, small1, small2)
+        )
+    give(7)
+    for i in range(8):
+        saves[i].wait()
+    for copy in pairs:
+        copy.wait()
+    for copy in halo + shares:
+        copy.wait_send()
+
+
+def step_call(small, big):
+    wide = [full(*((2,) if p else ()), *a.shape) for a, p in zip(OPERANDS, PICKED)]
+    edge = full(1, HALO * HOP)
     return pl.pallas_call(
-        forward_kernel,
-        out_shape=outs,
+        step_kernel,
+        out_shape=[*OPERANDS, *OPERANDS, IDS],
         in_specs=[spec(pltpu.VMEM)] * len(small) + [spec(pl.ANY)] * len(big),
-        out_specs=[spec(pl.ANY)] * len(SAVED) + [spec(pltpu.VMEM)],
-        scratch_shapes=vmem(SAVED)
-        + vmem(big)
+        out_specs=[spec(pl.ANY)] * 17,
+        scratch_shapes=vmem(big)
+        + vmem(SAVED)
+        + vmem(wide)
+        + vmem([edge, edge, IDS, IDS])
         + [
             pltpu.VMEM((ROWS, HOP), F32),
             pltpu.VMEM((ROWS, 2), F32),
@@ -396,250 +500,24 @@
             pltpu.VMEM((ROWS, WIDE1), BF16),
             pltpu.VMEM((2 * ROWS, NFFT), BF16),
             pltpu.VMEM((4 * ROWS, NFFT // 2), BF16),
-            pltpu.SemaphoreType.DMA((len(big),)),
-            pltpu.SemaphoreType.DMA((len(SAVED),)),
-        ],
-        compiler_params=pltpu.CompilerParams(vmem_limit_bytes=60 * MB),
-        name="forward",
-    )(*small, *big)
-
-
-def stat_kernel(stat, out, slots, send, recv):
-    tm = lax.axis_index("tm")
-    barrier = pltpu.get_barrier_semaphore()
-    others = [lax.rem(tm + j, 8) for j in range(1, 8)]
-    for there in others:
-        pl.semaphore_signal(barrier, inc=1, device_id={"tm": there}, device_id_type=MESH)
-    pl.semaphore_wait(barrier, 7)
-    copies = []
-    for j, there in enumerate(others):
-        copies.append(
-            pltpu.make_async_remote_copy(
-                src_ref=stat,
-                dst_ref=slots.at[tm],
-                send_sem=send.at[j],
-                recv_sem=recv.at[j],
-                device_id={"tm": there},
-                device_id_type=MESH,
-            )
-        )
-    for copy in copies:
-        copy.start()
-    slots[tm] = stat[...]
-    for copy in copies:
-        copy.wait()
-    total = slots[0]
-    for j in range(1, 8):
-        total = total + slots[j]
-    out[...] = total
-
-
-def stat_call(stat):
-    return pl.pallas_call(
-        stat_kernel,
-        out_shape=full(8, 128),
-        in_specs=[spec(pltpu.VMEM)],
-        out_specs=spec(pltpu.VMEM),
-        scratch_shapes=[
+            pltpu.VMEM((8, 128), F32),
             pltpu.VMEM((8, 8, 128), F32),
-            pltpu.SemaphoreType.DMA((7,)),
-            pltpu.SemaphoreType.DMA((7,)),
-        ],
-        compiler_params=pltpu.CompilerParams(collective_id=1, has_side_effects=True),
-        name="clip_sums",
-    )(stat)
-
-
-def backward_kernel(kern, scale_i, win, stat, loss_scale, *refs):
-    count = len(SAVED)
-    saved_h, refs = refs[:count], refs[count:]
-    big_h, refs = refs[:9], refs[9:]
-    outs, refs = refs[:8], refs[8:]
-    saved, refs = refs[:count], refs[count:]
-    (sin_i, rstd_i, y1_i, gp_i, hid_i, down_i, y2_i, re_i, im_i, d1_i, q1_i, d2_i, q2_i) = saved
-    (a1_v, a2_v, syn_v, head_v, down_v, up_v, pick_n, pick_h, pick_k), refs = refs[:9], refs[9:]
-    (nrm_o, hid_o, onm_o, dup_o, ddn_o, dhd_o, dem_o, kg_o), refs = refs[:8], refs[8:]
-    kept = (nrm_o, hid_o, onm_o, dup_o, ddn_o, dhd_o, dem_o, kg_o)
-    dfr, dphase, dhead, dup, small, sems, saved_sems, out_sems = refs
-    loads = [
-        pltpu.make_async_copy(h, v, saved_sems.at[i]) for i, (h, v) in enumerate(zip(saved_h, saved))
-    ]
-    copies = [
-        pltpu.make_async_copy(h, v, sems.at[i])
-        for i, (h, v) in enumerate(
-            zip(big_h, (a1_v, a2_v, syn_v, head_v, down_v, up_v, pick_n, pick_h, pick_k))
-        )
-    ]
-    saves = [pltpu.make_async_copy(v, h, out_sems.at[i]) for i, (v, h) in enumerate(zip(kept, outs))]
-    for copy in (loads[9], loads[10], copies[0]):
-        copy.start()
-    scale = scale_i[...].reshape(1, D)
-    own = slice(HALO, HALO + OWN)
-    places = frame_places()
-    valid = inside(places)
-
-    factor = loss_scale[...] * (0.5 / CLIPS)
-    loss = jnp.zeros((1, 1), F32)
-    cots = []
-    for level in range(2):
-        count = ((FRAMES * 513), (2 * FRAMES * 257))[level]
-        sum_a = stat[3 * level : 3 * level + 1, 0:1]
-        sum_b = stat[3 * level + 1 : 3 * level + 2, 0:1]
-        sum_g = stat[3 * level + 2 : 3 * level + 3, 0:1]
-        root_a, root_b = jnp.sqrt(sum_a + 1e-6), jnp.sqrt(sum_b + 1e-6)
-        loss = loss + root_a / root_b + sum_g * (1.0 / count)
-        cots.append((factor / (root_a * root_b), factor * (1.0 / count)))
-    loss = jnp.where(lax.axis_index("tm") == 0, loss, 0.0)
-
-    dx = jnp.zeros((ROWS, HOP), F32)
-    loads[9].wait()
-    loads[10].wait()
-    copies[0].wait()
-    for copy in (loads[11], loads[12], copies[1], copies[2], loads[7], loads[8]):
-        copy.start()
-    ds1 = (cots[0][0] * d1_i[...] + cots[0][1] * q1_i[...]).astype(BF16)
-    for p in range(4):
-        at = slice(HOP * p, HOP * (p + 1))
-        piece = mm_bt(ds1, a1_v[at, :]).astype(BF16).astype(F32) * win[0:1, at]
-        dx = dx + shift(piece, p - 2)
-    loads[11].wait()
-    loads[12].wait()
-    copies[1].wait()
-    for copy in (copies[3], loads[1], loads[6], loads[5]):
-        copy.start()
-    ds2 = (cots[1][0] * d2_i[...] + cots[1][1] * q2_i[...]).astype(BF16)
-    dseg = mm_bt(ds2, a2_v[...]).astype(BF16).astype(F32) * win[2:3, : NFFT // 2]
-    even, odd = dseg[:ROWS], dseg[ROWS:]
-    dx = dx + shift(even[:, :256], -1) + even[:, 256:] + odd[:, 128:384]
-    dx = dx + jnp.concatenate([shift(odd[:, 384:], 1), shift(odd[:, :128], -1)], axis=1)
-    dx = jnp.where(valid, dx / envelope(places, win), 0.0)
-    for p in range(4):
-        piece = jnp.where(valid, shift(dx, 2 - p), 0.0)
-        dfr[:, HOP * p : HOP * (p + 1)] = piece.astype(BF16)
-
-    copies[2].wait()
-    loads[7].wait()
-    loads[8].wait()
-    copies[4].start()
-    loads[3].start()
-    for c in range(CHUNKS1):
-        dsp = mm_bt(dfr[...], syn_v[256 * c : 256 * (c + 1), :]).astype(BF16).astype(F32)
-        dre, dim = dsp[:, :128], dsp[:, 128:]
-        re, im = re_i[:, 128 * c : 128 * (c + 1)], im_i[:, 128 * c : 128 * (c + 1)]
-        dlog, dph = dre * re + dim * im, dim * re - dre * im
-        if c < 4:
-            dhead[:, 128 * c : 128 * (c + 1)] = dlog.astype(BF16)
-        dphase[:, 128 * c : 128 * (c + 1)] = dph
-    moved = pltpu.roll(dphase[...], 1, 1)
-    dhead[:, 512:640] = (moved[:, :128] + dlog).astype(BF16)
-    dhead[:, 640:] = moved[:, 128:].astype(BF16)
-    dhd_o[...] = dhead[own, :].astype(F32)
-    saves[5].start()
-    copies[3].wait()
-    for copy in (copies[5], loads[2], loads[0]):
-        copy.start()
-    don = mm(dhead[:, :1026], head_v[...]).astype(BF16).astype(F32)
-    for i in (1, 6, 5):
-        loads[i].wait()
-    dstream = norm_back(don, y2_i[...], rstd_i[:, 2:3])
-
-    scale_grad = jnp.sum(dstream[own] * down_i[own, :], axis=0, keepdims=True)
-    ddn = (scale * dstream).astype(BF16)
-    ddn_o[...] = ddn[own].astype(F32)
-    saves[4].start()
-    copies[4].wait()
-    loads[3].wait()
-    for copy in (copies[6], loads[4], copies[7], copies[8]):
-        copy.start()
-    for c in range(FF // 256):
-        at = slice(256 * c, 256 * (c + 1))
-        dh = mm_bt(ddn, down_v[at, :]).astype(BF16).astype(F32)
-        dup[:, at] = (dh * gp_i[:, at]).astype(BF16)
-    dup_o[...] = dup[own, :].astype(F32)
-    saves[3].start()
-    copies[5].wait()
-    loads[2].wait()
-    loads[0].wait()
-    dnorm = mm_bt(dup[...], up_v[...]).astype(BF16).astype(F32)
-    dmix = norm_back(dnorm, y1_i[...], rstd_i[:, 1:2])
-    dmix = jnp.where(valid, dmix, 0.0)
-    y0 = sin_i[...]
-    dsin = dstream
-    small[...] = jnp.zeros((128, D), F32)
-    for k in range(7):
-        dsin = dsin + kern[k : k + 1, :] * shift(dmix, k - 3)
-        taps = dmix * shift(y0, 3 - k)
-        small[2 + k : 3 + k, :] = jnp.sum(taps[own], axis=0, keepdims=True)
-    demb = norm_back(dsin, y0, rstd_i[:, 0:1])
-    dem_o[...] = demb[own].astype(BF16).astype(F32)
-    saves[6].start()
-
-    small[9:10, :] = scale_grad
-    rest = loss
-    for i, grid in enumerate((65536.0, 1.0, 1.0 / 65536.0, 1.0 / 65536.0 / 65536.0)):
-        piece = jnp.floor(rest * (1.0 / grid)) * grid
-        rest = rest - piece
-        small[10 + i : 11 + i, :] = jnp.broadcast_to(piece, (1, D))
-
-    for copy in (copies[6], copies[7], copies[8], loads[4]):
-        copy.wait()
-    normed = y1_i[own, :].astype(BF16)
-    onorm = y2_i[own, :].astype(BF16)
-    small0 = small[...].astype(BF16)
-    left = small[...] - small0.astype(F32)
-    small1 = left.astype(BF16)
-    small2 = (left - small1.astype(F32)).astype(BF16)
-    for c in range(2):
-        nrm_o[c] = mm(normed, pick_n[c])
-        onm_o[c] = mm(onorm, pick_n[c])
-        for h in range(2):
-            out = slice(576 * h, 576 * (h + 1))
-            hid_o[c, :, out] = mm(hid_i[:, 1152 * h : 1152 * (h + 1)], pick_h[c])
-        kg_o[c] = sum(
-            lax.dot_general(pick_k[c], s, (((0,), (1,)), ((), ())), preferred_element_type=F32)
-            for s in (small0, small1, small2)
-        )
-    for i in (0, 1, 2, 7):
-        saves[i].start()
-    for save in saves:
-        save.wait()
-
-
-def backward_call(small, saved, big):
-    outs = [
-        full(2, OWN, 384), full(2, OWN, 1152), full(2, OWN, 384), full(OWN, FF), full(OWN, D),
-        full(OWN, 1152), full(OWN, D), full(2, 384, 128),
-    ]
-    return pl.pallas_call(
-        backward_kernel,
-        out_shape=outs,
-        in_specs=[spec(pltpu.VMEM)] * len(small) + [spec(pl.ANY)] * (len(saved) + len(big)),
-        out_specs=[spec(pl.ANY)] * len(outs),
-        scratch_shapes=vmem(saved)
-        + vmem(big)
-        + vmem(outs)
-        + [
             pltpu.VMEM((ROWS, NFFT), BF16),
             pltpu.VMEM((ROWS, CHUNKS1 * 128), F32),
             pltpu.VMEM((ROWS, 1152), BF16),
             pltpu.VMEM((ROWS, FF), BF16),
             pltpu.VMEM((128, D), F32),
-            pltpu.SemaphoreType.DMA((len(big),)),
-            pltpu.SemaphoreType.DMA((len(saved),)),
-            pltpu.SemaphoreType.DMA((len(outs),)),
-        ],
-        compiler_params=pltpu.CompilerParams(vmem_limit_bytes=60 * MB),
-        name="backward",
-    )(*small, *saved, *big)
+        ]
+        + [pltpu.SemaphoreType.DMA((n,)) for n in (len(big), 4, 4, 7, 7, 9, 9, 8)],
+        compiler_params=pltpu.CompilerParams(
+            collective_id=0, has_side_effects=True, vmem_limit_bytes=60 * MB
+        ),
+        name="forward_backward",
+    )(*small, *big)
 
 
 LAST_ROWS = (120, 128, 120)
 FIRST_ROWS = (0, 120, 248)
-OPERANDS = (
-    full(OWN, 384), full(OWN, 1152), full(OWN, 384), full(OWN, FF), full(OWN, D),
-    full(OWN, 1152), full(OWN, D), full(384, 128), full(2, OWN, dtype=jnp.int32),
-)
-
 
 def put(out, first, values, rows):
     for block in range(values.shape[1] // 128):
@@ -653,16 +531,15 @@
 
 
 def scatter_kernel(*refs):
-    here_h, (turn1, turn2, row_id), out_o, scratch = refs[0:9], refs[9:12], refs[12], refs[13:]
+    ins, (turn1, turn2, row_id), out_o, scratch = refs[0:18], refs[18:21], refs[21], refs[22:]
     here, there = scratch[0:9], scratch[9:18]
     parts, through, from_left, from_right = (scratch[18 + 3 * i : 21 + 3 * i] for i in range(4))
     got2a, got2b, last, got3 = (scratch[30 + 3 * i : 33 + 3 * i] for i in range(4))
-    send, recv, pair_send, pair_recv, load = scratch[42:]
+    send, recv, load = scratch[42:]
 
     dp, tm = lax.axis_index("dp"), lax.axis_index("tm")
     at = {"x": tm // 2, "y": dp // 4, "z": lax.rem(dp // 2, 2) * 2 + lax.rem(tm, 2)}
     core = lax.rem(dp, 2)
-    partner = {"dp": dp + 1 - 2 * core, "tm": tm}
 
     def device(axis, by):
         to = dict(at)
@@ -673,34 +550,21 @@
         }
 
     barrier = pltpu.get_barrier_semaphore()
-    pl.semaphore_signal(barrier, inc=1, device_id=partner, device_id_type=MESH)
     for axis in "xyz":
         for by in (1, 2, 3):
             pl.semaphore_signal(barrier, inc=1, device_id=device(axis, by), device_id_type=MESH)
-    order = (0, 3, 2, 5, 1, 4, 8, 6, 7)
-    loads, pairs = {}, {}
-    for i in order:
-        picked = len(here_h[i].shape) == 3
-        loads[i] = pltpu.make_async_copy(
-            here_h[i].at[core] if picked else here_h[i], here[i], load.at[i]
-        )
-        pairs[i] = pltpu.make_async_remote_copy(
-            src_ref=here_h[i].at[1 - core] if picked else here_h[i],
-            dst_ref=there[i],
-            send_sem=pair_send.at[i],
-            recv_sem=pair_recv.at[i],
-            device_id=partner,
-            device_id_type=MESH,
-        )
+    loads = [
+        pltpu.make_async_copy(h, v, load.at[i])
+        for i, (h, v) in enumerate(zip(ins, (*here, *there)))
+    ]
+    for i in (0, 3, 2, 5, 1, 4, 8, 6, 7):
         loads[i].start()
-    pl.semaphore_wait(barrier, 10)
-    for i in order:
-        pairs[i].start()
+        loads[i + 9].start()
 
     def need(*which):
         for i in which:
             loads[i].wait()
-            pairs[i].wait_recv()
+            loads[i + 9].wait()
 
     def both(i, cols=slice(None)):
         return jnp.concatenate([here[i][:, cols], there[i][:, cols]], axis=0).astype(BF16)
@@ -752,6 +616,7 @@
     need(2, 5)
     onorm = both(2)
     head_part(0, 432, onorm)
+    pl.semaphore_wait(barrier, 9)
     phase1(0)
     need(1, 4)
     hidden = both(1)
@@ -836,8 +701,6 @@
             sent[k][j].wait_recv()
         total = last[k][at[ORDERS[k][2]]] + got3[k][0] + got3[k][1] + got3[k][2]
         out_o[pl.ds(FIRST_ROWS[k], LAST_ROWS[k]), :] = total
-    for i in order:
-        pairs[i].wait_send()
     for k in range(3):
         for copy in sent[k]:
             copy.wait_send()
@@ -852,10 +715,9 @@
     return pl.pallas_call(
         scatter_kernel,
         out_shape=full(sum(LAST_ROWS), 128),
-        in_specs=[spec(pl.ANY)] * 9 + [spec(pltpu.VMEM)] * 3,
+        in_specs=[spec(pl.ANY)] * 18 + [spec(pltpu.VMEM)] * 3,
         out_specs=spec(pltpu.VMEM),
-        scratch_shapes=vmem(OPERANDS)
-        + vmem(OPERANDS)
+        scratch_shapes=vmem([*OPERANDS, IDS]) * 2
         + each(lambda k: (4, 4, rows[k], 128))
         + each(lambda k: (2, 2, rows[k], 128))
         + each(lambda k: (4, rows[k], 128))
@@ -867,9 +729,7 @@
         + [
             pltpu.SemaphoreType.DMA((3, 15)),
             pltpu.SemaphoreType.DMA((3, 15)),
-            pltpu.SemaphoreType.DMA((9,)),
-            pltpu.SemaphoreType.DMA((9,)),
-            pltpu.SemaphoreType.DMA((9,)),
+            pltpu.SemaphoreType.DMA((18,)),
         ],
         compiler_params=pltpu.CompilerParams(
             collective_id=3, has_side_effects=True, vmem_limit_bytes=60 * MB
@@ -918,17 +778,14 @@
     pick_n, pick_h, pick_k, turn1, turn2, row_id = make_orders()
     ids = jnp.swapaxes(code_ids, 1, 2).reshape(2, OWN)
     head_t = head_weight.T
-    left_t, right_t, left_i, right_i = halo_call(target, ids)
-    *saved, stat = forward_call(
-        (target, left_t, right_t, ids, left_i, right_i, kernel, layer_scale, win),
-        (code_table, up_weight, down_weight, head_t, syn, a1, a2),
+    operands = step_call(
+        (target, ids, kernel, layer_scale, win, loss_scale.reshape(1, 1)),
+        (
+            code_table, up_weight, down_weight, head_t, syn, a1, a2, pick_n, pick_h, pick_k,
+        ),
     )
-    operands = backward_call(
-        (kernel, layer_scale, win, stat_call(stat), loss_scale.reshape(1, 1)),
-        saved,
-        (a1, a2, syn, head_t, down_weight, up_weight, pick_n, pick_h, pick_k),
-    )
-    return finish_call(scatter_call([*operands, ids], turn1, turn2, row_id))
+    operands = [*operands[:8], ids, *operands[8:]]
+    return finish_call(scatter_call(operands, turn1, turn2, row_id))
 
 
 def solution(mesh):

time: 118 us -> 96.4 us (0.82); the launches traced: 116 us -> 96.2 us
  Pallas kernels: 115 us -> 94.9 us
    pallas_call x4 -> x1, Pallas kernels: 46.6 us -> 32 us  [step_call(): pl.pallas_call(step_kernel, out_shape=[*OPERANDS, *OPERANDS, IDS], in_spe...]
    pallas_call x1, Pallas kernels: 66.8 us -> 61.3 us  [scatter_call(): pl.pallas_call(scatter_kernel, out_shape=full(sum(LAST_ROWS), 128), in_sp...]
where the time goes in v5:
time: 96.4 us; the launch traced here: 96.2 us
  Pallas kernels  94.9 us (98%)
  between operations  1.3 us (1%)
    pallas_call x1, Pallas kernels, scatter_call(): pl.pallas_call(scatter_kernel, out_shape=full(sum(LAST_ROWS), 128), in_sp...  61.3 us
    pallas_call x1, Pallas kernels, step_call(): pl.pallas_call(step_kernel, out_shape=[*OPERANDS, *OPERANDS, IDS], in_spe...  32 us

profile of v5, /device:TPU:0, one launch (start us, length us, event | category | flops | bytes accessed | tf_op | source)
XLA Modules:
  0.0 96.2 jit_solution(16341031922862215192)
XLA Ops:
  1.3 32.0 %forward_backward.1 = (f32[128,384]{1,0:T(8,128)}, f32[128,1152]{1,0:T(8,128)}, f32[128,384]{1,0:T(8,128)}, f32[128,2304]{1,0:T(8,128)}, f32[128,768]{1,0:T(8,12...) custom-call(f32[1,32768]{1,0:T(1,128)} %target.1, ...), custom_call_target="tpu_custom_call" | custom-call | tf_op jit(solution)/shard_map/forward_backward/pallas_call | solution.py:486
  33.3 61.3 %weight_grads_scatter.1.sums = f32[368,128]{1,0:T(8,128)} custom-call(f32[128,384]{1,0:T(8,128)} %get-tuple-element.31.refs_0_, f32[128,1152]{1,0:T(8,128)} %get-tuple-element.32.refs_1_, f32[128,384]{1,0:T(8,128)} %get-tuple-element.33.refs_2_, f32[128,2304]{1,0:T(8,128)} %get-tuple-element.34.refs_3_, f32[128,768]{1,0:T(8,128)} %get-tuple-element.35.refs_4_, ...), custom_call_target="tpu_custom_call" | custom-call | tf_op jit(solution)/shard_map/weight_grads_scatter/pallas_call | solution.py:715
  94.6 1.6 %finish.1 = (f32[1,1]{1,0:T(1,128)}, f32[16,768]{1,0:T(8,128)}, f32[7,6]{1,0:T(8,128)}, f32[6,2304]{1,0:T(8,128)}, f32[18,768]{1,0:T(8,128)}, /*index=5*/f32[1,6]{1,0:T(1,128)}, f32[6,1026]{1,0:T(8,128)}) custom-call(f32[368,128]{1,0:T(8,128)} %weight_grads_scatter.1.sums), custom_call_target="tpu_custom_call" | custom-call | tf_op jit(solution)/shard_map/finish/pallas_call | solution.py:762

commit v6 on v0

v6 whole, which is shorter than its diff:
```python
import jax
import jax.numpy as jnp
import ml_dtypes
import numpy as np
from jax import lax
from jax.experimental import pallas as pl
from jax.experimental.pallas import tpu as pltpu
from jax.sharding import PartitionSpec as P

F32, BF16 = jnp.float32, jnp.bfloat16
MESH = pl.DeviceIdType.MESH
D, FF = 768, 2304
HOP, NFFT = 256, 1024
FRAMES, OWN, HALO = 1024, 128, 16
ROWS = OWN + 2 * HALO
CHUNKS1, CHUNKS2 = 5, 3
WIDE1, WIDE2 = CHUNKS1 * 256, CHUNKS2 * 256
CLIPS = 16
MB = 1 << 20
ORDERS = ("xyz", "yzx", "zxy")
HEAD_BLOCKS = ((0, 3), (3, 2), (5, 4))
MAIN_BLOCKS = ((18, 24), (6, 72), (6, 64))
RANGES = (((0, 72), (72, 504)), ((0, 480),), ((0, 72), (72, 480)))
PART_ROWS = (504, 480, 480)
LAST_ROWS = (128, 120, 120)
FIRST_ROWS = (0, 128, 248)


def bf(array):
    return np.asarray(array, np.float32).astype(ml_dtypes.bfloat16)


def hann(length):
    return 0.5 - 0.5 * np.cos(2.0 * np.pi * np.arange(length) / length)


def angles(length):
    product = np.arange(length // 2 + 1)[:, None] * np.arange(length)[None, :] % length
    return 2.0 * np.pi * product / length


def interleave(real, imag, chunks):
    bins, width = real.shape
    out = np.zeros((chunks, 2, 128, width), np.float64)
    for half, part in enumerate((real, imag)):
        padded = np.zeros((chunks * 128, width), np.float64)
        padded[:bins] = part
        out[:, half] = padded.reshape(chunks, 128, width)
    return out.reshape(chunks * 256, width)


def make_constants():
    ang = angles(NFFT)
    bins = np.arange(NFFT // 2 + 1)
    factor = np.where((bins == 0) | (bins == NFFT // 2), 1.0, 2.0)[:, None] / NFFT
    window = hann(NFFT)[None, :]
    synthesis = bf(interleave(factor * np.cos(ang) * window, -factor * np.sin(ang) * window, CHUNKS1))
    analysis1 = bf(interleave(np.cos(ang), -np.sin(ang), CHUNKS1).T)
    ang = angles(NFFT // 2)
    analysis2 = bf(interleave(np.cos(ang), -np.sin(ang), CHUNKS2).T)
    win = np.zeros((8, NFFT), np.float32)
    win[0] = hann(NFFT)
    win[1] = hann(NFFT) ** 2
    win[2, : NFFT // 2] = hann(NFFT // 2)
    return synthesis, analysis1, analysis2, win


def device_index(x, y, z, core):
    return ((y * 2 + z // 2) * 2 + core) * 8 + x * 2 + z % 2


def shard_order(order, core):
    places = []
    for a in range(4):
        for b in range(4):
            for c in range(4):
                at = dict(zip(order, (a, b, c)))
                places.append(device_index(at["x"], at["y"], at["z"], core))
    return np.array(places)


def columns_of(order, core, each):
    return (shard_order(order, core)[:, None] * each + np.arange(each)[None, :]).reshape(-1)


def one_hot_columns(sources, size):
    out = np.zeros((size, sources.size), np.float32)
    out[sources, np.arange(sources.size)] = 1.0
    return bf(out)


def make_orders():
    pick_n = np.stack([one_hot_columns(columns_of(ORDERS[0], c, 6), D).T for c in (0, 1)])
    half = [columns_of(ORDERS[1], c, 18)[: 4 * 4 * 2 * 18] for c in (0, 1)]
    pick_h = np.stack([one_hot_columns(h, FF // 2).T for h in half])
    pick_k = np.stack([one_hot_columns(columns_of(ORDERS[2], c, 6), D).T for c in (0, 1)])
    first = columns_of(ORDERS[0], 0, 6)
    where = {col: i for i, col in enumerate(first)}
    turns = []
    for k in (1, 2):
        sources = np.array([where[col] for col in columns_of(ORDERS[k], 0, 6)])
        turns.append(one_hot_columns(sources, 384).T)
    row_id = columns_of(ORDERS[2], 0, 16).astype(np.int32)[:, None]
    return pick_n, pick_h, pick_k, turns[0], turns[1], row_id


def mm(a, b):
    return jnp.dot(a, b, preferred_element_type=F32)


def mm_bt(a, b):
    return lax.dot_general(a, b, (((1,), (1,)), ((), ())), preferred_element_type=F32)


def mm_at(a, b):
    return lax.dot_general(a, b, (((0,), (0,)), ((), ())), preferred_element_type=F32)


def shift(values, by):
    by = by % values.shape[0]
    return values if by == 0 else pltpu.roll(values, by, 0)


def norm(values):
    centre = values - jnp.mean(values, axis=-1, keepdims=True)
    rstd = lax.rsqrt(jnp.mean(centre * centre, axis=-1, keepdims=True) + 1e-6)
    return centre * rstd, rstd


def norm_back(grad, y, rstd):
    mean_g = jnp.mean(grad, axis=-1, keepdims=True)
    mean_gy = jnp.mean(grad * y, axis=-1, keepdims=True)
    return rstd * (grad - mean_g - y * mean_gy)


def frame_places():
    first = lax.axis_index("tm") * OWN - HALO
    return (lax.broadcasted_iota(jnp.int32, (ROWS, 1), 0) + first).astype(F32)


def sin_cos(x):
    turns = jnp.round(x * 0.6366197723675814)
    r = x - turns * 1.5703125
    r = r - turns * 4.837512969970703125e-4
    r = r - turns * 7.549789954891882e-8
    z = r * r
    sine = r + r * z * (-1.6666654611e-1 + z * (8.3321608736e-3 + z * -1.9515295891e-4))
    cosine = (4.166664568298827e-2 + z * (-1.388731625493765e-3 + z * 2.443315711809948e-5)) * (z * z)
    cosine = cosine - 0.5 * z + 1.0
    quarter = turns.astype(jnp.int32)
    odd = (quarter & 1) == 1
    first, second = jnp.where(odd, cosine, sine), jnp.where(odd, sine, cosine)
    first = jnp.where((quarter & 2) == 2, -first, first)
    second = jnp.where(((quarter + 1) & 2) == 2, -second, second)
    return first, second


def inside(places):
    return (places >= 0.0) & (places < float(FRAMES))


def envelope(places, win):
    total = jnp.zeros((ROWS, HOP), F32)
    for p in range(4):
        total = total + jnp.where(inside(places + float(2 - p)), win[1:2, HOP * p : HOP * (p + 1)], 0.0)
    return jnp.where(inside(places), total, 1.0)


def spec(space):
    return pl.BlockSpec(memory_space=space)


def full(*shape, dtype=F32):
    return jax.ShapeDtypeStruct(shape, dtype)


def ids_column(ids):
    padded = jnp.concatenate([ids.astype(F32), jnp.zeros((126, OWN), F32)], axis=0)
    return jnp.transpose(padded)[:, :2]


OPERANDS = (
    full(384, OWN), full(1152, OWN), full(384, OWN), full(OWN, FF), full(OWN, D),
    full(OWN, 1152), full(OWN, D), full(384, 128),
)
PICKED = (True, True, True, False, False, False, False, True)
IDS = full(2, OWN, dtype=jnp.int32)
SAVED = (
    full(ROWS, D), full(ROWS, 128), full(ROWS, D), full(ROWS, FF),
    full(ROWS, D), full(ROWS, D), full(ROWS, CHUNKS1 * 128), full(ROWS, CHUNKS1 * 128),
    full(ROWS, WIDE1), full(ROWS, WIDE1), full(2 * ROWS, WIDE2), full(2 * ROWS, WIDE2),
)


def vmem(shapes):
    return [pltpu.VMEM(a.shape, a.dtype) for a in shapes]


def put(out, first, values, rows):
    for block in range(values.shape[1] // 128):
        part = values[:, 128 * block : 128 * (block + 1)].reshape(4, 4, rows, 128)
        out[:, :, first + rows * block : first + rows * (block + 1), :] = part


def halves_of(rows):
    upper = (rows // 2 + 7) // 8 * 8
    return pl.ds(0, upper), pl.ds(upper, rows - upper)


def step_kernel(target, ids, kern, scale_i, win, loss_scale, turn1, turn2, row_id, *refs):
    big_h, out_o, refs = refs[:10], refs[10], refs[11:]
    (up_v, down_v, head_v, syn_v, a1_v, a2_v, pick_k), refs = refs[:7], refs[7:]
    (sin_o, rstd_o, y1_o, gp_o, down_o, y2_o, re_o, im_o, d1_o, q1_o, d2_o, q2_o) = refs[:12]
    refs = refs[12:]
    here, there, refs = refs[:8], refs[8:17], refs[17:]
    (nrm_o, hid_o, onm_o, dup_o, ddn_o, dhd_o, dem_o, kg_o) = here
    (left_t, right_t, left_i, right_i, hid_v, stat_o, slots), refs = refs[:7], refs[7:]
    (dfr, dphase, dhead, dup, small), refs = refs[:5], refs[5:]
    through, from_left, from_right, got2a, got2b, last, got3 = (
        refs[3 * i : 3 * i + 3] for i in range(7)
    )
    (
        sems, halo_send, halo_recv, stat_send, stat_recv, pair_send, pair_recv, send, recv,
    ) = refs[21:]

    dp, tm = lax.axis_index("dp"), lax.axis_index("tm")
    core = lax.rem(dp, 2)
    other = 1 - core
    partner = {"dp": dp + 1 - 2 * core, "tm": tm}
    others = [{"dp": dp, "tm": lax.rem(tm + j, 8)} for j in range(1, 8)]
    spot = {"x": tm // 2, "y": dp // 4, "z": lax.rem(dp // 2, 2) * 2 + lax.rem(tm, 2)}

    def device(axis, by):
        to = dict(spot)
        to[axis] = lax.rem(spot[axis] + by, 4)
        return {
            "dp": (to["y"] * 2 + to["z"] // 2) * 2 + core,
            "tm": to["x"] * 2 + lax.rem(to["z"], 2),
        }

    barrier = pltpu.get_barrier_semaphore()
    around_me = [device(axis, by) for axis in "xyz" for by in (1, 2, 3)]
    for place in others + [partner] + around_me:
        pl.semaphore_signal(barrier, inc=1, device_id=place, device_id_type=MESH)

    def remote(src, dst, send, recv, place):
        return pltpu.make_async_remote_copy(
            src_ref=src, dst_ref=dst, send_sem=send, recv_sem=recv,
            device_id=place, device_id_type=MESH,
        )

    edge = HALO * HOP
    right, left = others[0], others[6]
    halo = [
        remote(src, dst, halo_send.at[i], halo_recv.at[i], place)
        for i, (src, dst, place) in enumerate(
            (
                (ids, left_i, right),
                (ids, right_i, left),
                (target.at[:, pl.ds(OWN * HOP - edge, edge)], left_t, right),
                (target.at[:, pl.ds(0, edge)], right_t, left),
            )
        )
    ]
    shares = [
        remote(stat_o, slots.at[tm], stat_send.at[j], stat_recv.at[j], place)
        for j, place in enumerate(others)
    ]
    pairs = [
        remote(ref.at[other] if picked else ref, there[i], pair_send.at[i], pair_recv.at[i], partner)
        for i, (ref, picked) in enumerate(zip((*here, ids), (*PICKED, False)))
    ]

    def give(i):
        pairs[i].start()

    own = slice(HALO, HALO + OWN)
    scale = scale_i[...].reshape(1, D)
    places = frame_places()
    valid = inside(places)

    def forward(table_v, pick_n, pick_h, goal, codes, head_s, spec_v, seg1, seg2):
        big_v = (table_v, up_v, down_v, head_v, syn_v, a1_v, a2_v, pick_n, pick_h, pick_k)
        copies = [
            pltpu.make_async_copy(h, v, sems.at[i]) for i, (h, v) in enumerate(zip(big_h, big_v))
        ]
        for copy in copies:
            copy.start()
        pl.semaphore_wait(barrier, 17)
        for copy in halo:
            copy.start()
        give(8)
        codes[HALO : HALO + OWN, :] = ids_column(ids[...])
        for source, first, count in (
            (target, HALO, OWN), (left_t, 0, HALO), (right_t, HALO + OWN, HALO),
        ):
            if source is left_t:
                for copy in halo:
                    copy.wait_recv()
            for r in range(count):
                goal[first + r : first + r + 1, :] = source[:, HOP * r : HOP * (r + 1)]
        codes[0:HALO, :] = ids_column(left_i[...])[OWN - HALO :]
        codes[HALO + OWN :, :] = ids_column(right_i[...])[:HALO]
        lane = lax.broadcasted_iota(jnp.int32, (ROWS, 2 * FRAMES), 1).astype(F32)
        hot = (lane == codes[:, 0:1]) | (lane == codes[:, 1:2] + 1024.0)
        hot = jnp.where(hot, 1.0, 0.0).astype(BF16)
        copies[0].wait()
        y0, rstd0 = norm(mm(hot, table_v[...]))
        y0 = jnp.where(valid, y0, 0.0)
        sin_o[...] = y0
        mixture = kern[0:1, :] * shift(y0, 3)
        for k in range(1, 7):
            mixture = mixture + kern[k : k + 1, :] * shift(y0, 3 - k)
        y1, rstd1 = norm(mixture)
        y1_o[...] = y1
        normed = y1.astype(BF16)
        copies[1].wait()
        for c in range(FF // 256):
            at = slice(256 * c, 256 * (c + 1))
            up = mm(normed, up_v[:, at])
            cdf = 0.5 * (1.0 + lax.erf(up * 0.7071067811865476))
            hid_v[:, at] = (up * cdf).astype(BF16)
            gp_o[:, at] = cdf + up * (0.3989422804014327 * jnp.exp(-0.5 * up * up))
        copies[2].wait()
        down = mm(hid_v[...], down_v[...])
        down_o[...] = down
        y2, rstd2 = norm(y0 + scale * down)
        y2_o[...] = y2
        places128 = lax.broadcasted_iota(jnp.int32, (ROWS, 128), 1)
        rstd_o[...] = jnp.where(places128 == 0, rstd0, jnp.where(places128 == 1, rstd1, rstd2))
        onorm = y2.astype(BF16)
        copies[3].wait()
        head_s[:, 1024:] = jnp.zeros((ROWS, 128), F32)
        for c in range(4):
            head_s[:, 256 * c : 256 * (c + 1)] = mm_bt(onorm, head_v[256 * c : 256 * (c + 1), :])
        head_s[:, 1024:1026] = mm_bt(onorm, head_v[1024:1026, :])
        phases = pltpu.roll(head_s[:, 512:], CHUNKS1 * 128 - 1, 1)
        for c in range(CHUNKS1):
            logmag = head_s[:, 128 * c : 128 * (c + 1)]
            if c == 4:
                logmag = jnp.where(places128 == 0, logmag, 0.0)
            mag = jnp.exp(logmag)
            phase = phases[:, 128 * c : 128 * (c + 1)]
            sine, cosine = sin_cos(phase)
            re, im = mag * cosine, mag * sine
            re_o[:, 128 * c : 128 * (c + 1)] = re
            im_o[:, 128 * c : 128 * (c + 1)] = im
            spec_v[:, 256 * c : 256 * c + 128] = re.astype(BF16)
            spec_v[:, 256 * c + 128 : 256 * (c + 1)] = im.astype(BF16)
        copies[4].wait()
        pred = jnp.zeros((ROWS, HOP), F32)
        for p in range(4):
            piece = jnp.where(valid, mm(spec_v[...], syn_v[:, HOP * p : HOP * (p + 1)]), 0.0)
            pred = pred + shift(piece, p - 2)
        pred = jnp.where(valid, pred / envelope(places, win), 0.0)
        for s, x in enumerate((pred, jnp.where(valid, goal[...], 0.0))):
            r1 = slice(ROWS * s, ROWS * (s + 1))
            for p in range(4):
                at = slice(HOP * p, HOP * (p + 1))
                seg1[r1, at] = (shift(x, 2 - p) * win[0:1, at]).astype(BF16)
            even = slice(2 * ROWS * s, 2 * ROWS * s + ROWS)
            odd = slice(2 * ROWS * s + ROWS, 2 * ROWS * (s + 1))
            before, after = shift(x, 1), shift(x, -1)
            seg2[even, 0:256] = (before * win[2:3, 0:256]).astype(BF16)
            seg2[even, 256:512] = (x * win[2:3, 256:512]).astype(BF16)
            seg2[odd, 0:128] = (before[:, 128:] * win[2:3, 0:128]).astype(BF16)
            seg2[odd, 128:384] = (x * win[2:3, 128:384]).astype(BF16)
            seg2[odd, 384:512] = (after[:, :128] * win[2:3, 384:512]).astype(BF16)
        for level in range(2):
            seg, table, chunks = ((seg1, a1_v, CHUNKS1), (seg2, a2_v, CHUNKS2))[level]
            d_o, q_o = ((d1_o, q1_o), (d2_o, q2_o))[level]
            copies[5 + level].wait()
            sums = [jnp.zeros((OWN, 128), F32) for _ in range(3)]
            for c in range(chunks):
                for sub in range(level + 1):
                    rows_p = slice(ROWS * sub, ROWS * (sub + 1))
                    base = ROWS * (level + 1)
                    rows_g = slice(base + ROWS * sub, base + ROWS * (sub + 1))
                    weights = table[:, 256 * c : 256 * (c + 1)]
                    sp, sg = mm(seg[rows_p, :], weights), mm(seg[rows_g, :], weights)
                    diff = sp - sg
                    pr, pi, gr, gi = sp[:, :128], sp[:, 128:], sg[:, :128], sg[:, 128:]
                    power_p, power_g = pr * pr + pi * pi, gr * gr + gi * gi
                    gap = jnp.log1p(power_p) - jnp.log1p(power_g)
                    slope = jnp.where(valid, 4.0 * gap / (1.0 + power_p), 0.0)
                    d_o[rows_p, 256 * c : 256 * (c + 1)] = jnp.where(valid, diff, 0.0)
                    q_o[rows_p, 256 * c : 256 * c + 128] = slope * pr
                    q_o[rows_p, 256 * c + 128 : 256 * (c + 1)] = slope * pi
                    dr, di = diff[own, :128], diff[own, 128:]
                    sums[0] = sums[0] + dr * dr + di * di
                    sums[1] = sums[1] + power_g[own]
                    sums[2] = sums[2] + gap[own] * gap[own]
            for i in range(3):
                total = jnp.sum(jnp.sum(sums[i], axis=0, keepdims=True), axis=1, keepdims=True)
                stat_o[3 * level + i : 3 * level + i + 1, :] = jnp.broadcast_to(total, (1, 128))
        stat_o[6:8, :] = jnp.zeros((2, 128), F32)
        for share in shares:
            share.start()
        slots[tm] = stat_o[...]

        copies[7].wait()
        copies[8].wait()
        normed = y1_o[own, :].astype(BF16)
        onorm = y2_o[own, :].astype(BF16)
        for c in range(2):
            nrm_o[c] = mm_bt(pick_n[c], normed)
            onm_o[c] = mm_bt(pick_n[c], onorm)
            for h in range(2):
                out = slice(576 * h, 576 * (h + 1))
                hid_o[c, out, :] = mm_bt(pick_h[c], hid_v[own, 1152 * h : 1152 * (h + 1)])
        for i in (0, 2, 1):
            give(i)
        copies[9].wait()

    pl.run_scoped(
        forward,
        *vmem([full(*shape, dtype=BF16) for shape in (BIG[0], BIG[7], BIG[8])]),
        pltpu.VMEM((ROWS, HOP), F32),
        pltpu.VMEM((ROWS, 2), F32),
        pltpu.VMEM((ROWS, 1152), F32),
        pltpu.VMEM((ROWS, WIDE1), BF16),
        pltpu.VMEM((2 * ROWS, NFFT), BF16),
        pltpu.VMEM((4 * ROWS, NFFT // 2), BF16),
    )

    def need(*which):
        for i in which:
            pairs[i].wait_recv()

    def lhs(i):
        return jnp.concatenate([here[i][core], there[i][...]], axis=1).astype(BF16)

    def rhs(i, cols):
        return jnp.concatenate([here[i][:, cols], there[i][:, cols]], axis=0).astype(BF16)

    def head_block(onorm, block):
        return mm(onorm, rhs(5, slice(128 * block, 128 * (block + 1))))

    def around(axis):
        i = spot[axis]
        return i, lax.rem(i + 1, 4), lax.rem(i + 2, 4), lax.rem(i + 3, 4)

    def backward(*parts):
        sent = [{}, {}, {}]

        def go(src, dst, k, slot, axis, by):
            sent[k][slot] = remote(src, dst, send.at[k, slot], recv.at[k, slot], device(axis, by))
            sent[k][slot].start()

        low, high = pl.ds(0, 2), pl.ds(2, 2)

        def phase1(k, s):
            axis, p = ORDERS[k][0], parts[k]
            i, right, opposite, left = around(axis)
            first, end = RANGES[k][s]
            rows = pl.ds(first, end - first)
            go(p.at[opposite, low, rows], through[k].at[0, :, rows], k, 6 * s, axis, 1)
            go(p.at[opposite, high, rows], through[k].at[1, :, rows], k, 6 * s + 1, axis, 3)
            go(p.at[right, high, rows], from_left[k].at[high, rows], k, 6 * s + 2, axis, 1)
            go(p.at[left, low, rows], from_right[k].at[low, rows], k, 6 * s + 3, axis, 3)

        def combine(k, s):
            axis, p = ORDERS[k][0], parts[k]
            i, right, opposite, left = around(axis)
            first, end = RANGES[k][s]
            rows = pl.ds(first, end - first)
            sent[k][6 * s].wait_recv()
            p[right, low, rows] += through[k][0, :, rows]
            go(p.at[right, low, rows], from_left[k].at[low, rows], k, 6 * s + 4, axis, 1)
            sent[k][6 * s + 1].wait_recv()
            p[left, high, rows] += through[k][1, :, rows]
            go(p.at[left, high, rows], from_right[k].at[high, rows], k, 6 * s + 5, axis, 3)

        for share in shares:
            share.wait_recv()
        total = slots[0]
        for j in range(1, 8):
            total = total + slots[j]

        factor = loss_scale[...] * (0.5 / CLIPS)
        loss = jnp.zeros((1, 1), F32)
        cots = []
        for level in range(2):
            count = ((FRAMES * 513), (2 * FRAMES * 257))[level]
            sum_a = total[3 * level : 3 * level + 1, 0:1]
            sum_b = total[3 * level + 1 : 3 * level + 2, 0:1]
            sum_g = total[3 * level + 2 : 3 * level + 3, 0:1]
            root_a, root_b = jnp.sqrt(sum_a + 1e-6), jnp.sqrt(sum_b + 1e-6)
            loss = loss + root_a / root_b + sum_g * (1.0 / count)
            cots.append((factor / (root_a * root_b), factor * (1.0 / count)))
        loss = jnp.where(lax.axis_index("tm") == 0, loss, 0.0)

        dx = jnp.zeros((ROWS, HOP), F32)
        ds1 = (cots[0][0] * d1_o[...] + cots[0][1] * q1_o[...]).astype(BF16)
        for p in range(4):
            at = slice(HOP * p, HOP * (p + 1))
            piece = mm_bt(ds1, a1_v[at, :]).astype(BF16).astype(F32) * win[0:1, at]
            dx = dx + shift(piece, p - 2)
        ds2 = (cots[1][0] * d2_o[...] + cots[1][1] * q2_o[...]).astype(BF16)
        dseg = mm_bt(ds2, a2_v[...]).astype(BF16).astype(F32) * win[2:3, : NFFT // 2]
        even, odd = dseg[:ROWS], dseg[ROWS:]
        dx = dx + shift(even[:, :256], -1) + even[:, 256:] + odd[:, 128:384]
        dx = dx + jnp.concatenate([shift(odd[:, 384:], 1), shift(odd[:, :128], -1)], axis=1)
        dx = jnp.where(valid, dx / envelope(places, win), 0.0)
        for p in range(4):
            piece = jnp.where(valid, shift(dx, 2 - p), 0.0)
            dfr[:, HOP * p : HOP * (p + 1)] = piece.astype(BF16)

        for c in range(CHUNKS1):
            dsp = mm_bt(dfr[...], syn_v[256 * c : 256 * (c + 1), :]).astype(BF16).astype(F32)
            dre, dim = dsp[:, :128], dsp[:, 128:]
            re, im = re_o[:, 128 * c : 128 * (c + 1)], im_o[:, 128 * c : 128 * (c + 1)]
            dlog, dph = dre * re + dim * im, dim * re - dre * im
            if c < 4:
                dhead[:, 128 * c : 128 * (c + 1)] = dlog.astype(BF16)
            dphase[:, 128 * c : 128 * (c + 1)] = dph
        moved = pltpu.roll(dphase[...], 1, 1)
        dhead[:, 512:640] = (moved[:, :128] + dlog).astype(BF16)
        dhead[:, 640:] = moved[:, 128:].astype(BF16)
        dhd_o[...] = dhead[own, :].astype(F32)
        give(5)
        don = mm(dhead[:, :1026], head_v[...]).astype(BF16).astype(F32)
        dstream = norm_back(don, y2_o[...], rstd_o[:, 2:3])

        scale_grad = jnp.sum(dstream[own] * down_o[own, :], axis=0, keepdims=True)
        ddn = (scale * dstream).astype(BF16)
        ddn_o[...] = ddn[own].astype(F32)
        give(4)
        for c in range(FF // 256):
            at = slice(256 * c, 256 * (c + 1))
            dh = mm_bt(ddn, down_v[at, :]).astype(BF16).astype(F32)
            dup[:, at] = (dh * gp_o[:, at]).astype(BF16)
        dup_o[...] = dup[own, :].astype(F32)
        give(3)

        need(2, 5)
        onorm = [lhs(2)]
        onorm += [mm(turn[...], onorm[0]).astype(BF16) for turn in (turn1, turn2)]
        for k in range(3):
            start, blocks = HEAD_BLOCKS[k]
            for b in range(min(blocks, 8 - start)):
                put(parts[k], 24 * b, head_block(onorm[k], start + b), 24)
        phase1(0, 0)
        phase1(2, 0)
        need(1, 4)
        hidden = lhs(1)
        for c in range(3):
            put(parts[1], 48 + 144 * c, mm(hidden, rhs(4, slice(256 * c, 256 * (c + 1)))), 72)
        phase1(1, 0)

        dnorm = mm_bt(dup[...], up_v[...]).astype(BF16).astype(F32)
        dmix = norm_back(dnorm, y1_o[...], rstd_o[:, 1:2])
        dmix = jnp.where(valid, dmix, 0.0)
        y0 = sin_o[...]
        dsin = dstream
        small[...] = jnp.zeros((128, D), F32)
        for k in range(7):
            dsin = dsin + kern[k : k + 1, :] * shift(dmix, k - 3)
            taps = dmix * shift(y0, 3 - k)
            small[2 + k : 3 + k, :] = jnp.sum(taps[own], axis=0, keepdims=True)
        demb = norm_back(dsin, y0, rstd_o[:, 0:1])
        dem_o[...] = demb[own].astype(BF16).astype(F32)
        give(6)

        small[9:10, :] = scale_grad
        rest = loss
        for i, grid in enumerate((65536.0, 1.0, 1.0 / 65536.0, 1.0 / 65536.0 / 65536.0)):
            piece = jnp.floor(rest * (1.0 / grid)) * grid
            rest = rest - piece
            small[10 + i : 11 + i, :] = jnp.broadcast_to(piece, (1, D))

        small0 = small[...].astype(BF16)
        rest = small[...] - small0.astype(F32)
        small1 = rest.astype(BF16)
        small2 = (rest - small1.astype(F32)).astype(BF16)
        for c in range(2):
            kg_o[c] = sum(mm_bt(pick_k[c], part) for part in (small0, small1, small2))
        give(7)

        combine(0, 0)
        combine(2, 0)
        need(0, 3)
        normed = lhs(0)
        for c in range(FF // 256):
            put(parts[0], 72 + 48 * c, mm(normed, rhs(3, slice(256 * c, 256 * (c + 1)))), 24)
        phase1(0, 1)
        need(8, 6, 7)
        put(parts[2], 72, head_block(onorm[2], 8) + here[7][core] + there[7][...], 24)
        both_ids = jnp.concatenate([ids[...], there[8][...]], axis=1)
        code_rows = row_id[...] + OWN * core
        hot = (code_rows == both_ids[0:1, :]) | (code_rows == both_ids[1:2, :] + 1024)
        hot = jnp.where(hot, 1.0, 0.0).astype(BF16)
        for c in range(3):
            put(parts[2], 96 + 128 * c, mm(hot, rhs(6, slice(256 * c, 256 * (c + 1)))), 64)
        phase1(2, 1)
        combine(1, 0)
        combine(0, 1)
        combine(2, 1)

        for k in (1, 0, 2):
            mine = spot[ORDERS[k][0]]
            axis, p, a, b = ORDERS[k][1], parts[k], got2a[k], got2b[k]
            i, right, opposite, left = around(axis)
            upper, lower = halves_of(PART_ROWS[k])
            for s in range(len(RANGES[k])):
                for j in (2, 3, 4, 5):
                    sent[k][6 * s + j].wait_recv()
            p[mine, opposite] += from_left[k][opposite] + from_right[k][opposite]
            go(p.at[mine, opposite, upper], a.at[0], k, 12, axis, 1)
            go(p.at[mine, opposite, lower], b.at[0], k, 13, axis, 3)
            p[mine, right] += from_left[k][right] + from_right[k][right]
            go(p.at[mine, right, lower], b.at[1], k, 14, axis, 1)
            p[mine, left] += from_left[k][left] + from_right[k][left]
            go(p.at[mine, left, upper], a.at[1], k, 15, axis, 3)
            p[mine, i] += from_left[k][i] + from_right[k][i]
        for k in (1, 0, 2):
            mine = spot[ORDERS[k][0]]
            axis, p, a, b = ORDERS[k][1], parts[k], got2a[k], got2b[k]
            i, right, opposite, left = around(axis)
            upper, lower = halves_of(PART_ROWS[k])
            sent[k][12].wait_recv()
            p[mine, right, upper] += a[0]
            go(p.at[mine, right, upper], a.at[2], k, 16, axis, 1)
            sent[k][13].wait_recv()
            p[mine, left, lower] += b[0]
            go(p.at[mine, left, lower], b.at[2], k, 17, axis, 3)
        for k in (1, 0, 2):
            mine = spot[ORDERS[k][0]]
            i = spot[ORDERS[k][1]]
            p, a, b, out = parts[k], got2a[k], got2b[k], last[k]
            upper, lower = halves_of(PART_ROWS[k])
            for j in (14, 15, 16, 17):
                sent[k][j].wait_recv()
            p[mine, i, upper] += a[1] + a[2]
            p[mine, i, lower] += b[1] + b[2]
            start, place = 0, 0
            for count, rows in ((HEAD_BLOCKS[k][1], 24), MAIN_BLOCKS[k]):
                each = rows // 4
                for _ in range(count):
                    for d in range(4):
                        out[d, pl.ds(place, each)] = p[mine, i, pl.ds(start + d * each, each)]
                    start += rows
                    place += each
            if place < LAST_ROWS[k]:
                for d in range(4):
                    out[d, pl.ds(place, LAST_ROWS[k] - place)] = jnp.zeros(
                        (LAST_ROWS[k] - place, 128), F32
                    )
            axis = ORDERS[k][2]
            for by in (1, 2, 3):
                to = lax.rem(spot[axis] + by, 4)
                go(out.at[to], got3[k].at[by - 1], k, 17 + by, axis, by)
        for k in (1, 0, 2):
            for j in (18, 19, 20):
                sent[k][j].wait_recv()
            total = last[k][spot[ORDERS[k][2]]] + got3[k][0] + got3[k][1] + got3[k][2]
            out_o[pl.ds(FIRST_ROWS[k], LAST_ROWS[k]), :] = total
        for copy in halo + shares + pairs:
            copy.wait_send()
        for k in range(3):
            for copy in sent[k].values():
                copy.wait_send()

    pl.run_scoped(backward, *[pltpu.VMEM((4, 4, n, 128), F32) for n in PART_ROWS])


BIG = (
    (2 * FRAMES, D), (D, FF), (FF, D), (2 * 513, D), (WIDE1, NFFT), (NFFT, WIDE1),
    (NFFT // 2, WIDE2), (2, 384, D), (2, 576, FF // 2), (2, 384, D),
)


def step_call(small, big):
    wide = [full(*((2,) if p else ()), *a.shape) for a, p in zip(OPERANDS, PICKED)]
    edge = full(1, HALO * HOP)
    rows = PART_ROWS
    cuts = [halves_of(n)[0].size for n in rows]

    def each(make):
        return [pltpu.VMEM(make(k), F32) for k in range(3)]

    return pl.pallas_call(
        step_kernel,
        out_shape=full(sum(LAST_ROWS), 128),
        in_specs=[spec(pltpu.VMEM)] * len(small) + [spec(pl.ANY)] * len(big),
        out_specs=spec(pltpu.VMEM),
        scratch_shapes=vmem([full(*BIG[i], dtype=BF16) for i in (1, 2, 3, 4, 5, 6, 9)])
        + vmem(SAVED)
        + vmem(wide)
        + vmem([*OPERANDS, IDS])
        + vmem([edge, edge, IDS, IDS])
        + [
            pltpu.VMEM((ROWS, FF), BF16),
            pltpu.VMEM((8, 128), F32),
            pltpu.VMEM((8, 8, 128), F32),
            pltpu.VMEM((ROWS, NFFT), BF16),
            pltpu.VMEM((ROWS, CHUNKS1 * 128), F32),
            pltpu.VMEM((ROWS, 1152), BF16),
            pltpu.VMEM((ROWS, FF), BF16),
            pltpu.VMEM((128, D), F32),
        ]
        + each(lambda k: (2, 2, rows[k], 128))
        + each(lambda k: (4, rows[k], 128))
        + each(lambda k: (4, rows[k], 128))
        + each(lambda k: (3, cuts[k], 128))
        + each(lambda k: (3, rows[k] - cuts[k], 128))
        + each(lambda k: (4, LAST_ROWS[k], 128))
        + each(lambda k: (3, LAST_ROWS[k], 128))
        + [pltpu.SemaphoreType.DMA((n,)) for n in (len(big), 4, 4, 7, 7, 9, 9)]
        + [pltpu.SemaphoreType.DMA((3, 21))] * 2,
        compiler_params=pltpu.CompilerParams(
            collective_id=0, has_side_effects=True, vmem_limit_bytes=64 * MB
        ),
        name="train_step",
    )(*small, *big)


def finish_kernel(sums, loss_o, table_o, kern_o, up_o, down_o, scale_o, head_o):
    for k, (out, count, each) in enumerate(((up_o, 18, 6), (down_o, 6, 18), (table_o, 6, 16))):
        start, blocks = HEAD_BLOCKS[k]
        for c in range(blocks):
            rows = FIRST_ROWS[k] + 6 * c
            values = sums[rows : rows + 6, :]
            if start + c < 8:
                head_o[:, 128 * (start + c) : 128 * (start + c + 1)] = values
            else:
                head_o[:, 1024:1026] = values[:, 0:2]
                tail = jnp.transpose(jnp.concatenate([values, jnp.zeros((122, 128), F32)], axis=0))
                kern_o[...] = tail[2:9, 0:6]
                scale_o[...] = tail[9:10, 0:6]
                pieces = values[0:1, 10:14]
                loss_o[...] = jnp.sum(pieces, axis=1, keepdims=True) * (0.5 / CLIPS)
        for c in range(count):
            rows = FIRST_ROWS[k] + 6 * blocks + each * c
            out[:, 128 * c : 128 * (c + 1)] = sums[rows : rows + each, :]


def finish_call(sums):
    loss, table, kern, up, down, scale, head = pl.pallas_call(
        finish_kernel,
        out_shape=[
            full(1, 1), full(16, D), full(7, 6), full(6, FF), full(18, D), full(1, 6), full(6, 1026),
        ],
        in_specs=[spec(pltpu.VMEM)],
        out_specs=[spec(pltpu.VMEM)] * 7,
        name="finish",
    )(sums)
    return loss.reshape(()), table, kern, up, down, scale.reshape(6), head


def body(
    code_ids, code_table, kernel, up_weight, down_weight, layer_scale, head_weight, target, loss_scale
):
    syn, a1, a2, win = make_constants()
    pick_n, pick_h, pick_k, turn1, turn2, row_id = make_orders()
    ids = jnp.swapaxes(code_ids, 1, 2).reshape(2, OWN)
    head_t = head_weight.T
    sums = step_call(
        (target, ids, kernel, layer_scale, win, loss_scale.reshape(1, 1), turn1, turn2, row_id),
        (
            code_table, up_weight, down_weight, head_t, syn, a1, a2, pick_n, pick_h, pick_k,
        ),
    )
    return finish_call(sums)


def solution(mesh):
    in_specs = (P("dp", "tm", None), P(), P(), P(), P(), P(), P(), P("dp", "tm"), P())
    out_specs = (
        P(),
        P(("dp", "tm"), None),
        P(None, ("dp", "tm")),
        P(("dp", "tm"), None),
        P(("dp", "tm"), None),
        P(("dp", "tm")),
        P(("dp", "tm"), None),
    )
    return jax.shard_map(body, mesh=mesh, in_specs=in_specs, out_specs=out_specs, check_vma=False)
```

time: 1200 us -> 87.4 us (0.07); the launches traced: 1180 us -> 87.3 us
  blocking collectives: 619 us -> 0 us
  starting transfers between devices: 248 us -> 0 us
  local copies, waits for them, and re-layouts: 146 us -> 0 us
  other arithmetic: 86.7 us -> 0 us
  Pallas kernels: 0 us -> 86 us
  matrix products: 45.4 us -> 0 us
  between operations: 22.3 us -> 1.29 us
  waiting for transfers between devices: 14.5 us -> 0 us
    unnamed x2 -> x0, blocking collectives: 565 us -> none
    unnamed x65 -> x0, starting transfers between devices: 215 us -> none
    unnamed x190 -> x0, local copies, waits for them, and re-layouts: 119 us -> none
    pallas_call x0 -> x2, Pallas kernels: none -> 86 us  [the longest x1 84.4 us: step_call(): pl.pallas_call(step_kernel, out_shape=full(sum(LAST_ROWS), 128), in_specs...]
    psum x2 -> x0, blocking collectives: 54 us -> none  [the longest x1 34.4 us: body(): lax.psum(jnp.sum(per_clip_loss(clip_stats, frame_total)), 'dp')]
    dot_general x19 -> x0, matrix products: 45.4 us -> none  [the longest x4 15.5 us: weight_grad(): return jnp.dot(left_side.T, right_side, preferred_element_type=jnp.float32)]
    div x12 -> x0, other arithmetic: 34.5 us -> none  [the longest x1 17 us: body(): add_ends(outputs[1], rim_ext[:, :half_frame], rim_ext[:, -half_frame:])]
    ppermute x12 -> x0, starting transfers between devices: 33 us -> none  [the longest x6 24.9 us: extended_2(): lax.ppermute(lax.slice_in_dim(block, block.shape[dim] - width, None, axis...]
  transfers between devices with their start and end apart: 78 -> 0, of which waited for: 5 -> 0; matrix products, arithmetic and copies ran while one was open for 56% -> 0% of each run, Pallas kernels for 0% -> 0%
where the time goes in v6:
time: 87.4 us; the launch traced here: 87.3 us
  Pallas kernels  86 us (98%)
  between operations  1.29 us (1%)
    pallas_call x1, Pallas kernels, step_call(): pl.pallas_call(step_kernel, out_shape=full(sum(LAST_ROWS), 128), in_specs...  84.4 us

profile of v6, /device:TPU:0, one launch (start us, length us, event | category | flops | bytes accessed | tf_op | source)
XLA Modules:
  0.0 87.3 jit_solution(14023144686981905066)
XLA Ops:
  1.3 84.4 %train_step.1.sums = f32[368,128]{1,0:T(8,128)} custom-call(f32[1,32768]{1,0:T(1,128)} %target.1, s32[2,128]{1,0:T(2,128)} %bitcast.9, f32[7,768]{1,0:T(8,128)} %kern.1, f32[768]{0:T(1024)} %scale_i.1, f32[8,1024]{1,0:T(8,128)} %constant.20.clone.win, f32[1,1]{1,0:T(1,128)} %bitcast.7.loss_scale, bf16[384,384]{1,0:T(8,128)(2,1)} %constant.21.clone.turn1, ...), custom_call_target="tpu_custom_call" | custom-call | tf_op jit(solution)/shard_map/train_step/pallas_call | solution.py:682
  85.7 1.6 %finish.1 = (f32[1,1]{1,0:T(1,128)}, f32[16,768]{1,0:T(8,128)}, f32[7,6]{1,0:T(8,128)}, f32[6,2304]{1,0:T(8,128)}, f32[18,768]{1,0:T(8,128)}, /*index=5*/f32[1,6]{1,0:T(1,128)}, f32[6,1026]{1,0:T(8,128)}) custom-call(f32[368,128]{1,0:T(8,128)} %train_step.1.sums), custom_call_target="tpu_custom_call" | custom-call | tf_op jit(solution)/shard_map/finish/pallas_call | solution.py:739

commit v7 on v6

--- a/solution.py
+++ b/solution.py
@@ -18,12 +18,19 @@
 CLIPS = 16
 MB = 1 << 20
 ORDERS = ("xyz", "yzx", "zxy")
-HEAD_BLOCKS = ((0, 3), (3, 2), (5, 4))
-MAIN_BLOCKS = ((18, 24), (6, 72), (6, 64))
-RANGES = (((0, 72), (72, 504)), ((0, 480),), ((0, 72), (72, 480)))
-PART_ROWS = (504, 480, 480)
-LAST_ROWS = (128, 120, 120)
-FIRST_ROWS = (0, 128, 248)
+BLOCKS = (
+    (("head", 0, 3, 24), ("up", 0, 15, 24)),
+    (("head", 3, 2, 24), ("down", 0, 6, 72), ("up", 15, 3, 24)),
+    (("head", 5, 3, 24), ("table", 0, 6, 64), ("head", 8, 1, 24)),
+)
+RANGES = (
+    ((0, 72), (72, 264), (264, 432)),
+    ((0, 264), (264, 480), (480, 552)),
+    ((0, 72), (72, 264), (264, 480)),
+)
+PART_ROWS = (432, 552, 480)
+LAST_ROWS = (112, 144, 120)
+FIRST_ROWS = (0, 112, 256)
 
 
 def bf(array):
@@ -202,9 +209,9 @@
         out[:, :, first + rows * block : first + rows * (block + 1), :] = part
 
 
-def halves_of(rows):
-    upper = (rows // 2 + 7) // 8 * 8
-    return pl.ds(0, upper), pl.ds(upper, rows - upper)
+def halves_of(first, end):
+    middle = first + ((end - first) // 2 + 7) // 8 * 8
+    return pl.ds(first, middle - first), pl.ds(middle, end - middle)
 
 
 def step_kernel(target, ids, kern, scale_i, win, loss_scale, turn1, turn2, row_id, *refs):
@@ -216,12 +223,10 @@
     (nrm_o, hid_o, onm_o, dup_o, ddn_o, dhd_o, dem_o, kg_o) = here
     (left_t, right_t, left_i, right_i, hid_v, stat_o, slots), refs = refs[:7], refs[7:]
     (dfr, dphase, dhead, dup, small), refs = refs[:5], refs[5:]
-    through, from_left, from_right, got2a, got2b, last, got3 = (
-        refs[3 * i : 3 * i + 3] for i in range(7)
-    )
+    through, from_left, from_right, got2, last, got3 = (refs[3 * i : 3 * i + 3] for i in range(6))
     (
         sems, halo_send, halo_recv, stat_send, stat_recv, pair_send, pair_recv, send, recv,
-    ) = refs[21:]
+    ) = refs[18:]
 
     dp, tm = lax.axis_index("dp"), lax.axis_index("tm")
     core = lax.rem(dp, 2)
@@ -372,12 +377,12 @@
             copies[5 + level].wait()
             sums = [jnp.zeros((OWN, 128), F32) for _ in range(3)]
             for c in range(chunks):
+                spectra = mm(seg[...], table[:, 256 * c : 256 * (c + 1)])
                 for sub in range(level + 1):
                     rows_p = slice(ROWS * sub, ROWS * (sub + 1))
                     base = ROWS * (level + 1)
                     rows_g = slice(base + ROWS * sub, base + ROWS * (sub + 1))
-                    weights = table[:, 256 * c : 256 * (c + 1)]
-                    sp, sg = mm(seg[rows_p, :], weights), mm(seg[rows_g, :], weights)
+                    sp, sg = spectra[rows_p], spectra[rows_g]
                     diff = sp - sg
                     pr, pi, gr, gi = sp[:, :128], sp[:, 128:], sg[:, :128], sg[:, 128:]
                     power_p, power_g = pr * pr + pi * pi, gr * gr + gi * gi
@@ -471,6 +476,40 @@
             p[left, high, rows] += through[k][1, :, rows]
             go(p.at[left, high, rows], from_right[k].at[high, rows], k, 6 * s + 5, axis, 3)
 
+        def phase2(k, s):
+            mine, axis, p, g = spot[ORDERS[k][0]], ORDERS[k][1], parts[k], got2[k]
+            i, right, opposite, left = around(axis)
+            first, end = RANGES[k][s]
+            rows = pl.ds(first, end - first)
+            upper, lower = halves_of(first, end)
+            slot = 18 + 6 * s
+            for j in (2, 3, 4, 5):
+                sent[k][6 * s + j].wait_recv()
+
+            def add(j):
+                p[mine, j, rows] += from_left[k][j, rows] + from_right[k][j, rows]
+
+            add(opposite)
+            go(p.at[mine, opposite, upper], g.at[0, upper], k, slot, axis, 1)
+            go(p.at[mine, opposite, lower], g.at[0, lower], k, slot + 1, axis, 3)
+            add(right)
+            go(p.at[mine, right, lower], g.at[1, lower], k, slot + 2, axis, 1)
+            add(left)
+            go(p.at[mine, left, upper], g.at[2, upper], k, slot + 3, axis, 3)
+            add(i)
+
+        def forward2(k, s):
+            mine, axis, p, g = spot[ORDERS[k][0]], ORDERS[k][1], parts[k], got2[k]
+            i, right, opposite, left = around(axis)
+            upper, lower = halves_of(*RANGES[k][s])
+            slot = 18 + 6 * s
+            sent[k][slot].wait_recv()
+            p[mine, right, upper] += g[0, upper]
+            go(p.at[mine, right, upper], g.at[1, upper], k, slot + 4, axis, 1)
+            sent[k][slot + 1].wait_recv()
+            p[mine, left, lower] += g[0, lower]
+            go(p.at[mine, left, lower], g.at[2, lower], k, slot + 5, axis, 3)
+
         for share in shares:
             share.wait_recv()
         total = slots[0]
@@ -537,8 +576,8 @@
         onorm = [lhs(2)]
         onorm += [mm(turn[...], onorm[0]).astype(BF16) for turn in (turn1, turn2)]
         for k in range(3):
-            start, blocks = HEAD_BLOCKS[k]
-            for b in range(min(blocks, 8 - start)):
+            start, blocks = BLOCKS[k][0][1:3]
+            for b in range(blocks):
                 put(parts[k], 24 * b, head_block(onorm[k], start + b), 24)
         phase1(0, 0)
         phase1(2, 0)
@@ -546,7 +585,9 @@
         hidden = lhs(1)
         for c in range(3):
             put(parts[1], 48 + 144 * c, mm(hidden, rhs(4, slice(256 * c, 256 * (c + 1)))), 72)
-        phase1(1, 0)
+            if c == 1:
+                phase1(1, 0)
+        phase1(1, 1)
 
         dnorm = mm_bt(dup[...], up_v[...]).astype(BF16).astype(F32)
         dmix = norm_back(dnorm, y1_o[...], rstd_o[:, 1:2])
@@ -579,62 +620,60 @@
 
         combine(0, 0)
         combine(2, 0)
-        need(0, 3)
-        normed = lhs(0)
-        for c in range(FF // 256):
-            put(parts[0], 72 + 48 * c, mm(normed, rhs(3, slice(256 * c, 256 * (c + 1)))), 24)
-        phase1(0, 1)
-        need(8, 6, 7)
-        put(parts[2], 72, head_block(onorm[2], 8) + here[7][core] + there[7][...], 24)
+        need(8, 6)
         both_ids = jnp.concatenate([ids[...], there[8][...]], axis=1)
         code_rows = row_id[...] + OWN * core
         hot = (code_rows == both_ids[0:1, :]) | (code_rows == both_ids[1:2, :] + 1024)
         hot = jnp.where(hot, 1.0, 0.0).astype(BF16)
-        for c in range(3):
-            put(parts[2], 96 + 128 * c, mm(hot, rhs(6, slice(256 * c, 256 * (c + 1)))), 64)
+        put(parts[2], 72, mm(hot, rhs(6, slice(0, 384))), 64)
         phase1(2, 1)
+        need(7)
+        put(parts[2], 264, mm(hot, rhs(6, slice(384, 768))), 64)
+        put(parts[2], 456, head_block(onorm[2], 8) + here[7][core] + there[7][...], 24)
+        phase1(2, 2)
+        need(0, 3)
+        normed = lhs(0)
+        for c in range(5):
+            put(parts[0], 72 + 72 * c, mm(normed, rhs(3, slice(384 * c, 384 * (c + 1)))), 24)
+            if c == 2:
+                phase1(0, 1)
+        phase1(0, 2)
+        normed = mm(turn1[...], normed).astype(BF16)
+        put(parts[1], 480, mm(normed, rhs(3, slice(1920, 2304))), 24)
+        phase1(1, 2)
+        phase2(0, 0)
+        phase2(2, 0)
         combine(1, 0)
+        forward2(0, 0)
+        forward2(2, 0)
+        combine(2, 1)
         combine(0, 1)
-        combine(2, 1)
-
-        for k in (1, 0, 2):
-            mine = spot[ORDERS[k][0]]
-            axis, p, a, b = ORDERS[k][1], parts[k], got2a[k], got2b[k]
-            i, right, opposite, left = around(axis)
-            upper, lower = halves_of(PART_ROWS[k])
-            for s in range(len(RANGES[k])):
-                for j in (2, 3, 4, 5):
-                    sent[k][6 * s + j].wait_recv()
-            p[mine, opposite] += from_left[k][opposite] + from_right[k][opposite]
-            go(p.at[mine, opposite, upper], a.at[0], k, 12, axis, 1)
-            go(p.at[mine, opposite, lower], b.at[0], k, 13, axis, 3)
-            p[mine, right] += from_left[k][right] + from_right[k][right]
-            go(p.at[mine, right, lower], b.at[1], k, 14, axis, 1)
-            p[mine, left] += from_left[k][left] + from_right[k][left]
-            go(p.at[mine, left, upper], a.at[1], k, 15, axis, 3)
-            p[mine, i] += from_left[k][i] + from_right[k][i]
-        for k in (1, 0, 2):
-            mine = spot[ORDERS[k][0]]
-            axis, p, a, b = ORDERS[k][1], parts[k], got2a[k], got2b[k]
-            i, right, opposite, left = around(axis)
-            upper, lower = halves_of(PART_ROWS[k])
-            sent[k][12].wait_recv()
-            p[mine, right, upper] += a[0]
-            go(p.at[mine, right, upper], a.at[2], k, 16, axis, 1)
-            sent[k][13].wait_recv()
-            p[mine, left, lower] += b[0]
-            go(p.at[mine, left, lower], b.at[2], k, 17, axis, 3)
-        for k in (1, 0, 2):
+        combine(1, 1)
+        phase2(1, 0)
+        combine(2, 2)
+        combine(0, 2)
+        combine(1, 2)
+        phase2(2, 1)
+        phase2(0, 1)
+        forward2(1, 0)
+        phase2(1, 1)
+        forward2(2, 1)
+        forward2(0, 1)
+        phase2(2, 2)
+        phase2(0, 2)
+        phase2(1, 2)
+        for k, t in ((1, 1), (2, 2), (0, 2), (1, 2)):
+            forward2(k, t)
+        for k in (1, 2, 0):
             mine = spot[ORDERS[k][0]]
             i = spot[ORDERS[k][1]]
-            p, a, b, out = parts[k], got2a[k], got2b[k], last[k]
-            upper, lower = halves_of(PART_ROWS[k])
-            for j in (14, 15, 16, 17):
-                sent[k][j].wait_recv()
-            p[mine, i, upper] += a[1] + a[2]
-            p[mine, i, lower] += b[1] + b[2]
+            p, g, out = parts[k], got2[k], last[k]
+            for t in range(3):
+                for j in (2, 3, 4, 5):
+                    sent[k][18 + 6 * t + j].wait_recv()
+            p[mine, i] += g[1] + g[2]
             start, place = 0, 0
-            for count, rows in ((HEAD_BLOCKS[k][1], 24), MAIN_BLOCKS[k]):
+            for _, _, count, rows in BLOCKS[k]:
                 each = rows // 4
                 for _ in range(count):
                     for d in range(4):
@@ -649,9 +688,9 @@
             axis = ORDERS[k][2]
             for by in (1, 2, 3):
                 to = lax.rem(spot[axis] + by, 4)
-                go(out.at[to], got3[k].at[by - 1], k, 17 + by, axis, by)
-        for k in (1, 0, 2):
-            for j in (18, 19, 20):
+                go(out.at[to], got3[k].at[by - 1], k, 35 + by, axis, by)
+        for k in (1, 2, 0):
+            for j in (36, 37, 38):
                 sent[k][j].wait_recv()
             total = last[k][spot[ORDERS[k][2]]] + got3[k][0] + got3[k][1] + got3[k][2]
             out_o[pl.ds(FIRST_ROWS[k], LAST_ROWS[k]), :] = total
@@ -674,7 +713,6 @@
     wide = [full(*((2,) if p else ()), *a.shape) for a, p in zip(OPERANDS, PICKED)]
     edge = full(1, HALO * HOP)
     rows = PART_ROWS
-    cuts = [halves_of(n)[0].size for n in rows]
 
     def each(make):
         return [pltpu.VMEM(make(k), F32) for k in range(3)]
@@ -702,12 +740,11 @@
         + each(lambda k: (2, 2, rows[k], 128))
         + each(lambda k: (4, rows[k], 128))
         + each(lambda k: (4, rows[k], 128))
-        + each(lambda k: (3, cuts[k], 128))
-        + each(lambda k: (3, rows[k] - cuts[k], 128))
+        + each(lambda k: (3, rows[k], 128))
         + each(lambda k: (4, LAST_ROWS[k], 128))
         + each(lambda k: (3, LAST_ROWS[k], 128))
         + [pltpu.SemaphoreType.DMA((n,)) for n in (len(big), 4, 4, 7, 7, 9, 9)]
-        + [pltpu.SemaphoreType.DMA((3, 21))] * 2,
+        + [pltpu.SemaphoreType.DMA((3, 39))] * 2,
         compiler_params=pltpu.CompilerParams(
             collective_id=0, has_side_effects=True, vmem_limit_bytes=64 * MB
         ),
@@ -716,23 +753,22 @@
 
 
 def finish_kernel(sums, loss_o, table_o, kern_o, up_o, down_o, scale_o, head_o):
-    for k, (out, count, each) in enumerate(((up_o, 18, 6), (down_o, 6, 18), (table_o, 6, 16))):
-        start, blocks = HEAD_BLOCKS[k]
-        for c in range(blocks):
-            rows = FIRST_ROWS[k] + 6 * c
-            values = sums[rows : rows + 6, :]
-            if start + c < 8:
-                head_o[:, 128 * (start + c) : 128 * (start + c + 1)] = values
-            else:
+    outs = {"up": up_o, "down": down_o, "table": table_o, "head": head_o}
+    for k in range(3):
+        rows = FIRST_ROWS[k]
+        for name, start, count, block in BLOCKS[k]:
+            for c in range(start, start + count):
+                values = sums[rows : rows + block // 4, :]
+                rows += block // 4
+                if (name, c) != ("head", 8):
+                    outs[name][:, 128 * c : 128 * (c + 1)] = values
+                    continue
                 head_o[:, 1024:1026] = values[:, 0:2]
                 tail = jnp.transpose(jnp.concatenate([values, jnp.zeros((122, 128), F32)], axis=0))
                 kern_o[...] = tail[2:9, 0:6]
                 scale_o[...] = tail[9:10, 0:6]
                 pieces = values[0:1, 10:14]
                 loss_o[...] = jnp.sum(pieces, axis=1, keepdims=True) * (0.5 / CLIPS)
-        for c in range(count):
-            rows = FIRST_ROWS[k] + 6 * blocks + each * c
-            out[:, 128 * c : 128 * (c + 1)] = sums[rows : rows + each, :]
 
 
 def finish_call(sums):

time: 87.4 us -> 94.4 us (1.080)
  Pallas kernels: 86 us -> 93 us
    pallas_call x1, Pallas kernels: 84.4 us -> 91.3 us  [step_call(): pl.pallas_call(step_kernel, out_shape=full(sum(LAST_ROWS), 128), in_specs...]
where the time goes in v7:
time: 94.4 us; the launch traced here: 94.2 us
  Pallas kernels  93 us (99%)
  between operations  1.29 us (1%)
    pallas_call x1, Pallas kernels, step_call(): pl.pallas_call(step_kernel, out_shape=full(sum(LAST_ROWS), 128), in_specs...  91.3 us

profile of v7, /device:TPU:0, one launch (start us, length us, event | category | flops | bytes accessed | tf_op | source)
XLA Modules:
  0.0 94.2 jit_solution(4332661648759339513)
XLA Ops:
  1.3 91.3 %train_step.1.sums = f32[376,128]{1,0:T(8,128)} custom-call(f32[1,32768]{1,0:T(1,128)} %target.1, s32[2,128]{1,0:T(2,128)} %bitcast.9, f32[7,768]{1,0:T(8,128)} %kern.1, f32[768]{0:T(1024)} %scale_i.1, f32[8,1024]{1,0:T(8,128)} %constant.20.clone.win, f32[1,1]{1,0:T(1,128)} %bitcast.7.loss_scale, bf16[384,384]{1,0:T(8,128)(2,1)} %constant.21.clone.turn1, ...), custom_call_target="tpu_custom_call" | custom-call | tf_op jit(solution)/shard_map/train_step/pallas_call | solution.py:720
  92.6 1.6 %finish.1 = (f32[1,1]{1,0:T(1,128)}, f32[16,768]{1,0:T(8,128)}, f32[7,6]{1,0:T(8,128)}, f32[6,2304]{1,0:T(8,128)}, f32[18,768]{1,0:T(8,128)}, /*index=5*/f32[1,6]{1,0:T(1,128)}, f32[6,1026]{1,0:T(8,128)}) custom-call(f32[376,128]{1,0:T(8,128)} %train_step.1.sums), custom_call_target="tpu_custom_call" | custom-call | tf_op jit(solution)/shard_map/finish/pallas_call | solution.py:775

commit v8 on v6

--- a/solution.py
+++ b/solution.py
@@ -18,12 +18,15 @@
 CLIPS = 16
 MB = 1 << 20
 ORDERS = ("xyz", "yzx", "zxy")
-HEAD_BLOCKS = ((0, 3), (3, 2), (5, 4))
-MAIN_BLOCKS = ((18, 24), (6, 72), (6, 64))
-RANGES = (((0, 72), (72, 504)), ((0, 480),), ((0, 72), (72, 480)))
-PART_ROWS = (504, 480, 480)
-LAST_ROWS = (128, 120, 120)
-FIRST_ROWS = (0, 128, 248)
+BLOCKS = (
+    (("head", 0, 3, 24), ("up", 0, 15, 24)),
+    (("head", 3, 2, 24), ("down", 0, 6, 72), ("up", 15, 3, 24)),
+    (("head", 5, 4, 24), ("table", 0, 6, 64)),
+)
+RANGES = (((0, 72), (72, 432)), ((0, 480), (480, 552)), ((0, 72), (72, 480)))
+PART_ROWS = (432, 552, 480)
+LAST_ROWS = (112, 144, 120)
+FIRST_ROWS = (0, 112, 256)
 
 
 def bf(array):
@@ -537,7 +540,7 @@
         onorm = [lhs(2)]
         onorm += [mm(turn[...], onorm[0]).astype(BF16) for turn in (turn1, turn2)]
         for k in range(3):
-            start, blocks = HEAD_BLOCKS[k]
+            start, blocks = BLOCKS[k][0][1:3]
             for b in range(min(blocks, 8 - start)):
                 put(parts[k], 24 * b, head_block(onorm[k], start + b), 24)
         phase1(0, 0)
@@ -553,7 +556,7 @@
         dmix = jnp.where(valid, dmix, 0.0)
         y0 = sin_o[...]
         dsin = dstream
-        small[...] = jnp.zeros((128, D), F32)
+        small[...] = jnp.zeros((16, D), F32)
         for k in range(7):
             dsin = dsin + kern[k : k + 1, :] * shift(dmix, k - 3)
             taps = dmix * shift(y0, 3 - k)
@@ -573,31 +576,40 @@
         rest = small[...] - small0.astype(F32)
         small1 = rest.astype(BF16)
         small2 = (rest - small1.astype(F32)).astype(BF16)
+        pieces = jnp.concatenate([small0, small1, small2], axis=0)
         for c in range(2):
-            kg_o[c] = sum(mm_bt(pick_k[c], part) for part in (small0, small1, small2))
+            picked = mm_bt(pieces, pick_k[c])
+            picked = picked[0:16] + picked[16:32] + picked[32:48]
+            picked = jnp.concatenate([picked, jnp.zeros((112, 384), F32)], axis=0)
+            kg_o[c] = jnp.transpose(picked)
         give(7)
 
         combine(0, 0)
         combine(2, 0)
-        need(0, 3)
-        normed = lhs(0)
-        for c in range(FF // 256):
-            put(parts[0], 72 + 48 * c, mm(normed, rhs(3, slice(256 * c, 256 * (c + 1)))), 24)
-        phase1(0, 1)
-        need(8, 6, 7)
-        put(parts[2], 72, head_block(onorm[2], 8) + here[7][core] + there[7][...], 24)
+        need(8, 6)
         both_ids = jnp.concatenate([ids[...], there[8][...]], axis=1)
         code_rows = row_id[...] + OWN * core
         hot = (code_rows == both_ids[0:1, :]) | (code_rows == both_ids[1:2, :] + 1024)
         hot = jnp.where(hot, 1.0, 0.0).astype(BF16)
         for c in range(3):
             put(parts[2], 96 + 128 * c, mm(hot, rhs(6, slice(256 * c, 256 * (c + 1)))), 64)
+        need(7)
+        put(parts[2], 72, head_block(onorm[2], 8) + here[7][core] + there[7][...], 24)
         phase1(2, 1)
+        need(0, 3)
+        normed = lhs(0)
+        for c in range(5):
+            put(parts[0], 72 + 72 * c, mm(normed, rhs(3, slice(384 * c, 384 * (c + 1)))), 24)
+        phase1(0, 1)
+        normed = mm(turn1[...], normed).astype(BF16)
+        put(parts[1], 480, mm(normed, rhs(3, slice(1920, 2304))), 24)
+        phase1(1, 1)
         combine(1, 0)
+        combine(2, 1)
         combine(0, 1)
-        combine(2, 1)
-
-        for k in (1, 0, 2):
+        combine(1, 1)
+
+        for k in (1, 2, 0):
             mine = spot[ORDERS[k][0]]
             axis, p, a, b = ORDERS[k][1], parts[k], got2a[k], got2b[k]
             i, right, opposite, left = around(axis)
@@ -613,7 +625,7 @@
             p[mine, left] += from_left[k][left] + from_right[k][left]
             go(p.at[mine, left, upper], a.at[1], k, 15, axis, 3)
             p[mine, i] += from_left[k][i] + from_right[k][i]
-        for k in (1, 0, 2):
+        for k in (1, 2, 0):
             mine = spot[ORDERS[k][0]]
             axis, p, a, b = ORDERS[k][1], parts[k], got2a[k], got2b[k]
             i, right, opposite, left = around(axis)
@@ -624,7 +636,7 @@
             sent[k][13].wait_recv()
             p[mine, left, lower] += b[0]
             go(p.at[mine, left, lower], b.at[2], k, 17, axis, 3)
-        for k in (1, 0, 2):
+        for k in (1, 2, 0):
             mine = spot[ORDERS[k][0]]
             i = spot[ORDERS[k][1]]
             p, a, b, out = parts[k], got2a[k], got2b[k], last[k]
@@ -634,7 +646,7 @@
             p[mine, i, upper] += a[1] + a[2]
             p[mine, i, lower] += b[1] + b[2]
             start, place = 0, 0
-            for count, rows in ((HEAD_BLOCKS[k][1], 24), MAIN_BLOCKS[k]):
+            for _, _, count, rows in BLOCKS[k]:
                 each = rows // 4
                 for _ in range(count):
                     for d in range(4):
@@ -650,7 +662,7 @@
             for by in (1, 2, 3):
                 to = lax.rem(spot[axis] + by, 4)
                 go(out.at[to], got3[k].at[by - 1], k, 17 + by, axis, by)
-        for k in (1, 0, 2):
+        for k in (1, 2, 0):
             for j in (18, 19, 20):
                 sent[k][j].wait_recv()
             total = last[k][spot[ORDERS[k][2]]] + got3[k][0] + got3[k][1] + got3[k][2]
@@ -697,7 +709,7 @@
             pltpu.VMEM((ROWS, CHUNKS1 * 128), F32),
             pltpu.VMEM((ROWS, 1152), BF16),
             pltpu.VMEM((ROWS, FF), BF16),
-            pltpu.VMEM((128, D), F32),
+            pltpu.VMEM((16, D), F32),
         ]
         + each(lambda k: (2, 2, rows[k], 128))
         + each(lambda k: (4, rows[k], 128))
@@ -716,23 +728,22 @@
 
 
 def finish_kernel(sums, loss_o, table_o, kern_o, up_o, down_o, scale_o, head_o):
-    for k, (out, count, each) in enumerate(((up_o, 18, 6), (down_o, 6, 18), (table_o, 6, 16))):
-        start, blocks = HEAD_BLOCKS[k]
-        for c in range(blocks):
-            rows = FIRST_ROWS[k] + 6 * c
-            values = sums[rows : rows + 6, :]
-            if start + c < 8:
-                head_o[:, 128 * (start + c) : 128 * (start + c + 1)] = values
-            else:
+    outs = {"up": up_o, "down": down_o, "table": table_o, "head": head_o}
+    for k in range(3):
+        rows = FIRST_ROWS[k]
+        for name, start, count, block in BLOCKS[k]:
+            for c in range(start, start + count):
+                values = sums[rows : rows + block // 4, :]
+                rows += block // 4
+                if (name, c) != ("head", 8):
+                    outs[name][:, 128 * c : 128 * (c + 1)] = values
+                    continue
                 head_o[:, 1024:1026] = values[:, 0:2]
                 tail = jnp.transpose(jnp.concatenate([values, jnp.zeros((122, 128), F32)], axis=0))
                 kern_o[...] = tail[2:9, 0:6]
                 scale_o[...] = tail[9:10, 0:6]
                 pieces = values[0:1, 10:14]
                 loss_o[...] = jnp.sum(pieces, axis=1, keepdims=True) * (0.5 / CLIPS)
-        for c in range(count):
-            rows = FIRST_ROWS[k] + 6 * blocks + each * c
-            out[:, 128 * c : 128 * (c + 1)] = sums[rows : rows + each, :]
 
 
 def finish_call(sums):

time: 87.4 us -> 90.8 us (1.039)
  Pallas kernels: 86 us -> 89.3 us
    pallas_call x1, Pallas kernels: 84.4 us -> 87.7 us  [step_call(): pl.pallas_call(step_kernel, out_shape=full(sum(LAST_ROWS), 128), in_specs...]
where the time goes in v8:
time: 90.8 us; the launch traced here: 90.6 us
  Pallas kernels  89.3 us (98%)
  between operations  1.29 us (1%)
    pallas_call x1, Pallas kernels, step_call(): pl.pallas_call(step_kernel, out_shape=full(sum(LAST_ROWS), 128), in_specs...  87.7 us

profile of v8, /device:TPU:0, one launch (start us, length us, event | category | flops | bytes accessed | tf_op | source)
XLA Modules:
  0.0 90.6 jit_solution(6120946578518434595)
XLA Ops:
  1.3 87.7 %train_step.1.sums = f32[376,128]{1,0:T(8,128)} custom-call(f32[1,32768]{1,0:T(1,128)} %target.1, s32[2,128]{1,0:T(2,128)} %bitcast.9, f32[7,768]{1,0:T(8,128)} %kern.1, f32[768]{0:T(1024)} %scale_i.1, f32[8,1024]{1,0:T(8,128)} %constant.20.clone.win, f32[1,1]{1,0:T(1,128)} %bitcast.7.loss_scale, bf16[384,384]{1,0:T(8,128)(2,1)} %constant.21.clone.turn1, ...), custom_call_target="tpu_custom_call" | custom-call | tf_op jit(solution)/shard_map/train_step/pallas_call | solution.py:694
  89.0 1.6 %finish.1 = (f32[1,1]{1,0:T(1,128)}, f32[16,768]{1,0:T(8,128)}, f32[7,6]{1,0:T(8,128)}, f32[6,2304]{1,0:T(8,128)}, f32[18,768]{1,0:T(8,128)}, /*index=5*/f32[1,6]{1,0:T(1,128)}, f32[6,1026]{1,0:T(8,128)}) custom-call(f32[376,128]{1,0:T(8,128)} %train_step.1.sums), custom_call_target="tpu_custom_call" | custom-call | tf_op jit(solution)/shard_map/finish/pallas_call | solution.py:750

commit v9 on v6

--- a/solution.py
+++ b/solution.py
@@ -547,20 +547,26 @@
         for c in range(3):
             put(parts[1], 48 + 144 * c, mm(hidden, rhs(4, slice(256 * c, 256 * (c + 1)))), 72)
         phase1(1, 0)
+        need(0, 3)
+        normed = lhs(0)
+        for c in range(FF // 256):
+            put(parts[0], 72 + 48 * c, mm(normed, rhs(3, slice(256 * c, 256 * (c + 1)))), 24)
+        phase1(0, 1)
 
         dnorm = mm_bt(dup[...], up_v[...]).astype(BF16).astype(F32)
         dmix = norm_back(dnorm, y1_o[...], rstd_o[:, 1:2])
         dmix = jnp.where(valid, dmix, 0.0)
         y0 = sin_o[...]
         dsin = dstream
-        small[...] = jnp.zeros((128, D), F32)
         for k in range(7):
             dsin = dsin + kern[k : k + 1, :] * shift(dmix, k - 3)
-            taps = dmix * shift(y0, 3 - k)
-            small[2 + k : 3 + k, :] = jnp.sum(taps[own], axis=0, keepdims=True)
         demb = norm_back(dsin, y0, rstd_o[:, 0:1])
         dem_o[...] = demb[own].astype(BF16).astype(F32)
         give(6)
+        small[...] = jnp.zeros((16, D), F32)
+        for k in range(7):
+            taps = dmix * shift(y0, 3 - k)
+            small[2 + k : 3 + k, :] = jnp.sum(taps[own], axis=0, keepdims=True)
 
         small[9:10, :] = scale_grad
         rest = loss
@@ -573,25 +579,25 @@
         rest = small[...] - small0.astype(F32)
         small1 = rest.astype(BF16)
         small2 = (rest - small1.astype(F32)).astype(BF16)
+        pieces = jnp.concatenate([small0, small1, small2], axis=0)
         for c in range(2):
-            kg_o[c] = sum(mm_bt(pick_k[c], part) for part in (small0, small1, small2))
+            picked = mm_bt(pieces, pick_k[c])
+            picked = picked[0:16] + picked[16:32] + picked[32:48]
+            picked = jnp.concatenate([picked, jnp.zeros((112, 384), F32)], axis=0)
+            kg_o[c] = jnp.transpose(picked)
         give(7)
 
         combine(0, 0)
         combine(2, 0)
-        need(0, 3)
-        normed = lhs(0)
-        for c in range(FF // 256):
-            put(parts[0], 72 + 48 * c, mm(normed, rhs(3, slice(256 * c, 256 * (c + 1)))), 24)
-        phase1(0, 1)
-        need(8, 6, 7)
-        put(parts[2], 72, head_block(onorm[2], 8) + here[7][core] + there[7][...], 24)
+        need(8, 6)
         both_ids = jnp.concatenate([ids[...], there[8][...]], axis=1)
         code_rows = row_id[...] + OWN * core
         hot = (code_rows == both_ids[0:1, :]) | (code_rows == both_ids[1:2, :] + 1024)
         hot = jnp.where(hot, 1.0, 0.0).astype(BF16)
         for c in range(3):
             put(parts[2], 96 + 128 * c, mm(hot, rhs(6, slice(256 * c, 256 * (c + 1)))), 64)
+        need(7)
+        put(parts[2], 72, head_block(onorm[2], 8) + here[7][core] + there[7][...], 24)
         phase1(2, 1)
         combine(1, 0)
         combine(0, 1)
@@ -697,7 +703,7 @@
             pltpu.VMEM((ROWS, CHUNKS1 * 128), F32),
             pltpu.VMEM((ROWS, 1152), BF16),
             pltpu.VMEM((ROWS, FF), BF16),
-            pltpu.VMEM((128, D), F32),
+            pltpu.VMEM((16, D), F32),
         ]
         + each(lambda k: (2, 2, rows[k], 128))
         + each(lambda k: (4, rows[k], 128))

time: 87.4 us -> 87.7 us (level)
  no operation moved by 1% of the time
where the time goes in v9:
time: 87.7 us; the launch traced here: 87.3 us
  Pallas kernels  86.1 us (98%)
  between operations  1.29 us (1%)
    pallas_call x1, Pallas kernels, step_call(): pl.pallas_call(step_kernel, out_shape=full(sum(LAST_ROWS), 128), in_specs...  84.4 us

profile of v9, /device:TPU:0, one launch (start us, length us, event | category | flops | bytes accessed | tf_op | source)
XLA Modules:
  0.0 87.3 jit_solution(10224770343029545914)
XLA Ops:
  1.3 84.4 %train_step.1.sums = f32[368,128]{1,0:T(8,128)} custom-call(f32[1,32768]{1,0:T(1,128)} %target.1, s32[2,128]{1,0:T(2,128)} %bitcast.9, f32[7,768]{1,0:T(8,128)} %kern.1, f32[768]{0:T(1024)} %scale_i.1, f32[8,1024]{1,0:T(8,128)} %constant.20.clone.win, f32[1,1]{1,0:T(1,128)} %bitcast.7.loss_scale, bf16[384,384]{1,0:T(8,128)(2,1)} %constant.21.clone.turn1, ...), custom_call_target="tpu_custom_call" | custom-call | tf_op jit(solution)/shard_map/train_step/pallas_call | solution.py:688
  85.7 1.6 %finish.1 = (f32[1,1]{1,0:T(1,128)}, f32[16,768]{1,0:T(8,128)}, f32[7,6]{1,0:T(8,128)}, f32[6,2304]{1,0:T(8,128)}, f32[18,768]{1,0:T(8,128)}, /*index=5*/f32[1,6]{1,0:T(1,128)}, f32[6,1026]{1,0:T(8,128)}) custom-call(f32[368,128]{1,0:T(8,128)} %train_step.1.sums), custom_call_target="tpu_custom_call" | custom-call | tf_op jit(solution)/shard_map/finish/pallas_call | solution.py:745

commit v10 on v9

--- a/solution.py
+++ b/solution.py
@@ -454,8 +454,10 @@
             i, right, opposite, left = around(axis)
             first, end = RANGES[k][s]
             rows = pl.ds(first, end - first)
-            go(p.at[opposite, low, rows], through[k].at[0, :, rows], k, 6 * s, axis, 1)
-            go(p.at[opposite, high, rows], through[k].at[1, :, rows], k, 6 * s + 1, axis, 3)
+            go(p.at[opposite, 0, rows], through[k].at[0, 0, rows], k, 6 * s, axis, 1)
+            go(p.at[opposite, 1, rows], through[k].at[0, 1, rows], k, 21 + 2 * s, axis, 1)
+            go(p.at[opposite, 2, rows], through[k].at[1, 0, rows], k, 6 * s + 1, axis, 3)
+            go(p.at[opposite, 3, rows], through[k].at[1, 1, rows], k, 22 + 2 * s, axis, 3)
             go(p.at[right, high, rows], from_left[k].at[high, rows], k, 6 * s + 2, axis, 1)
             go(p.at[left, low, rows], from_right[k].at[low, rows], k, 6 * s + 3, axis, 3)
 
@@ -465,9 +467,11 @@
             first, end = RANGES[k][s]
             rows = pl.ds(first, end - first)
             sent[k][6 * s].wait_recv()
+            sent[k][21 + 2 * s].wait_recv()
             p[right, low, rows] += through[k][0, :, rows]
             go(p.at[right, low, rows], from_left[k].at[low, rows], k, 6 * s + 4, axis, 1)
             sent[k][6 * s + 1].wait_recv()
+            sent[k][22 + 2 * s].wait_recv()
             p[left, high, rows] += through[k][1, :, rows]
             go(p.at[left, high, rows], from_right[k].at[high, rows], k, 6 * s + 5, axis, 3)
 
@@ -713,7 +717,7 @@
         + each(lambda k: (4, LAST_ROWS[k], 128))
         + each(lambda k: (3, LAST_ROWS[k], 128))
         + [pltpu.SemaphoreType.DMA((n,)) for n in (len(big), 4, 4, 7, 7, 9, 9)]
-        + [pltpu.SemaphoreType.DMA((3, 21))] * 2,
+        + [pltpu.SemaphoreType.DMA((3, 25))] * 2,
         compiler_params=pltpu.CompilerParams(
             collective_id=0, has_side_effects=True, vmem_limit_bytes=64 * MB
         ),

time: 87.7 us -> 88.1 us (level)
  no operation moved by 1% of the time
where the time goes in v10:
time: 88.1 us; the launch traced here: 87.7 us
  Pallas kernels  86.4 us (98%)
  between operations  1.29 us (1%)
    pallas_call x1, Pallas kernels, step_call(): pl.pallas_call(step_kernel, out_shape=full(sum(LAST_ROWS), 128), in_specs...  84.7 us

profile of v10, /device:TPU:0, one launch (start us, length us, event | category | flops | bytes accessed | tf_op | source)
XLA Modules:
  0.0 87.7 jit_solution(12012741464886839831)
XLA Ops:
  1.3 84.7 %train_step.1.sums = f32[368,128]{1,0:T(8,128)} custom-call(f32[1,32768]{1,0:T(1,128)} %target.1, s32[2,128]{1,0:T(2,128)} %bitcast.9, f32[7,768]{1,0:T(8,128)} %kern.1, f32[768]{0:T(1024)} %scale_i.1, f32[8,1024]{1,0:T(8,128)} %constant.20.clone.win, f32[1,1]{1,0:T(1,128)} %bitcast.7.loss_scale, bf16[384,384]{1,0:T(8,128)(2,1)} %constant.21.clone.turn1, ...), custom_call_target="tpu_custom_call" | custom-call | tf_op jit(solution)/shard_map/train_step/pallas_call | solution.py:692
  86.0 1.6 %finish.1 = (f32[1,1]{1,0:T(1,128)}, f32[16,768]{1,0:T(8,128)}, f32[7,6]{1,0:T(8,128)}, f32[6,2304]{1,0:T(8,128)}, f32[18,768]{1,0:T(8,128)}, /*index=5*/f32[1,6]{1,0:T(1,128)}, f32[6,1026]{1,0:T(8,128)}) custom-call(f32[368,128]{1,0:T(8,128)} %train_step.1.sums), custom_call_target="tpu_custom_call" | custom-call | tf_op jit(solution)/shard_map/finish/pallas_call | solution.py:749
